TPU v7x, 128 devices: a whole 4x4x4 slice. The times are simulated.
128 devices in a mesh: rows: 8 (over x, core), cols: 16 (over y, z).
Axes of the slice: x: 4, y: 4, z: 4, core: 2. Of those that a mesh axis runs over, the one named last changes fastest.
Arguments:
- masks: bfloat16 [768, 384, 384], P(('rows', 'cols'))
- owned_counts: int32 [8, 16], replicated, may hold values from 1 to 6, 32 in all within a row
- cell_ids: int32 [16, 64], P(None, 'cols'), may hold values from 0 to 255, as said below
- kernels: float32 [2, 16, 32, 32], replicated, may hold values from -6 to 6
- kernel_weights: float32 [16], replicated, may hold values from 0.02 to 0.2
- dose: float32 [16, 64], P('rows', 'cols'), may hold values from 0.5 to 1.5
- threshold: float32 [1], replicated, may hold values from 0.3 to 0.6
Outputs:
- resist: bfloat16 [6144, 24576], P('rows', 'cols')
Inputs may be any that keep to these rules, and one draw needn't show every extreme that they name: `owned_counts`: each row sums to 32, and some entry of each row equals 6. `cell_ids`: in the block of 2 x 4 instances of one device, at most 2 name cells of one mesh row (cells r * 32 to (r + 1) * 32 - 1), and every device reaches 2 for some row.
All inputs are finite; a program needn't handle non-finite values.
Results may differ from a plain program's by a relative error of at most 0.0034.
Values may be sent and summed in bfloat16 or wider, within the bound.
No kernel may reach another device: no remote copies, remote signals or barrier semaphores. Data moves between devices by JAX's collectives and lax.ppermute only.
A program may use at most 128 MiB of HBM per device.

v0:
```python
import functools

import jax
import jax.numpy as jnp
import ml_dtypes
import numpy as np
from jax import lax
from jax.experimental import pallas as pl
from jax.experimental.pallas import tpu as pltpu
from jax.sharding import PartitionSpec as P

REACH = 8
TILE = 384
NF = 32
NK = 16
Q = 64
SLOTS = 6
ROWS = 8
COLS = 16
CELLS = 32
LANES = 128
INFO = 3 * Q
PACKET = INFO + 16
OUTGOING = 2 * Q + 16
GROUPS = NK // 4
BF16 = jnp.bfloat16
F32 = jnp.float32


def split(table):
    high = table.astype(ml_dtypes.bfloat16)
    low = (table - high.astype(np.float64)).astype(ml_dtypes.bfloat16)
    return high, low


@functools.lru_cache(maxsize=None)
def tables():
    freq = np.arange(NF) - NF // 2
    pixels = np.arange(TILE)
    points = np.arange(Q)
    turn = np.mod(freq[:, None] * pixels[None, :], TILE) * (2.0 * np.pi / TILE)
    forward = np.concatenate([np.cos(turn), np.sin(turn)]) / TILE
    high, low = split(forward)
    forward_rows = np.concatenate([high, low])
    forward_cols = np.ascontiguousarray(forward_rows.T)

    turn = np.mod(points[:, None] * freq[None, :], Q) * (2.0 * np.pi / Q)
    cos, sin = np.cos(turn), np.sin(turn)
    left = np.block([[cos, -sin], [sin, cos]])
    high, low = split(left)
    inverse_left = np.concatenate([high, high, low], axis=1)
    right = np.zeros((2 * LANES, 4 * LANES))
    for k in range(4):
        re = slice(k * NF, (k + 1) * NF)
        im = slice(LANES + k * NF, LANES + (k + 1) * NF)
        out_re = slice(k * LANES, k * LANES + Q)
        out_im = slice(k * LANES + Q, (k + 1) * LANES)
        right[re, out_re], right[re, out_im] = cos.T, sin.T
        right[im, out_re], right[im, out_im] = -sin.T, cos.T
    inverse_right = np.stack(split(right))

    harmonic = np.arange(Q) - Q // 2
    fine = np.mod(pixels[:, None] * harmonic[None, :], TILE) * (2.0 * np.pi / TILE)
    grid = np.mod(points[:, None] * harmonic[None, :], Q) * (2.0 * np.pi / Q)
    interp = (np.cos(fine) @ np.cos(grid).T + np.sin(fine) @ np.sin(grid).T) / Q
    interp16 = interp.astype(ml_dtypes.bfloat16)
    interp = interp16.astype(np.float64)

    offsets = np.arange(2 * REACH + 1) - REACH
    taps = np.exp(-offsets * offsets / 32.0)
    taps = taps / taps.sum()

    def blur(out_pixels, in_pixels):
        gap = out_pixels[:, None] - in_pixels[None, :]
        inside = np.abs(gap) <= REACH
        return np.where(inside, taps[np.clip(gap + REACH, 0, 2 * REACH)], 0.0)

    edge = np.concatenate([interp16[TILE - REACH :], interp16[:REACH]])
    edge_pad = np.zeros((2, 16, LANES), ml_dtypes.bfloat16)
    edge_pad[0, :, :Q] = edge
    edge_pad[1, :, Q:] = edge

    reach_cols = np.concatenate(
        [np.arange(TILE), np.arange(-LANES, 0), np.arange(TILE, TILE + LANES)]
    )
    spread = (blur(reach_cols, pixels) @ interp).T
    across = np.zeros((2, LANES, 5 * LANES))
    across[0, :Q] = spread
    across[1, Q:] = spread
    across = across.astype(ml_dtypes.bfloat16)

    out_rows = np.arange(2 * TILE)
    down = np.concatenate(
        [
            blur(out_rows, pixels) @ interp,
            blur(out_rows, pixels + TILE) @ interp,
            blur(out_rows, np.arange(-REACH, 0)),
            blur(out_rows, np.arange(2 * TILE, 2 * TILE + REACH)),
        ],
        axis=1,
    )
    down = np.stack(split(4.0 * down))

    lane = np.arange(LANES)
    side = np.concatenate(
        [
            blur(lane, np.arange(-REACH, 0)).T,
            blur(lane, np.arange(LANES, LANES + REACH)).T,
        ]
    ).astype(ml_dtypes.bfloat16)
    return dict(
        forward_rows=forward_rows,
        forward_cols=forward_cols,
        inverse_left=inverse_left,
        inverse_right=inverse_right,
        edge=edge,
        edge_pad=edge_pad,
        across=across,
        down=down,
        side=side,
    )


def dot(a, b):
    return jnp.dot(a, b, preferred_element_type=F32)


def halves(x):
    high = x.astype(BF16)
    return high, (x - high.astype(F32)).astype(BF16)


def lanes_of(shape):
    return lax.broadcasted_iota(jnp.int32, shape, 1)


def imaging_kernel(
    mask, kernels, weights, ids, dose, fwd_cols, fwd_rows, inv_left, inv_right, out, ker, info
):
    step = pl.program_id(0)

    @pl.when(step == 0)
    def _():
        for part in range(2):
            for group in range(GROUPS):
                four = [
                    kernels[part, 4 * group + i]
                    * jnp.sqrt(jnp.full((NF, NF), weights[4 * group + i], F32))
                    for i in range(4)
                ]
                ker[part, group] = jnp.concatenate(four, axis=1)
        info[...] = jnp.zeros_like(info)
        info[:, 0:4] = ids[...].astype(F32)
        first = dose[...].astype(BF16).astype(F32)
        second = (dose[...] - first).astype(BF16).astype(F32)
        info[0:2, 4:8] = first
        info[0:2, 8:12] = second
        info[0:2, 12:16] = dose[...] - first - second
        packed = info[...].astype(BF16)
        for c in range(COLS):
            out[c, INFO : INFO + 16, :] = packed

    lane = lanes_of((NF, LANES))
    even = (lane // NF) % 2 == 0
    images = []
    for slot in range(2):
        cols = dot(mask[slot], fwd_cols[...])
        cols = cols + pltpu.roll(cols, Q, 1)
        high, low = halves(cols)
        pair = jnp.where(lanes_of((TILE, LANES)) < Q, high.astype(F32), low.astype(F32))
        both = dot(fwd_rows[...], pair.astype(BF16))
        both = both[:Q] + both[Q:]
        both = both + pltpu.roll(both, Q, 1)
        top, bottom = both[:NF], both[NF:]
        real = top - pltpu.roll(bottom, NF, 1)
        imag = -(bottom + pltpu.roll(top, NF, 1))
        real = jnp.where(even, real, pltpu.roll(real, NF, 1))
        imag = jnp.where(even, imag, pltpu.roll(imag, NF, 1))
        highs, lows = [], []
        for group in range(GROUPS):
            kr, ki = ker[0, group], ker[1, group]
            prod = jnp.concatenate([kr * real - ki * imag, kr * imag + ki * real], axis=0)
            high, low = halves(prod)
            highs.append(high)
            lows.append(low)
        high = jnp.concatenate(highs, axis=1)
        low = jnp.concatenate(lows, axis=1)
        half = dot(inv_left[...], jnp.concatenate([high, low, high], axis=0))
        blocks = []
        for group in range(GROUPS):
            g = slice(group * LANES, (group + 1) * LANES)
            blocks.append(jnp.concatenate([half[:Q, g], half[Q:, g]], axis=1))
        high, low = halves(jnp.concatenate(blocks, axis=0))
        field = dot(high, inv_right[0]) + (dot(high, inv_right[1]) + dot(low, inv_right[0]))
        power = field * field
        total = None
        for group in range(GROUPS):
            for k in range(4):
                part = power[group * Q : (group + 1) * Q, k * LANES : (k + 1) * LANES]
                total = part if total is None else total + part
        images.append(total + pltpu.roll(total, Q, 1))
    tile = jnp.where(lanes_of((Q, LANES)) < Q, images[0], images[1]).astype(BF16)
    at = pl.multiple_of(step * Q, Q)
    for c in range(COLS):
        out[c, pl.ds(at, Q), :] = tile


def routing_kernel(
    packets, counts, edge, edge_pad, out, strips, where_v, where_s, cell_slot, sem
):
    row, col = lax.axis_index("rows"), lax.axis_index("cols")
    before = packets[jnp.maximum(col - 1, 0), INFO : INFO + 16, :].astype(F32)
    here = packets[col, INFO : INFO + 16, :].astype(F32)
    after = packets[jnp.minimum(col + 1, COLS - 1), INFO : INFO + 16, :].astype(F32)
    lane = lanes_of((16, LANES))

    window = jnp.where(
        lane == 0,
        pltpu.roll(before, LANES - 3, 1),
        jnp.where(lane < 5, pltpu.roll(here, 1, 1), pltpu.roll(after, 5, 1)),
    ).astype(jnp.int32)
    cell = window - row * CELLS
    exists = ((lane > 0) | (col > 0)) & ((lane < 5) | (col < COLS - 1)) & (lane < 6)
    mine = (cell >= 0) & (cell < CELLS) & exists
    where_v[...] = jnp.where(mine, cell, -1)
    copy = pltpu.make_async_copy(where_v, where_s, sem)
    copy.start()

    start = jnp.int32(0)
    for c in range(COLS):
        for s in range(SLOTS):
            cell_slot[start + s] = jnp.int32(c * 8 + s)
        start = start + counts[row, c]

    left = lane < Q
    for cell_index in range(CELLS):
        place = cell_slot[cell_index]
        odd = place & 1
        at = pl.multiple_of(((place >> 1) & 3) * Q, Q)
        pair = packets[place >> 3, pl.ds(at, Q), :]
        along = dot(edge[...], pair)
        strips[cell_index, 0:16, :] = jnp.where(left == (odd == 0), along, pltpu.roll(along, Q, 1))
        strips[cell_index, 16:32, :] = lax.dot_general(
            edge_pad[odd],
            jnp.concatenate([pair, pair], axis=0),
            (((1,), (1,)), ((), ())),
            preferred_element_type=F32,
        )
    copy.wait()

    left8 = lanes_of((REACH, LANES)) < Q

    def strip(index, kind):
        value = strips[jnp.maximum(index, 0), kind * REACH : (kind + 1) * REACH, :]
        return jnp.where(index >= 0, value, 0.0)

    def two(first, second, kind):
        return jnp.where(left8, strip(first, kind), strip(second, kind))

    none = jnp.int32(-1)
    info = jnp.where(
        lane < 16,
        before,
        jnp.where(lane < 32, pltpu.roll(here, 16, 1), pltpu.roll(after, 32, 1)),
    ).astype(BF16)
    left64 = lanes_of((Q, LANES)) < Q
    for dest in range(ROWS):
        first, second = none, none
        for i in range(2):
            for j in range(4):
                here_cell = where_s[2 * dest + i, 1 + j]
                held = here_cell >= 0
                second = jnp.where(held & (first >= 0) & (second < 0), here_cell, second)
                first = jnp.where(held & (first < 0), here_cell, first)
        tiles = []
        for index in (first, second):
            place = cell_slot[jnp.maximum(index, 0)]
            at = pl.multiple_of(((place >> 1) & 3) * Q, Q)
            pair = packets[place >> 3, pl.ds(at, Q), :].astype(F32)
            pair = jnp.where(left64 == ((place & 1) == 0), pair, pltpu.roll(pair, Q, 1))
            tiles.append(jnp.where(index >= 0, pair, 0.0))
        out[dest, 0:Q, :] = jnp.where(left64, tiles[0], tiles[1]).astype(BF16)

        def index(i, j):
            inside = 0 <= i < 2 * ROWS
            return where_s[i, j] if inside else none

        up, low = 2 * dest - 1, 2 * dest + 2
        blocks = [two(index(up, j), index(up, j + 1), 0) for j in (0, 2, 4)]
        blocks += [two(index(low, j), index(low, j + 1), 1) for j in (0, 2, 4)]
        blocks.append(two(index(2 * dest, 0), index(2 * dest + 1, 0), 2))
        blocks.append(two(index(2 * dest, 5), index(2 * dest + 1, 5), 3))
        for i in range(4):
            both = jnp.concatenate([blocks[2 * i], blocks[2 * i + 1]], axis=0)
            out[dest, Q + 16 * i : Q + 16 * (i + 1), :] = both.astype(BF16)
        out[dest, 2 * Q : 2 * Q + 16, :] = info


def develop_kernel(tiles, ids, dose, threshold, across, side, down, out, wide, narrow):
    step = pl.program_id(0)
    row = lax.axis_index("rows")

    @pl.when(step == 0)
    def _():
        wide[...] = jnp.zeros_like(wide)

        def add(rows, value, j):
            if 0 <= j < 4:
                wide[rows, j * TILE : (j + 1) * TILE] += value[:, :TILE]
            if j >= 1:
                wide[rows, j * TILE - LANES : j * TILE] += value[:, TILE : TILE + LANES]
            if j <= 2:
                wide[rows, (j + 1) * TILE : (j + 1) * TILE + LANES] += value[:, TILE + LANES :]

        sources = [[ids[2 * row + i, j] // CELLS for j in range(4)] for i in range(2)]
        flat = sources[0] + sources[1]
        for i in range(2):
            for j in range(4):
                n = 4 * i + j
                rank = jnp.int32(0)
                for m in range(n):
                    rank = rank + (flat[m] == flat[n]).astype(jnp.int32)
                rank = jnp.minimum(rank, 1)
                value = dot(tiles[flat[n], 0:Q, :], across[rank]) * dose[i, j]
                add(slice(i * Q, (i + 1) * Q), value, j)

        strips = tiles[0, Q : 2 * Q, :].astype(F32)
        for source in range(1, ROWS):
            strips = strips + tiles[source, Q : 2 * Q, :].astype(F32)

        def doses(source):
            info = tiles[source, 2 * Q : 2 * Q + 16, :].astype(F32)
            return info + pltpu.roll(info, LANES - 4, 1) + pltpu.roll(info, LANES - 8, 1)

        own = doses(row)
        above = doses(jnp.maximum(row - 1, 0))
        below = doses(jnp.minimum(row + 1, ROWS - 1))
        lane_of = [7] + [20 + j for j in range(4)] + [36]
        for j in range(-1, 5):
            block, half = (j + 1) // 2, (j + 1) % 2
            upper = strips[block * 8 : (block + 1) * 8]
            lower = strips[24 + block * 8 : 24 + (block + 1) * 8]
            both = jnp.concatenate([upper, lower], axis=0).astype(BF16)
            value = dot(both, across[half])
            at = lane_of[j + 1]
            top = jnp.broadcast_to(above[1:2, at : at + 1], (REACH, 5 * LANES))
            bottom = jnp.broadcast_to(below[0:1, at : at + 1], (REACH, 5 * LANES))
            add(slice(2 * Q, 2 * Q + 16), value * jnp.concatenate([top, bottom], axis=0), j)

        sides = strips[48:64]
        for end in range(2):
            pixels = jnp.transpose(sides[8 * end : 8 * end + 8]).astype(BF16)
            at = lane_of[0] if end == 0 else lane_of[5]
            value = dot(pixels, side[8 * end : 8 * end + 8, :])
            scale = jnp.concatenate(
                [jnp.broadcast_to(own[i : i + 1, at : at + 1], (Q, LANES)) for i in range(2)],
                axis=0,
            )
            cols = slice(0, LANES) if end == 0 else slice(4 * TILE - LANES, 4 * TILE)
            wide[0 : 2 * Q, cols] += value * scale
        narrow[...] = wide[...].astype(BF16)

    columns = narrow[:, pl.ds(pl.multiple_of(step * TILE, TILE), TILE)]
    level = dot(down[0], columns) + dot(down[1], columns)
    out[...] = (0.5 * jnp.tanh(level - 4.0 * threshold[0]) + 0.5).astype(BF16)


def whole(array):
    return pl.BlockSpec(array.shape, lambda *_: (0,) * array.ndim)


def scalars():
    return pl.BlockSpec(memory_space=pltpu.SMEM)


PARAMS = pltpu.CompilerParams(vmem_limit_bytes=48 * 1024 * 1024)


def local(masks, owned_counts, cell_ids, kernels, kernel_weights, dose, threshold):
    table = {name: jnp.asarray(value) for name, value in tables().items()}

    constants = [
        table[n] for n in ("forward_cols", "forward_rows", "inverse_left", "inverse_right")
    ]
    packet = pl.pallas_call(
        imaging_kernel,
        grid=(SLOTS // 2,),
        out_shape=jax.ShapeDtypeStruct((COLS, PACKET, LANES), BF16),
        in_specs=[
            pl.BlockSpec((2, TILE, TILE), lambda s: (s, 0, 0)),
            whole(kernels),
            scalars(),
            whole(cell_ids),
            whole(dose),
            *[whole(t) for t in constants],
        ],
        out_specs=pl.BlockSpec((COLS, PACKET, LANES), lambda s: (0, 0, 0)),
        scratch_shapes=[
            pltpu.VMEM((2, GROUPS, NF, LANES), F32),
            pltpu.VMEM((16, LANES), F32),
        ],
        compiler_params=PARAMS,
    )(masks, kernels, kernel_weights, cell_ids, dose, *constants)

    packets = lax.all_to_all(packet, "cols", split_axis=0, concat_axis=0, tiled=True)

    outgoing = pl.pallas_call(
        routing_kernel,
        out_shape=jax.ShapeDtypeStruct((ROWS, OUTGOING, LANES), BF16),
        in_specs=[
            pl.BlockSpec(memory_space=pltpu.VMEM),
            scalars(),
            pl.BlockSpec(memory_space=pltpu.VMEM),
            pl.BlockSpec(memory_space=pltpu.VMEM),
        ],
        out_specs=pl.BlockSpec(memory_space=pltpu.VMEM),
        scratch_shapes=[
            pltpu.VMEM((CELLS, 32, LANES), F32),
            pltpu.VMEM((16, LANES), jnp.int32),
            pltpu.SMEM((16, LANES), jnp.int32),
            pltpu.SMEM((CELLS + SLOTS,), jnp.int32),
            pltpu.SemaphoreType.DMA,
        ],
        compiler_params=PARAMS,
    )(packets, owned_counts, table["edge"], table["edge_pad"])

    incoming = lax.all_to_all(outgoing, "rows", split_axis=0, concat_axis=0, tiled=True)

    constants = [table[n] for n in ("across", "side", "down")]
    return pl.pallas_call(
        develop_kernel,
        grid=(4,),
        out_shape=jax.ShapeDtypeStruct((2 * TILE, 4 * TILE), BF16),
        in_specs=[
            whole(incoming),
            scalars(),
            scalars(),
            scalars(),
            *[whole(t) for t in constants],
        ],
        out_specs=pl.BlockSpec((2 * TILE, TILE), lambda s: (0, s)),
        scratch_shapes=[
            pltpu.VMEM((OUTGOING, 4 * TILE), F32),
            pltpu.VMEM((OUTGOING, 4 * TILE), BF16),
        ],
        compiler_params=PARAMS,
    )(incoming, cell_ids, dose, threshold, *constants)


def solution(mesh):
    return jax.shard_map(
        local,
        mesh=mesh,
        in_specs=(
            P(("rows", "cols"), None, None),
            P(),
            P(None, "cols"),
            P(),
            P(),
            P("rows", "cols"),
            P(),
        ),
        out_specs=P("rows", "cols"),
        check_vma=False,
    )
```

profile of v0, /device:TPU:1, one launch (start us, length us, event | category | flops | bytes accessed | tf_op | source)
XLA Modules:
  0.0 59.6 jit_solution(14292434864134131866)
XLA Ops:
  0.0 0.8 %copy.17.ids = s32[16,4]{1,0:T(8,128)S(1)} copy(s32[16,4]{0,1:T(4,128)} %param.18) | data formatting | bytes 512 | tf_op args[2]
  0.8 1.5 %copy-done = bf16[6,384,384]{2,1,0:T(8,128)(2,1)S(1)} copy-done((bf16[6,384,384]{2,1,0:T(8,128)(2,1)S(1)}, bf16[6,384,384]{2,1,0:T(8,128)(2,1)}, u32[]{:S(2)}) %copy-start) | copy-done | bytes 1769496
  2.2 1.0 %copy-done.2 = f32[2,16,32,32]{3,2,1,0:T(8,128)S(1)} copy-done((f32[2,16,32,32]{3,2,1,0:T(8,128)S(1)}, f32[2,16,32,32]{3,2,1,0:T(8,128)}, u32[]{:S(2)}) %copy-start.2) | copy-done | bytes 131096
  3.3 1.0 %copy-done.3 = bf16[2,256,512]{2,1,0:T(8,128)(2,1)S(1)} copy-done((bf16[2,256,512]{2,1,0:T(8,128)(2,1)S(1)}, bf16[2,256,512]{2,1,0:T(8,128)(2,1)}, u32[]{:S(2)}) %copy-start.3) | copy-done | bytes 524312
  4.3 0.9 %copy-done.5 = bf16[384,128]{1,0:T(8,128)(2,1)S(1)} copy-done((bf16[384,128]{1,0:T(8,128)(2,1)S(1)}, bf16[384,128]{1,0:T(8,128)(2,1)}, u32[]{:S(2)}) %copy-start.5) | copy-done | bytes 98328
  5.2 0.9 %copy-done.6 = bf16[128,384]{1,0:T(8,128)(2,1)S(1)} copy-done((bf16[128,384]{1,0:T(8,128)(2,1)S(1)}, bf16[128,384]{1,0:T(8,128)(2,1)}, u32[]{:S(2)}) %copy-start.6) | copy-done | bytes 98328
  6.1 0.8 %copy-done.7 = bf16[128,192]{1,0:T(8,128)(2,1)S(1)} copy-done((bf16[128,192]{1,0:T(8,128)(2,1)S(1)}, bf16[128,192]{1,0:T(8,128)(2,1)}, u32[]{:S(2)}) %copy-start.7) | copy-done | bytes 49176
  6.9 0.7 %copy-done.12 = f32[2,4]{1,0:T(2,128)S(1)} copy-done((f32[2,4]{1,0:T(2,128)S(1)}, f32[2,4]{1,0:T(2,128)}, u32[]{:S(2)}) %copy-start.12) | copy-done | bytes 56
  7.6 0.7 %copy-done.14 = f32[16]{0:T(128)S(1)} copy-done((f32[16]{0:T(128)S(1)}, f32[16]{0:T(128)}, u32[]{:S(2)}) %copy-start.14) | copy-done | bytes 88
  8.3 7.7 %shard_map.154 = bf16[16,208,128]{2,1,0:T(8,128)(2,1)S(1)} custom-call(bf16[6,384,384]{2,1,0:T(8,128)(2,1)S(1)} %copy-done, f32[2,16,32,32]{3,2,1,0:T(8,128)S(1)} %copy-done.2, f32[16]{0:T(128)S(1)} %copy-done.14, s32[16,4]{1,0:T(8,128)S(1)} %copy.17.ids, f32[2,4]{1,0:T(2,128)S(1)} %copy-done.12, bf16[384,128]{1,0:T(8,128)(2,1)S(1)} %copy-done.5, ...), custom_call_target="tpu_custom_call" | custom-call | tf_op jit(solution)/shard_map/pallas_call | solution.py:385
  16.0 0.0 copy-start.1
  16.0 0.0 copy-start.4
  16.0 0.0 copy-start.11
  16.0 0.0 copy-start.13
  16.1 22.4 %all_to_all.10.packets = bf16[16,208,128]{2,1,0:T(8,128)(2,1)S(1)} all-to-all(bf16[16,208,128]{2,1,0:T(8,128)(2,1)S(1)} %shard_map.154), channel_id=1, replica_groups=mesh['rows'=8,'cols'=16] {'cols'}, dimensions={0} | all-to-all | bytes 1703936 | tf_op jit(solution)/shard_map/all_to_all | solution.py:405
  38.5 0.0 copy-done.8
  38.5 0.0 copy-done.9
  38.5 0.0 copy-done.10
  38.5 3.5 %shard_map.155 = bf16[8,144,128]{2,1,0:T(8,128)(2,1)} custom-call(bf16[16,208,128]{2,1,0:T(8,128)(2,1)S(1)} %all_to_all.10.packets, s32[8,16]{1,0:T(8,128)S(1)} %copy-done.9, bf16[16,64]{1,0:T(8,128)(2,1)S(1)} %copy-done.10, bf16[2,16,128]{2,1,0:T(8,128)(2,1)S(1)} %copy-done.8), custom_call_target="tpu_custom_call" | custom-call | tf_op jit(solution)/shard_map/pallas_call | solution.py:407
  42.0 6.2 %all-to-all-start.1 = ((bf16[8,144,128]{2,1,0:T(8,128)(2,1)}), bf16[8,144,128]{2,1,0:T(8,128)(2,1)S(1)}, u32[]{:S(2)}, u32[]{:S(2)}) async-start(bf16[8,144,128]{2,1,0:T(8,128)(2,1)} %shard_map.155), calls=%async_computation.1 | async-start | bytes 589824 | tf_op jit(solution)/shard_map/all_to_all | solution.py:427
  48.8 6.2 %all-to-all-done.1.tiles = bf16[8,144,128]{2,1,0:T(8,128)(2,1)S(1)} async-done(((bf16[8,144,128]{2,1,0:T(8,128)(2,1)}), bf16[8,144,128]{2,1,0:T(8,128)(2,1)S(1)}, u32[]{:S(2)}, u32[]{:S(2)}) %all-to-all-start.1) | async-done | bytes 294944 | tf_op jit(solution)/shard_map/all_to_all | solution.py:427
  54.9 0.0 copy-done.1
  54.9 0.0 copy-done.11
  55.0 4.6 %shard_map.156 = bf16[768,1536]{1,0:T(8,128)(2,1)} custom-call(bf16[8,144,128]{2,1,0:T(8,128)(2,1)S(1)} %all-to-all-done.1.tiles, s32[16,4]{1,0:T(8,128)S(1)} %copy.17.ids, f32[2,4]{1,0:T(2,128)S(1)} %copy-done.13, f32[1]{0:T(128)S(6)} %copy.19.threshold, bf16[2,128,640]{2,1,0:T(8,128)(2,1)S(1)} %copy-done.4, bf16[16,128]{1,0:T(8,128)(2,1)S(1)} %copy-done.11, ...), custom_call_target="tpu_custom_call" | custom-call | tf_op jit(solution)/shard_map/pallas_call | solution.py:430
  (13 shorter events, 0.0 us)
Async XLA Ops:
  0.8 1.5 %copy-start = (bf16[6,384,384]{2,1,0:T(8,128)(2,1)S(1)}, bf16[6,384,384]{2,1,0:T(8,128)(2,1)}, u32[]{:S(2)}) copy-start(bf16[6,384,384]{2,1,0:T(8,128)(2,1)} %mask.1) | copy-start | bytes 5308420
  2.2 1.0 %copy-start.2 = (f32[2,16,32,32]{3,2,1,0:T(8,128)S(1)}, f32[2,16,32,32]{3,2,1,0:T(8,128)}, u32[]{:S(2)}) copy-start(f32[2,16,32,32]{3,2,1,0:T(8,128)} %kernels.1) | copy-start | bytes 393220
  3.3 1.0 %copy-start.3 = (bf16[2,256,512]{2,1,0:T(8,128)(2,1)S(1)}, bf16[2,256,512]{2,1,0:T(8,128)(2,1)}, u32[]{:S(2)}) copy-start(bf16[2,256,512]{2,1,0:T(8,128)(2,1)} %constant.21.clone.inv_right) | copy-start | bytes 1572868
  4.3 0.9 %copy-start.5 = (bf16[384,128]{1,0:T(8,128)(2,1)S(1)}, bf16[384,128]{1,0:T(8,128)(2,1)}, u32[]{:S(2)}) copy-start(bf16[384,128]{1,0:T(8,128)(2,1)} %constant.19.clone.fwd_cols) | copy-start | bytes 294916
  5.2 0.9 %copy-start.6 = (bf16[128,384]{1,0:T(8,128)(2,1)S(1)}, bf16[128,384]{1,0:T(8,128)(2,1)}, u32[]{:S(2)}) copy-start(bf16[128,384]{1,0:T(8,128)(2,1)} %constant.18.clone.fwd_rows) | copy-start | bytes 294916
  6.1 0.8 %copy-start.7 = (bf16[128,192]{1,0:T(8,128)(2,1)S(1)}, bf16[128,192]{1,0:T(8,128)(2,1)}, u32[]{:S(2)}) copy-start(bf16[128,192]{1,0:T(8,128)(2,1)} %constant.20.clone.inv_left) | copy-start | bytes 147460
  6.9 0.7 %copy-start.12 = (f32[2,4]{1,0:T(2,128)S(1)}, f32[2,4]{1,0:T(2,128)}, u32[]{:S(2)}) copy-start(f32[2,4]{1,0:T(2,128)} %dose.3) | copy-start | bytes 100
  7.6 0.7 %copy-start.14 = (f32[16]{0:T(128)S(1)}, f32[16]{0:T(128)}, u32[]{:S(2)}) copy-start(f32[16]{0:T(128)} %weights.1) | copy-start | bytes 196
  8.3 30.2 %copy-start.8 = (bf16[2,16,128]{2,1,0:T(8,128)(2,1)S(1)}, bf16[2,16,128]{2,1,0:T(8,128)(2,1)}, u32[]{:S(2)}) copy-start(bf16[2,16,128]{2,1,0:T(8,128)(2,1)} %constant.23.clone.edge_pad) | copy-start | bytes 24580
  8.3 30.2 %copy-start.9 = (s32[8,16]{1,0:T(8,128)S(1)}, s32[8,16]{1,0:T(8,128)}, u32[]{:S(2)}) copy-start(s32[8,16]{1,0:T(8,128)} %counts.1) | copy-start | bytes 1540
  8.3 30.2 %copy-start.10 = (bf16[16,64]{1,0:T(8,128)(2,1)S(1)}, bf16[16,64]{1,0:T(8,128)(2,1)}, u32[]{:S(2)}) copy-start(bf16[16,64]{1,0:T(8,128)(2,1)} %constant.22.clone.edge) | copy-start | bytes 6148
  16.0 38.9 %copy-start.1 = (bf16[2,768,144]{2,1,0:T(8,128)(2,1)S(1)}, bf16[2,768,144]{2,1,0:T(8,128)(2,1)}, u32[]{:S(2)}) copy-start(bf16[2,768,144]{2,1,0:T(8,128)(2,1)} %constant.25.clone.down) | copy-start | bytes 1327108
  16.0 38.9 %copy-start.4 = (bf16[2,128,640]{2,1,0:T(8,128)(2,1)S(1)}, bf16[2,128,640]{2,1,0:T(8,128)(2,1)}, u32[]{:S(2)}) copy-start(bf16[2,128,640]{2,1,0:T(8,128)(2,1)} %constant.24.clone.across) | copy-start | bytes 983044
  16.0 38.9 %copy-start.11 = (bf16[16,128]{1,0:T(8,128)(2,1)S(1)}, bf16[16,128]{1,0:T(8,128)(2,1)}, u32[]{:S(2)}) copy-start(bf16[16,128]{1,0:T(8,128)(2,1)} %constant.26.clone.side) | copy-start | bytes 12292
  16.0 38.9 %copy-start.13 = (f32[2,4]{1,0:T(2,128)S(1)}, f32[2,4]{1,0:T(2,128)}, u32[]{:S(2)}) copy-start(f32[2,4]{1,0:T(2,128)} %dose.3) | copy-start | bytes 100
  42.0 13.0 %all-to-all-start.1 = ((bf16[8,144,128]{2,1,0:T(8,128)(2,1)}), bf16[8,144,128]{2,1,0:T(8,128)(2,1)S(1)}, u32[]{:S(2)}, u32[]{:S(2)}) async-start(bf16[8,144,128]{2,1,0:T(8,128)(2,1)} %shard_map.155), calls=%async_computation.1 | async-start | bytes 589824 | tf_op jit(solution)/shard_map/all_to_all | solution.py:427
where the time goes:
time: 60.1 us; the launch traced here: 59.6 us
  blocking collectives  22.4 us (37%)
  Pallas kernels  15.8 us (26%)
  local copies, waits for them, and re-layouts  8.31 us (14%)
  starting transfers between devices  6.16 us (10%)
  waiting for transfers between devices  6.16 us (10%)
  between operations  0.73 us (1%)
    all_to_all x1, blocking collectives, local(): lax.all_to_all(packet, 'cols', split_axis=0, concat_axis=0, tiled=True)  22.4 us
    unnamed x31, local copies, waits for them, and re-layouts  8.31 us
    pallas_call x1, Pallas kernels, local(): pl.pallas_call(imaging_kernel, grid=(SLOTS // 2,), out_shape=jax.ShapeDty...  7.72 us
    all_to_all x1, waiting for transfers between devices, local(): lax.all_to_all(outgoing, 'rows', split_axis=0, concat_axis=0, tiled=True)  6.16 us
    all_to_all x1, starting transfers between devices, local(): lax.all_to_all(outgoing, 'rows', split_axis=0, concat_axis=0, tiled=True)  6.16 us
    pallas_call x1, Pallas kernels, local(): pl.pallas_call(develop_kernel, grid=(4,), out_shape=jax.ShapeDtypeStruct(...  4.62 us
    pallas_call x1, Pallas kernels, local(): pl.pallas_call(routing_kernel, out_shape=jax.ShapeDtypeStruct((ROWS, OUTG...  3.48 us
  transfers between devices with their start and end apart: 1, of which 1 were waited for; matrix products, arithmetic and copies ran while one was open for 0% of the time, Pallas kernels for 0%

commit v1 on v0

--- a/solution.py
+++ b/solution.py
@@ -22,7 +22,6 @@
 INFO = 3 * Q
 PACKET = INFO + 16
 OUTGOING = 2 * Q + 16
-GROUPS = NK // 4
 BF16 = jnp.bfloat16
 F32 = jnp.float32
 
@@ -46,18 +45,18 @@
 
     turn = np.mod(points[:, None] * freq[None, :], Q) * (2.0 * np.pi / Q)
     cos, sin = np.cos(turn), np.sin(turn)
-    left = np.block([[cos, -sin], [sin, cos]])
-    high, low = split(left)
+    high, low = split(np.concatenate([cos, -sin], axis=1))
     inverse_left = np.concatenate([high, high, low], axis=1)
-    right = np.zeros((2 * LANES, 4 * LANES))
-    for k in range(4):
-        re = slice(k * NF, (k + 1) * NF)
-        im = slice(LANES + k * NF, LANES + (k + 1) * NF)
+    right = np.zeros((LANES, 2 * LANES))
+    for k in range(2):
+        re = slice(2 * k * NF, (2 * k + 1) * NF)
+        im = slice((2 * k + 1) * NF, (2 * k + 2) * NF)
         out_re = slice(k * LANES, k * LANES + Q)
         out_im = slice(k * LANES + Q, (k + 1) * LANES)
         right[re, out_re], right[re, out_im] = cos.T, sin.T
         right[im, out_re], right[im, out_im] = -sin.T, cos.T
-    inverse_right = np.stack(split(right))
+    high, low = split(right)
+    inverse_right = np.concatenate([high, high, low])
 
     harmonic = np.arange(Q) - Q // 2
     fine = np.mod(pixels[:, None] * harmonic[None, :], TILE) * (2.0 * np.pi / TILE)
@@ -135,40 +134,53 @@
 
 
 def imaging_kernel(
-    mask, kernels, weights, ids, dose, fwd_cols, fwd_rows, inv_left, inv_right, out, ker, info
+    mask, kernels, weights, ids, dose, fwd_cols, fwd_rows, inv_left, inv_right,
+    out,
+    mask_v, kernels_v, weights_s, ids_v, dose_v, cols_v, rows_v, left_v, right_v,
+    ker, info, sems,
 ):
-    step = pl.program_id(0)
-
-    @pl.when(step == 0)
-    def _():
-        for part in range(2):
-            for group in range(GROUPS):
-                four = [
-                    kernels[part, 4 * group + i]
-                    * jnp.sqrt(jnp.full((NF, NF), weights[4 * group + i], F32))
-                    for i in range(4)
-                ]
-                ker[part, group] = jnp.concatenate(four, axis=1)
-        info[...] = jnp.zeros_like(info)
-        info[:, 0:4] = ids[...].astype(F32)
-        first = dose[...].astype(BF16).astype(F32)
-        second = (dose[...] - first).astype(BF16).astype(F32)
-        info[0:2, 4:8] = first
-        info[0:2, 8:12] = second
-        info[0:2, 12:16] = dose[...] - first - second
-        packed = info[...].astype(BF16)
-        for c in range(COLS):
-            out[c, INFO : INFO + 16, :] = packed
-
-    lane = lanes_of((NF, LANES))
-    even = (lane // NF) % 2 == 0
+    moves = [(kernels, kernels_v), (weights, weights_s), (fwd_cols, cols_v)]
+    moves += [(mask.at[s], mask_v.at[s]) for s in range(SLOTS)]
+    moves += [(fwd_rows, rows_v), (inv_left, left_v), (inv_right, right_v)]
+    moves += [(ids, ids_v), (dose, dose_v)]
+    copies = [
+        pltpu.make_async_copy(src, dst, sems.at[i]) for i, (src, dst) in enumerate(moves)
+    ]
+    for copy in copies:
+        copy.start()
+    copies[0].wait()
+    copies[1].wait()
+    for two in range(NK // 2):
+        re, im = [], []
+        for k in (2 * two, 2 * two + 1):
+            scale = jnp.sqrt(jnp.full((NF, NF), weights_s[k], F32))
+            re.append(kernels_v[0, k] * scale)
+            im.append(kernels_v[1, k] * scale)
+        ker[0, two] = jnp.concatenate([re[0], im[0], re[1], im[1]], axis=1)
+        ker[1, two] = jnp.concatenate([-im[0], re[0], -im[1], re[1]], axis=1)
+    for copy in copies[2:]:
+        copy.wait()
+
+    info[...] = jnp.zeros_like(info)
+    info[0:4, 0:16] = ids_v[...].astype(F32)
+    first = dose_v[...].astype(BF16).astype(F32)
+    second = (dose_v[...] - first).astype(BF16).astype(F32)
+    info[8:10, 4:8] = first
+    info[8:10, 8:12] = second
+    info[8:10, 12:16] = dose_v[...] - first - second
+    packed = info[...].astype(BF16)
+    for c in range(COLS):
+        out[c, INFO : INFO + 16, :] = packed
+
+    even = (lanes_of((NF, LANES)) // NF) % 2 == 0
+    left = lanes_of((TILE, LANES)) < Q
     images = []
-    for slot in range(2):
-        cols = dot(mask[slot], fwd_cols[...])
+    for slot in range(SLOTS):
+        cols = dot(mask_v[slot], cols_v[...])
         cols = cols + pltpu.roll(cols, Q, 1)
-        high, low = halves(cols)
-        pair = jnp.where(lanes_of((TILE, LANES)) < Q, high.astype(F32), low.astype(F32))
-        both = dot(fwd_rows[...], pair.astype(BF16))
+        high = cols.astype(BF16).astype(F32)
+        pair = jnp.where(left, high, cols - high).astype(BF16)
+        both = dot(rows_v[...], pair)
         both = both[:Q] + both[Q:]
         both = both + pltpu.roll(both, Q, 1)
         top, bottom = both[:NF], both[NF:]
@@ -177,32 +189,31 @@
         real = jnp.where(even, real, pltpu.roll(real, NF, 1))
         imag = jnp.where(even, imag, pltpu.roll(imag, NF, 1))
         highs, lows = [], []
-        for group in range(GROUPS):
-            kr, ki = ker[0, group], ker[1, group]
-            prod = jnp.concatenate([kr * real - ki * imag, kr * imag + ki * real], axis=0)
+        for two in range(NK // 2):
+            ka, kb = ker[0, two], ker[1, two]
+            prod = jnp.concatenate([ka * real + kb * imag, ka * imag - kb * real], axis=0)
             high, low = halves(prod)
             highs.append(high)
             lows.append(low)
         high = jnp.concatenate(highs, axis=1)
         low = jnp.concatenate(lows, axis=1)
-        half = dot(inv_left[...], jnp.concatenate([high, low, high], axis=0))
-        blocks = []
-        for group in range(GROUPS):
-            g = slice(group * LANES, (group + 1) * LANES)
-            blocks.append(jnp.concatenate([half[:Q, g], half[Q:, g]], axis=1))
-        high, low = halves(jnp.concatenate(blocks, axis=0))
-        field = dot(high, inv_right[0]) + (dot(high, inv_right[1]) + dot(low, inv_right[0]))
+        half = dot(left_v[...], jnp.concatenate([high, low, high], axis=0))
+        rows = jnp.concatenate(
+            [half[:, i * LANES : (i + 1) * LANES] for i in range(NK // 2)], axis=0
+        )
+        high, low = halves(rows)
+        field = dot(jnp.concatenate([high, low, high], axis=1), right_v[...])
         power = field * field
-        total = None
-        for group in range(GROUPS):
-            for k in range(4):
-                part = power[group * Q : (group + 1) * Q, k * LANES : (k + 1) * LANES]
-                total = part if total is None else total + part
+        power = power[:, :LANES] + power[:, LANES:]
+        total = power[:Q]
+        for i in range(1, NK // 2):
+            total = total + power[i * Q : (i + 1) * Q]
         images.append(total + pltpu.roll(total, Q, 1))
-    tile = jnp.where(lanes_of((Q, LANES)) < Q, images[0], images[1]).astype(BF16)
-    at = pl.multiple_of(step * Q, Q)
-    for c in range(COLS):
-        out[c, pl.ds(at, Q), :] = tile
+    left = lanes_of((Q, LANES)) < Q
+    for i in range(SLOTS // 2):
+        tile = jnp.where(left, images[2 * i], images[2 * i + 1]).astype(BF16)
+        for c in range(COLS):
+            out[c, i * Q : (i + 1) * Q, :] = tile
 
 
 def routing_kernel(
@@ -214,13 +225,14 @@
     after = packets[jnp.minimum(col + 1, COLS - 1), INFO : INFO + 16, :].astype(F32)
     lane = lanes_of((16, LANES))
 
+    line = lax.broadcasted_iota(jnp.int32, (16, LANES), 0)
     window = jnp.where(
-        lane == 0,
-        pltpu.roll(before, LANES - 3, 1),
-        jnp.where(lane < 5, pltpu.roll(here, 1, 1), pltpu.roll(after, 5, 1)),
+        line == 0,
+        pltpu.roll(before, 13, 0),
+        jnp.where(line < 5, pltpu.roll(here, 1, 0), pltpu.roll(after, 5, 0)),
     ).astype(jnp.int32)
     cell = window - row * CELLS
-    exists = ((lane > 0) | (col > 0)) & ((lane < 5) | (col < COLS - 1)) & (lane < 6)
+    exists = ((line > 0) | (col > 0)) & ((line < 5) | (col < COLS - 1)) & (line < 6)
     mine = (cell >= 0) & (cell < CELLS) & exists
     where_v[...] = jnp.where(mine, cell, -1)
     copy = pltpu.make_async_copy(where_v, where_s, sem)
@@ -268,7 +280,7 @@
         first, second = none, none
         for i in range(2):
             for j in range(4):
-                here_cell = where_s[2 * dest + i, 1 + j]
+                here_cell = where_s[1 + j, 2 * dest + i]
                 held = here_cell >= 0
                 second = jnp.where(held & (first >= 0) & (second < 0), here_cell, second)
                 first = jnp.where(held & (first < 0), here_cell, first)
@@ -283,7 +295,7 @@
 
         def index(i, j):
             inside = 0 <= i < 2 * ROWS
-            return where_s[i, j] if inside else none
+            return where_s[j, i] if inside else none
 
         up, low = 2 * dest - 1, 2 * dest + 2
         blocks = [two(index(up, j), index(up, j + 1), 0) for j in (0, 2, 4)]
@@ -312,7 +324,7 @@
             if j <= 2:
                 wide[rows, (j + 1) * TILE : (j + 1) * TILE + LANES] += value[:, TILE + LANES :]
 
-        sources = [[ids[2 * row + i, j] // CELLS for j in range(4)] for i in range(2)]
+        sources = [[ids[j, 2 * row + i] // CELLS for j in range(4)] for i in range(2)]
         flat = sources[0] + sources[1]
         for i in range(2):
             for j in range(4):
@@ -329,7 +341,7 @@
             strips = strips + tiles[source, Q : 2 * Q, :].astype(F32)
 
         def doses(source):
-            info = tiles[source, 2 * Q : 2 * Q + 16, :].astype(F32)
+            info = tiles[source, 2 * Q : 2 * Q + 16, :].astype(F32)[8:]
             return info + pltpu.roll(info, LANES - 4, 1) + pltpu.roll(info, LANES - 8, 1)
 
         own = doses(row)
@@ -379,28 +391,28 @@
 def local(masks, owned_counts, cell_ids, kernels, kernel_weights, dose, threshold):
     table = {name: jnp.asarray(value) for name, value in tables().items()}
 
+    ids = cell_ids.T
     constants = [
         table[n] for n in ("forward_cols", "forward_rows", "inverse_left", "inverse_right")
     ]
+    operands = [masks, kernels, kernel_weights, ids, dose, *constants]
+    placed = [pltpu.with_memory_space_constraint(op, pltpu.HBM) for op in operands]
     packet = pl.pallas_call(
         imaging_kernel,
-        grid=(SLOTS // 2,),
         out_shape=jax.ShapeDtypeStruct((COLS, PACKET, LANES), BF16),
-        in_specs=[
-            pl.BlockSpec((2, TILE, TILE), lambda s: (s, 0, 0)),
-            whole(kernels),
-            scalars(),
-            whole(cell_ids),
-            whole(dose),
-            *[whole(t) for t in constants],
-        ],
-        out_specs=pl.BlockSpec((COLS, PACKET, LANES), lambda s: (0, 0, 0)),
+        in_specs=[pl.BlockSpec(memory_space=pltpu.HBM)] * len(operands),
+        out_specs=pl.BlockSpec(memory_space=pltpu.VMEM),
         scratch_shapes=[
-            pltpu.VMEM((2, GROUPS, NF, LANES), F32),
+            *[
+                (pltpu.SMEM if op is kernel_weights else pltpu.VMEM)(op.shape, op.dtype)
+                for op in operands
+            ],
+            pltpu.VMEM((2, NK // 2, NF, LANES), F32),
             pltpu.VMEM((16, LANES), F32),
+            pltpu.SemaphoreType.DMA((len(operands) + SLOTS - 1,)),
         ],
         compiler_params=PARAMS,
-    )(masks, kernels, kernel_weights, cell_ids, dose, *constants)
+    )(*placed)
 
     packets = lax.all_to_all(packet, "cols", split_axis=0, concat_axis=0, tiled=True)
 
@@ -444,7 +456,7 @@
             pltpu.VMEM((OUTGOING, 4 * TILE), BF16),
         ],
         compiler_params=PARAMS,
-    )(incoming, cell_ids, dose, threshold, *constants)
+    )(incoming, ids, dose, threshold, *constants)
 
 
 def solution(mesh):

time: 60.1 us -> 51.2 us (0.85)
  local copies, waits for them, and re-layouts: 8.31 us -> 0.04 us
    unnamed x31 -> x16, local copies, waits for them, and re-layouts: 8.31 us -> 0.04 us
where the time goes in v1:
time: 51.2 us; the launch traced here: 50.9 us
  blocking collectives  22.4 us (44%)
  Pallas kernels  15.4 us (30%)
  starting transfers between devices  6.17 us (12%)
  waiting for transfers between devices  6.16 us (12%)
  between operations  0.74 us (1%)
    all_to_all x1, blocking collectives, local(): lax.all_to_all(packet, 'cols', split_axis=0, concat_axis=0, tiled=True)  22.4 us
    pallas_call x1, Pallas kernels, local(): pl.pallas_call(imaging_kernel, out_shape=jax.ShapeDtypeStruct((COLS, PACK...  7.37 us
    all_to_all x1, starting transfers between devices, local(): lax.all_to_all(outgoing, 'rows', split_axis=0, concat_axis=0, tiled=True)  6.17 us
    all_to_all x1, waiting for transfers between devices, local(): lax.all_to_all(outgoing, 'rows', split_axis=0, concat_axis=0, tiled=True)  6.16 us
    pallas_call x1, Pallas kernels, local(): pl.pallas_call(develop_kernel, grid=(4,), out_shape=jax.ShapeDtypeStruct(...  4.52 us
    pallas_call x1, Pallas kernels, local(): pl.pallas_call(routing_kernel, out_shape=jax.ShapeDtypeStruct((ROWS, OUTG...  3.53 us
  transfers between devices with their start and end apart: 1, of which 1 were waited for; matrix products, arithmetic and copies ran while one was open for 0% of the time, Pallas kernels for 0%

profile of v1, /device:TPU:1, one launch (start us, length us, event | category | flops | bytes accessed | tf_op | source)
XLA Modules:
  0.0 50.9 jit_solution(5349624157474836616)
XLA Ops:
  0.0 0.0 copy-start.3
  0.0 0.0 copy-start.4
  0.0 0.0 copy-start.6
  0.0 7.4 %shard_map.154 = bf16[16,208,128]{2,1,0:T(8,128)(2,1)S(1)} custom-call(bf16[6,384,384]{2,1,0:T(8,128)(2,1)} %mask.1, f32[2,16,32,32]{3,2,1,0:T(8,128)} %kernels.1, f32[16]{0:T(128)} %weights.1, s32[4,16]{1,0:T(4,128)} %bitcast.1, f32[2,4]{1,0:T(2,128)} %dose.3, bf16[384,128]{1,0:T(8,128)(2,1)} %constant.19.clone.fwd_cols, ...), custom_call_target="tpu_custom_call" | custom-call | tf_op jit(solution)/shard_map/pallas_call | solution.py:400
  7.4 0.0 copy-start
  7.4 0.0 copy-start.1
  7.4 0.0 copy-start.2
  7.4 0.0 copy-start.5
  7.4 0.0 copy-start.7
  7.4 22.4 %all_to_all.10.packets = bf16[16,208,128]{2,1,0:T(8,128)(2,1)S(1)} all-to-all(bf16[16,208,128]{2,1,0:T(8,128)(2,1)S(1)} %shard_map.154), channel_id=1, replica_groups=mesh['rows'=8,'cols'=16] {'cols'}, dimensions={0} | all-to-all | bytes 1703936 | tf_op jit(solution)/shard_map/all_to_all | solution.py:417
  29.9 0.0 copy-done.3
  29.9 0.0 copy-done.4
  29.9 0.0 copy-done.6
  29.9 3.5 %shard_map.155 = bf16[8,144,128]{2,1,0:T(8,128)(2,1)} custom-call(bf16[16,208,128]{2,1,0:T(8,128)(2,1)S(1)} %all_to_all.10.packets, s32[8,16]{1,0:T(8,128)S(1)} %copy-done.4, bf16[16,64]{1,0:T(8,128)(2,1)S(1)} %copy-done.6, bf16[2,16,128]{2,1,0:T(8,128)(2,1)S(1)} %copy-done.3), custom_call_target="tpu_custom_call" | custom-call | tf_op jit(solution)/shard_map/pallas_call | solution.py:419
  33.4 6.2 %all-to-all-start.1 = ((bf16[8,144,128]{2,1,0:T(8,128)(2,1)}), bf16[8,144,128]{2,1,0:T(8,128)(2,1)S(1)}, u32[]{:S(2)}, u32[]{:S(2)}) async-start(bf16[8,144,128]{2,1,0:T(8,128)(2,1)} %shard_map.155), calls=%async_computation.1 | async-start | bytes 589824 | tf_op jit(solution)/shard_map/all_to_all | solution.py:439
  40.2 6.2 %all-to-all-done.1.tiles = bf16[8,144,128]{2,1,0:T(8,128)(2,1)S(1)} async-done(((bf16[8,144,128]{2,1,0:T(8,128)(2,1)}), bf16[8,144,128]{2,1,0:T(8,128)(2,1)S(1)}, u32[]{:S(2)}, u32[]{:S(2)}) %all-to-all-start.1) | async-done | bytes 294944 | tf_op jit(solution)/shard_map/all_to_all | solution.py:439
  46.4 0.0 copy-done
  46.4 0.0 copy-done.1
  46.4 0.0 copy-done.2
  46.4 0.0 copy-done.5
  46.4 0.0 copy-done.7
  46.4 4.5 %shard_map.156 = bf16[768,1536]{1,0:T(8,128)(2,1)} custom-call(bf16[8,144,128]{2,1,0:T(8,128)(2,1)S(1)} %all-to-all-done.1.tiles, s32[4,16]{1,0:T(4,128)S(1)} %bitcast.2, f32[2,4]{1,0:T(2,128)S(1)} %copy-done.7, f32[1]{0:T(128)S(6)} %copy.17.threshold, bf16[2,128,640]{2,1,0:T(8,128)(2,1)S(1)} %copy-done.1, bf16[16,128]{1,0:T(8,128)(2,1)S(1)} %copy-done.5, ...), custom_call_target="tpu_custom_call" | custom-call | tf_op jit(solution)/shard_map/pallas_call | solution.py:442
Async XLA Ops:
  0.0 29.9 %copy-start.3 = (bf16[2,16,128]{2,1,0:T(8,128)(2,1)S(1)}, bf16[2,16,128]{2,1,0:T(8,128)(2,1)}, u32[]{:S(2)}) copy-start(bf16[2,16,128]{2,1,0:T(8,128)(2,1)} %constant.23.clone.edge_pad) | copy-start | bytes 24580
  0.0 29.9 %copy-start.4 = (s32[8,16]{1,0:T(8,128)S(1)}, s32[8,16]{1,0:T(8,128)}, u32[]{:S(2)}) copy-start(s32[8,16]{1,0:T(8,128)} %counts.1) | copy-start | bytes 1540
  0.0 29.9 %copy-start.6 = (bf16[16,64]{1,0:T(8,128)(2,1)S(1)}, bf16[16,64]{1,0:T(8,128)(2,1)}, u32[]{:S(2)}) copy-start(bf16[16,64]{1,0:T(8,128)(2,1)} %constant.22.clone.edge) | copy-start | bytes 6148
  7.4 39.0 %copy-start = (bf16[2,768,144]{2,1,0:T(8,128)(2,1)S(1)}, bf16[2,768,144]{2,1,0:T(8,128)(2,1)}, u32[]{:S(2)}) copy-start(bf16[2,768,144]{2,1,0:T(8,128)(2,1)} %constant.25.clone.down) | copy-start | bytes 1327108
  7.4 39.0 %copy-start.1 = (bf16[2,128,640]{2,1,0:T(8,128)(2,1)S(1)}, bf16[2,128,640]{2,1,0:T(8,128)(2,1)}, u32[]{:S(2)}) copy-start(bf16[2,128,640]{2,1,0:T(8,128)(2,1)} %constant.24.clone.across) | copy-start | bytes 983044
  7.4 39.0 %copy-start.2 = (s32[16,4]{0,1:T(4,128)S(1)}, s32[16,4]{0,1:T(4,128)}, u32[]{:S(2)}) copy-start(s32[16,4]{0,1:T(4,128)} %param.18) | copy-start | bytes 772
  7.4 39.0 %copy-start.5 = (bf16[16,128]{1,0:T(8,128)(2,1)S(1)}, bf16[16,128]{1,0:T(8,128)(2,1)}, u32[]{:S(2)}) copy-start(bf16[16,128]{1,0:T(8,128)(2,1)} %constant.26.clone.side) | copy-start | bytes 12292
  7.4 39.0 %copy-start.7 = (f32[2,4]{1,0:T(2,128)S(1)}, f32[2,4]{1,0:T(2,128)}, u32[]{:S(2)}) copy-start(f32[2,4]{1,0:T(2,128)} %dose.3) | copy-start | bytes 100
  33.4 13.0 %all-to-all-start.1 = ((bf16[8,144,128]{2,1,0:T(8,128)(2,1)}), bf16[8,144,128]{2,1,0:T(8,128)(2,1)S(1)}, u32[]{:S(2)}, u32[]{:S(2)}) async-start(bf16[8,144,128]{2,1,0:T(8,128)(2,1)} %shard_map.155), calls=%async_computation.1 | async-start | bytes 589824 | tf_op jit(solution)/shard_map/all_to_all | solution.py:439

commit v2 on v1

v2 whole, which is shorter than its diff:
```python
import functools

import jax
import jax.numpy as jnp
import ml_dtypes
import numpy as np
from jax import lax
from jax.experimental import pallas as pl
from jax.experimental.pallas import tpu as pltpu
from jax.sharding import PartitionSpec as P

REACH = 8
TILE = 384
NF = 32
NK = 16
Q = 64
SLOTS = 6
ROWS = 8
COLS = 16
CELLS = 32
LANES = 128
HALF = NF // 2
EXTRA = 3 * HALF
IDS = EXTRA + SLOTS
DOSES = IDS + 4
PACKET = EXTRA + 16
WINDOW = 4 * 6
REST = WINDOW * HALF // 2
WINDOW_DOSES = REST + WINDOW
OUTGOING = REST + 32
BF16 = jnp.bfloat16
F32 = jnp.float32


def split(table):
    high = table.astype(ml_dtypes.bfloat16)
    low = (table - high.astype(np.float64)).astype(ml_dtypes.bfloat16)
    return high, low


@functools.lru_cache(maxsize=None)
def tables():
    freq = np.arange(NF) - NF // 2
    pixels = np.arange(TILE)
    points = np.arange(Q)
    turn = np.mod(freq[:, None] * pixels[None, :], TILE) * (2.0 * np.pi / TILE)
    forward = np.concatenate([np.cos(turn), np.sin(turn)]) / TILE
    high, low = split(forward)
    forward_rows = np.concatenate([high, low])
    forward_cols = np.ascontiguousarray(forward_rows.T)

    turn = np.mod(points[:, None] * freq[None, :], Q) * (2.0 * np.pi / Q)
    cos, sin = np.cos(turn), np.sin(turn)
    inverse_left = np.concatenate([cos, -sin], axis=1)
    edges = np.concatenate([np.arange(TILE - REACH, TILE), np.arange(REACH)])
    turn = np.mod(edges[:, None] * freq[None, :], TILE) * (2.0 * np.pi / TILE)
    edge_left = np.concatenate([np.cos(turn), -np.sin(turn)], axis=1)
    right = np.zeros((LANES, 2 * LANES))
    for k in range(2):
        re = slice(2 * k * NF, (2 * k + 1) * NF)
        im = slice((2 * k + 1) * NF, (2 * k + 2) * NF)
        out_re = slice(k * LANES, k * LANES + Q)
        out_im = slice(k * LANES + Q, (k + 1) * LANES)
        right[re, out_re], right[re, out_im] = cos.T, sin.T
        right[im, out_re], right[im, out_im] = -sin.T, cos.T

    spread_up = np.zeros((LANES, 4 * LANES))
    spread_low = np.zeros((LANES, 4 * LANES))
    rest = np.zeros((LANES, 2 * LANES))
    for copy in range(4):
        for part in range(2):
            for b in range(NF):
                for tile in range(2):
                    lane = tile * Q + part * NF + b
                    base = tile * 2 * LANES + part * LANES + copy * NF
                    spread_up[lane, base + b] = 1.0
                    if b:
                        spread_low[lane, base + NF - b] = -1.0 if part else 1.0
                rest[part * NF + b, part * LANES + copy * NF + b] = 1.0
            for i in range(1, HALF):
                rest[Q + part * (HALF - 1) + i - 1, part * LANES + copy * NF] = 1.0
        rest[Q + 2 * (HALF - 1), copy * NF + HALF] = 1.0
    rest_mask = np.zeros((HALF, LANES), np.float32)
    rest_mask[0, :Q] = rest_mask[0, Q + 2 * (HALF - 1)] = 1.0
    turned = np.zeros((REST, REST))
    for i in range(1, HALF):
        rest_mask[i, Q + i - 1] = rest_mask[i, Q + HALF - 1 + i - 1] = 1.0
        for pair in range(WINDOW // 2):
            turned[pair * HALF + i, pair * HALF + HALF - i] = 1.0

    harmonic = np.arange(Q) - Q // 2
    fine = np.mod(pixels[:, None] * harmonic[None, :], TILE) * (2.0 * np.pi / TILE)
    grid = np.mod(points[:, None] * harmonic[None, :], Q) * (2.0 * np.pi / Q)
    interp = (np.cos(fine) @ np.cos(grid).T + np.sin(fine) @ np.sin(grid).T) / Q
    interp = interp.astype(ml_dtypes.bfloat16).astype(np.float64)

    offsets = np.arange(2 * REACH + 1) - REACH
    taps = np.exp(-offsets * offsets / 32.0)
    taps = taps / taps.sum()

    def blur(out_pixels, in_pixels):
        gap = out_pixels[:, None] - in_pixels[None, :]
        inside = np.abs(gap) <= REACH
        return np.where(inside, taps[np.clip(gap + REACH, 0, 2 * REACH)], 0.0)

    reach_cols = np.concatenate(
        [np.arange(TILE), np.arange(-LANES, 0), np.arange(TILE, TILE + LANES)]
    )
    spread = (blur(reach_cols, pixels) @ interp).T
    across = np.zeros((LANES, 5 * LANES))
    across[:Q] = spread

    out_rows = np.arange(2 * TILE)
    down = np.concatenate(
        [
            blur(out_rows, pixels) @ interp,
            blur(out_rows, pixels + TILE) @ interp,
            blur(out_rows, np.arange(-REACH, 0)),
            blur(out_rows, np.arange(2 * TILE, 2 * TILE + REACH)),
        ],
        axis=1,
    )
    bf16 = dict(
        forward_rows=forward_rows,
        forward_cols=forward_cols,
        inverse_left=inverse_left,
        edge_left=edge_left,
        inverse_right=right,
        spread_up=spread_up,
        spread_low=spread_low,
        rest=rest,
        turned=turned,
        across=across,
        down=4.0 * down,
    )
    out = {name: value.astype(ml_dtypes.bfloat16) for name, value in bf16.items()}
    out["rest_mask"] = rest_mask
    return out


def dot(a, b):
    return jnp.dot(a, b, preferred_element_type=F32)


def halves(x):
    high = x.astype(BF16)
    return high, (x - high.astype(F32)).astype(BF16)


def lanes_of(shape):
    return lax.broadcasted_iota(jnp.int32, shape, 1)


def spectra_kernel(
    mask, kernels, weights, ids, dose, fwd_cols, fwd_rows,
    out, ker,
    mask_v, kernels_v, weights_s, ids_v, dose_v, cols_v, rows_v, extra, sems,
):
    moves = [(fwd_cols, cols_v)]
    moves += [(mask.at[s], mask_v.at[s]) for s in range(SLOTS)]
    moves += [(kernels, kernels_v), (weights, weights_s), (fwd_rows, rows_v)]
    moves += [(ids, ids_v), (dose, dose_v)]
    copies = [
        pltpu.make_async_copy(src, dst, sems.at[i]) for i, (src, dst) in enumerate(moves)
    ]
    for copy in copies:
        copy.start()
    for copy in copies[:4]:
        copy.wait()

    left = lanes_of((TILE, LANES)) < Q
    pairs = []
    for slot in range(SLOTS):
        if slot == 3:
            for copy in copies[4:]:
                copy.wait()
            for two in range(NK // 2):
                re, im = [], []
                for k in (2 * two, 2 * two + 1):
                    scale = jnp.sqrt(jnp.full((NF, NF), weights_s[k], F32))
                    re.append(kernels_v[0, k] * scale)
                    im.append(kernels_v[1, k] * scale)
                ker[0, two] = jnp.concatenate([re[0], im[0], re[1], im[1]], axis=1)
                ker[1, two] = jnp.concatenate([-im[0], re[0], -im[1], re[1]], axis=1)
        cols = dot(mask_v[slot], cols_v[...])
        cols = cols + pltpu.roll(cols, Q, 1)
        high = cols.astype(BF16).astype(F32)
        pairs.append(jnp.where(left, high, cols - high).astype(BF16))

    lane = lanes_of((NF, LANES))
    line = lax.broadcasted_iota(jnp.int32, (NF, LANES), 0)
    even = (lane // NF) % 2 == 0
    in_re = lane == line + Q - HALF - 1
    in_im = lane == line + Q - HALF - 1 + HALF - 1
    column = line > HALF
    lane1 = lanes_of((1, LANES))
    blocks, rows = [], []
    for slot in range(SLOTS):
        both = dot(rows_v[...], pairs[slot])
        both = both[:Q] + both[Q:]
        both = both + pltpu.roll(both, Q, 1)
        top, bottom = both[:NF], both[NF:]
        real = top - pltpu.roll(bottom, NF, 1)
        imag = -(bottom + pltpu.roll(top, NF, 1))
        blocks.append(jnp.where(even, real, pltpu.roll(imag, NF, 1)))
        first = jnp.where(column & in_re, jnp.broadcast_to(real[:, 0:1], (NF, LANES)), 0.0)
        second = jnp.where(column & in_im, jnp.broadcast_to(imag[:, 0:1], (NF, LANES)), 0.0)
        turned = jnp.sum(first + second, axis=0, keepdims=True)
        mean = real[HALF : HALF + 1, HALF : HALF + 1]
        mean = jnp.broadcast_to(mean - mean.astype(BF16).astype(F32), (1, LANES))
        turned = jnp.where(lane1 == Q + 2 * (HALF - 1), mean, turned)
        rows.append(jnp.where(lane1 < Q, blocks[slot][HALF : HALF + 1], turned))
    half = lanes_of((HALF, LANES)) < Q
    packed = [
        jnp.where(half, blocks[2 * i][:HALF], blocks[2 * i + 1][:HALF]).astype(BF16)
        for i in range(SLOTS // 2)
    ]
    extra[...] = jnp.zeros_like(extra)
    for slot in range(SLOTS):
        extra[slot : slot + 1, :] = rows[slot]
    extra[IDS - EXTRA : IDS - EXTRA + 4, 0:16] = ids_v[...].astype(F32)
    at = slice(DOSES - EXTRA, DOSES - EXTRA + 2)
    high = dose_v[...].astype(BF16).astype(F32)
    middle = (dose_v[...] - high).astype(BF16).astype(F32)
    extra[at, 4:8] = high
    extra[at, 8:12] = middle
    extra[at, 12:16] = dose_v[...] - high - middle
    packed.append(extra[...].astype(BF16))
    for c in range(COLS):
        for i in range(4):
            out[c, i * HALF : (i + 1) * HALF, :] = packed[i]


def routing_kernel(packets, counts, out, held, rests, buffer, where_v, where_s, sem):
    row, col = lax.axis_index("rows"), lax.axis_index("cols")
    for c in range(COLS):
        rests[c * 16 : (c + 1) * 16, :] = packets[c, EXTRA : EXTRA + 16, :].astype(F32)

    def rest_of(c):
        return rests[pl.ds(pl.multiple_of(c * 16, 16), 16), :]

    before = rest_of(jnp.maximum(col - 1, 0))
    here = rest_of(col)
    after = rest_of(jnp.minimum(col + 1, COLS - 1))
    line = lax.broadcasted_iota(jnp.int32, (16, LANES), 0)
    first = IDS - EXTRA
    window = jnp.where(
        line == 0,
        pltpu.roll(before, 16 - first - 3, 0),
        jnp.where(line < 5, pltpu.roll(here, 16 - first + 1, 0), pltpu.roll(after, 16 - first + 5, 0)),
    ).astype(jnp.int32)
    cell = window - row * CELLS
    exists = ((line > 0) | (col > 0)) & ((line < 5) | (col < COLS - 1)) & (line < 6)
    mine = (cell >= 0) & (cell < CELLS) & exists
    where_v[...] = jnp.where(mine, cell, CELLS)
    copy = pltpu.make_async_copy(where_v, where_s, sem)
    copy.start()

    left = lanes_of((HALF, LANES)) < Q
    start = jnp.int32(0)
    for c in range(COLS):
        count = counts[row, c]
        for s in range(SLOTS):
            pair = packets[c, (s // 2) * HALF : (s // 2 + 1) * HALF, :].astype(F32)
            moved = pltpu.roll(pair, Q, 1)
            both = jnp.where(left, moved, pair) if s % 2 else jnp.where(left, pair, moved)
            held[start + s] = both
            buffer[pl.ds(start + s, 1), :] = rests[c * 16 + s : c * 16 + s + 1, :]
        start = start + count
    held[CELLS] = jnp.zeros((HALF, LANES), F32)
    buffer[CELLS : CELLS + 1, :] = jnp.zeros((1, LANES), F32)

    lane = lanes_of((2, LANES))
    at = slice(DOSES - EXTRA, DOSES - EXTRA + 2)
    doses = jnp.where(
        lane < 16,
        before[at],
        jnp.where(lane < 32, pltpu.roll(here[at], 16, 1), pltpu.roll(after[at], 32, 1)),
    )
    tail = jnp.concatenate([doses, jnp.zeros((6, LANES), F32)], axis=0)
    copy.wait()
    for dest in range(ROWS):
        rows = []
        for i in range(4):
            tile_row = 2 * dest - 1 + i
            if not 0 <= tile_row < 2 * ROWS:
                for pair in range(3):
                    at = (3 * i + pair) * HALF
                    out[dest, at : at + HALF, :] = jnp.zeros((HALF, LANES), BF16)
                rows += [jnp.zeros((1, LANES), F32)] * 6
                continue
            for pair in range(3):
                one, two = where_s[2 * pair, tile_row], where_s[2 * pair + 1, tile_row]
                at = (3 * i + pair) * HALF
                out[dest, at : at + HALF, :] = jnp.where(left, held[one], held[two]).astype(BF16)
                rows += [buffer[pl.ds(one, 1), :], buffer[pl.ds(two, 1), :]]
        rest = jnp.concatenate(rows + [tail], axis=0).astype(BF16)
        out[dest, REST : REST + 32, :] = rest


def develop_kernel(
    tiles, ker, threshold, turned, spread_up, spread_low, rest, rest_mask,
    inv_left, edge_left, inv_right, across, down,
    out,
    narrow, stage, sems,
):
    row = lax.axis_index("rows")
    window = tiles[0].astype(F32)
    for source in range(1, ROWS):
        window = window + tiles[source].astype(F32)
    held = window[:REST].astype(BF16)
    upper = dot(held, spread_up[...])
    lower = dot(dot(turned[...], held).astype(BF16), spread_low[...])
    rests = [
        jnp.broadcast_to(window[REST + t : REST + t + 1], (HALF, LANES)) * rest_mask[...]
        for t in range(WINDOW)
    ]
    rests = dot(jnp.concatenate(rests, axis=0).astype(BF16), rest[...])

    def doses(source):
        info = tiles[source, REST + 16 : REST + 32, :].astype(F32)[8:]
        return info + pltpu.roll(info, LANES - 4, 1) + pltpu.roll(info, LANES - 8, 1)

    own = doses(row)
    above = doses(jnp.maximum(row - 1, 0))
    below = doses(jnp.minimum(row + 1, ROWS - 1))

    images = []
    for i in range(4):
        whole_tile = i in (1, 2)
        halfway = []
        for j in range(6):
            m, t = 3 * i + j // 2, 6 * i + j
            a, r = slice(m * HALF, (m + 1) * HALF), slice(t * HALF, (t + 1) * HALF)
            re = slice((j % 2) * 2 * LANES, (j % 2) * 2 * LANES + LANES)
            im = slice(re.stop, re.stop + LANES)
            real = jnp.concatenate([upper[a, re], lower[a, re] + rests[r, :LANES]], axis=0)
            imag = jnp.concatenate([upper[a, im], lower[a, im] + rests[r, LANES:]], axis=0)
            prods = []
            for two in range(NK // 2):
                ka, kb = ker[0, two], ker[1, two]
                prod = jnp.concatenate([ka * real + kb * imag, ka * imag - kb * real], axis=0)
                prods.append(prod.astype(BF16))
            prod = jnp.concatenate(prods, axis=1)
            table = inv_left[...] if whole_tile else edge_left[...]
            half = dot(table, prod)
            if not whole_tile:
                half = half[:REACH] if i == 0 else half[REACH:]
            halfway.append(
                jnp.concatenate(
                    [half[:, n * LANES : (n + 1) * LANES] for n in range(NK // 2)], axis=0
                ).astype(BF16)
            )
        line = []
        for j in range(6):
            field = dot(halfway[j], inv_right[...])
            power = field * field
            power = power[:, :LANES] + power[:, LANES:]
            height = power.shape[0] // (NK // 2)
            total = power[:height]
            for n in range(1, NK // 2):
                total = total + power[n * height : (n + 1) * height]
            line.append(total + pltpu.roll(total, Q, 1))
        images.append(line)

    lane_of = [7] + [20 + j for j in range(4)] + [36]
    values = []
    for j in range(6):
        rows = [images[1][j], images[2][j], images[0][j], images[3][j]]
        block = jnp.concatenate(rows, axis=0).astype(BF16)
        cols = slice(0, 5 * LANES)
        if j == 0:
            cols = slice(4 * LANES, 5 * LANES)
        if j == 5:
            cols = slice(3 * LANES, 4 * LANES)
        value = dot(block, across[:, cols])
        at = slice(lane_of[j], lane_of[j] + 1)
        scales = [own[0:1, at], own[1:2, at], above[1:2, at], below[0:1, at]]
        heights = [Q, Q, REACH, REACH]
        scale = jnp.concatenate(
            [jnp.broadcast_to(s, (h, LANES)) for s, h in zip(scales, heights)], axis=0
        )
        values.append([value[:, n : n + LANES] * scale for n in range(0, value.shape[1], LANES)])
    for j in range(1, 5):
        parts = values[j][:3]
        before = values[j - 1][-1]
        after = values[j + 1][3] if j < 4 else values[j + 1][0]
        parts = [parts[0] + before, parts[1], parts[2] + after]
        for n in range(3):
            at = (j - 1) * TILE + n * LANES
            narrow[:, at : at + LANES] = parts[n].astype(BF16)

    shift = 4.0 * threshold[0]
    chunk = 2 * TILE // 4
    copies = []
    for n in range(4):
        rows = pl.ds(n * chunk, chunk)
        level = dot(down[rows, :], narrow[...])
        stage[rows, :] = (0.5 * jnp.tanh(level - shift) + 0.5).astype(BF16)
        copy = pltpu.make_async_copy(stage.at[rows, :], out.at[rows, :], sems.at[n])
        copy.start()
        copies.append(copy)
    for copy in copies:
        copy.wait()


PARAMS = pltpu.CompilerParams(vmem_limit_bytes=48 * 1024 * 1024)
IN_HBM = pl.BlockSpec(memory_space=pltpu.HBM)
IN_VMEM = pl.BlockSpec(memory_space=pltpu.VMEM)
IN_SMEM = pl.BlockSpec(memory_space=pltpu.SMEM)


def image(masks, cell_ids, kernels, kernel_weights, dose):
    table = tables()
    operands = [masks, kernels, kernel_weights, cell_ids.T, dose]
    operands += [jnp.asarray(table[n]) for n in ("forward_cols", "forward_rows")]
    in_hbm = [pltpu.with_memory_space_constraint(op, pltpu.HBM) for op in operands]
    ker = (2, NK // 2, NF, LANES)
    return pl.pallas_call(
        spectra_kernel,
        out_shape=(
            jax.ShapeDtypeStruct((COLS, PACKET, LANES), BF16),
            jax.ShapeDtypeStruct(ker, F32),
        ),
        in_specs=[IN_HBM] * len(operands),
        out_specs=(IN_VMEM, IN_VMEM),
        scratch_shapes=[
            *[
                (pltpu.SMEM if op is kernel_weights else pltpu.VMEM)(op.shape, op.dtype)
                for op in operands
            ],
            pltpu.VMEM((16, LANES), F32),
            pltpu.SemaphoreType.DMA((len(operands) + SLOTS - 1,)),
        ],
        compiler_params=PARAMS,
    )(*in_hbm)


def route(packets, owned_counts):
    return pl.pallas_call(
        routing_kernel,
        out_shape=jax.ShapeDtypeStruct((ROWS, OUTGOING, LANES), BF16),
        in_specs=[IN_VMEM, IN_SMEM],
        out_specs=IN_VMEM,
        scratch_shapes=[
            pltpu.VMEM((CELLS + SLOTS, HALF, LANES), F32),
            pltpu.VMEM((COLS * 16, LANES), F32),
            pltpu.VMEM((CELLS + 8, LANES), F32),
            pltpu.VMEM((16, LANES), jnp.int32),
            pltpu.SMEM((16, LANES), jnp.int32),
            pltpu.SemaphoreType.DMA,
        ],
        compiler_params=PARAMS,
    )(packets, owned_counts)


def develop(incoming, ker, threshold):
    table = tables()
    names = ("turned", "spread_up", "spread_low", "rest", "rest_mask")
    names += ("inverse_left", "edge_left", "inverse_right", "across", "down")
    constants = [jnp.asarray(table[n]) for n in names]
    return pl.pallas_call(
        develop_kernel,
        out_shape=jax.ShapeDtypeStruct((2 * TILE, 4 * TILE), BF16),
        in_specs=[IN_VMEM, IN_VMEM, IN_SMEM, *[IN_VMEM] * len(constants)],
        out_specs=IN_HBM,
        scratch_shapes=[
            pltpu.VMEM((2 * Q + 2 * REACH, 4 * TILE), BF16),
            pltpu.VMEM((2 * TILE, 4 * TILE), BF16),
            pltpu.SemaphoreType.DMA((4,)),
        ],
        compiler_params=PARAMS,
    )(incoming, ker, threshold, *constants)


def local(masks, owned_counts, cell_ids, kernels, kernel_weights, dose, threshold):
    packet, ker = image(masks, cell_ids, kernels, kernel_weights, dose)
    packets = lax.all_to_all(packet, "cols", split_axis=0, concat_axis=0, tiled=True)
    outgoing = route(packets, owned_counts)
    incoming = lax.all_to_all(outgoing, "rows", split_axis=0, concat_axis=0, tiled=True)
    return develop(incoming, ker, threshold)


def solution(mesh):
    return jax.shard_map(
        local,
        mesh=mesh,
        in_specs=(
            P(("rows", "cols"), None, None),
            P(),
            P(None, "cols"),
            P(),
            P(),
            P("rows", "cols"),
            P(),
        ),
        out_specs=P("rows", "cols"),
        check_vma=False,
    )
```

time: 51.2 us -> 41 us (0.80)
  blocking collectives: 22.4 us -> 15.9 us
  Pallas kernels: 15.4 us -> 9.56 us
  waiting for transfers between devices: 6.16 us -> 8.13 us
    all_to_all x1, blocking collectives: 22.4 us -> 15.9 us  [local(): lax.all_to_all(packet, 'cols', split_axis=0, concat_axis=0, tiled=True)]
    pallas_call x3, Pallas kernels: 15.4 us -> 9.56 us  [the longest x1 4.34 us: develop(): pl.pallas_call(develop_kernel, out_shape=jax.ShapeDtypeStruct((2 * TILE,...]
    all_to_all x1, waiting for transfers between devices: 6.16 us -> 8.13 us  [local(): lax.all_to_all(outgoing, 'rows', split_axis=0, concat_axis=0, tiled=True)]
where the time goes in v2:
time: 41 us; the launch traced here: 40.7 us
  blocking collectives  15.9 us (39%)
  Pallas kernels  9.56 us (23%)
  waiting for transfers between devices  8.13 us (20%)
  starting transfers between devices  6.32 us (15%)
  between operations  0.8 us (2%)
    all_to_all x1, blocking collectives, local(): lax.all_to_all(packet, 'cols', split_axis=0, concat_axis=0, tiled=True)  15.9 us
    all_to_all x1, waiting for transfers between devices, local(): lax.all_to_all(outgoing, 'rows', split_axis=0, concat_axis=0, tiled=True)  8.13 us
    all_to_all x1, starting transfers between devices, local(): lax.all_to_all(outgoing, 'rows', split_axis=0, concat_axis=0, tiled=True)  6.32 us
    pallas_call x1, Pallas kernels, develop(): pl.pallas_call(develop_kernel, out_shape=jax.ShapeDtypeStruct((2 * TILE,...  4.34 us
    pallas_call x1, Pallas kernels, image(): pl.pallas_call(spectra_kernel, out_shape=(jax.ShapeDtypeStruct((COLS, PAC...  2.86 us
    pallas_call x1, Pallas kernels, route(): pl.pallas_call(routing_kernel, out_shape=jax.ShapeDtypeStruct((ROWS, OUTG...  2.36 us
  transfers between devices with their start and end apart: 1, of which 1 were waited for; matrix products, arithmetic and copies ran while one was open for 0% of the time, Pallas kernels for 0%

profile of v2, /device:TPU:1, one launch (start us, length us, event | category | flops | bytes accessed | tf_op | source)
XLA Modules:
  0.0 40.7 jit_solution(14825526518925864760)
XLA Ops:
  0.0 0.0 copy-start.10
  0.0 0.0 copy-start.7
  0.0 0.0 copy-start.8
  0.0 0.0 copy-start.6
  0.1 0.0 copy-start.2
  0.1 0.0 copy-start.3
  0.1 0.0 copy-start.4
  0.1 0.0 copy-start.9
  0.1 2.9 %shard_map.181 = (bf16[16,64,128]{2,1,0:T(8,128)(2,1)S(1)}, f32[2,8,32,128]{3,2,1,0:T(8,128)S(1)}) custom-call(bf16[6,384,384]{2,1,0:T(8,128)(2,1)} %mask.1, f32[2,16,32,32]{3,2,1,0:T(8,128)} %kernels.1, f32[16]{0:T(128)} %weights.1, s32[4,16]{1,0:T(4,128)} %bitcast.1, f32[2,4]{1,0:T(2,128)} %dose.1, bf16[384,128]{1,0:T(8,128)(2,1)} %constant.24.clone.fwd_cols, ...), custom_call_target="tpu_custom_call" | custom-call | tf_op jit(solution)/shard_map/pallas_call | solution.py:419
  3.0 15.9 %all_to_all.10.packets = bf16[16,64,128]{2,1,0:T(8,128)(2,1)S(1)} all-to-all(bf16[16,64,128]{2,1,0:T(8,128)(2,1)S(1)} %get-tuple-element.7), channel_id=1, replica_groups=mesh['rows'=8,'cols'=16] {'cols'}, dimensions={0} | all-to-all | bytes 524288 | tf_op jit(solution)/shard_map/all_to_all | solution.py:478
  18.8 0.0 copy-done.9
  18.8 2.4 %shard_map.182 = bf16[8,224,128]{2,1,0:T(8,128)(2,1)} custom-call(bf16[16,64,128]{2,1,0:T(8,128)(2,1)S(1)} %all_to_all.10.packets, s32[8,16]{1,0:T(8,128)S(1)} %copy-done.9), custom_call_target="tpu_custom_call" | custom-call | tf_op jit(solution)/shard_map/pallas_call | solution.py:440
  21.2 6.3 %all-to-all-start.1 = ((bf16[8,224,128]{2,1,0:T(8,128)(2,1)}), bf16[8,224,128]{2,1,0:T(8,128)(2,1)S(1)}, u32[]{:S(2)}, u32[]{:S(2)}) async-start(bf16[8,224,128]{2,1,0:T(8,128)(2,1)} %shard_map.182), calls=%async_computation.1 | async-start | bytes 917504 | tf_op jit(solution)/shard_map/all_to_all | solution.py:480
  28.2 8.1 %all-to-all-done.1.tiles = bf16[8,224,128]{2,1,0:T(8,128)(2,1)S(1)} async-done(((bf16[8,224,128]{2,1,0:T(8,128)(2,1)}), bf16[8,224,128]{2,1,0:T(8,128)(2,1)S(1)}, u32[]{:S(2)}, u32[]{:S(2)}) %all-to-all-start.1) | async-done | bytes 458784 | tf_op jit(solution)/shard_map/all_to_all | solution.py:480
  36.3 0.0 copy-done
  36.3 0.0 copy-done.1
  36.3 0.0 copy-done.5
  36.3 0.0 copy-done.10
  36.3 0.0 copy-done.7
  36.3 0.0 copy-done.8
  36.3 0.0 copy-done.6
  36.4 0.0 copy-done.2
  36.4 0.0 copy-done.3
  36.4 4.3 %shard_map.183 = bf16[768,1536]{1,0:T(8,128)(2,1)} custom-call(bf16[8,224,128]{2,1,0:T(8,128)(2,1)S(1)} %all-to-all-done.1.tiles, f32[2,8,32,128]{3,2,1,0:T(8,128)S(1)} %get-tuple-element.8.ker, f32[1]{0:T(128)S(6)} %copy.20.threshold, bf16[192,192]{1,0:T(8,128)(2,1)S(1)} %copy-done.4, bf16[128,512]{1,0:T(8,128)(2,1)S(1)} %copy-done.3, ...), custom_call_target="tpu_custom_call" | custom-call | tf_op jit(solution)/shard_map/pallas_call | solution.py:462
  (4 shorter events, 0.0 us)
Async XLA Ops:
  0.0 36.3 %copy-start = (bf16[768,144]{1,0:T(8,128)(2,1)S(1)}, bf16[768,144]{1,0:T(8,128)(2,1)}, u32[]{:S(2)}) copy-start(bf16[768,144]{1,0:T(8,128)(2,1)} %constant.35.clone.down) | copy-start | bytes 663556
  0.0 36.3 %copy-start.1 = (bf16[128,640]{1,0:T(8,128)(2,1)S(1)}, bf16[128,640]{1,0:T(8,128)(2,1)}, u32[]{:S(2)}) copy-start(bf16[128,640]{1,0:T(8,128)(2,1)} %constant.34.clone.across) | copy-start | bytes 491524
  0.0 36.3 %copy-start.5 = (bf16[128,256]{1,0:T(8,128)(2,1)S(1)}, bf16[128,256]{1,0:T(8,128)(2,1)}, u32[]{:S(2)}) copy-start(bf16[128,256]{1,0:T(8,128)(2,1)} %constant.33.clone.inv_right) | copy-start | bytes 196612
  0.0 36.3 %copy-start.10 = (bf16[16,64]{1,0:T(8,128)(2,1)S(1)}, bf16[16,64]{1,0:T(8,128)(2,1)}, u32[]{:S(2)}) copy-start(bf16[16,64]{1,0:T(8,128)(2,1)} %constant.32.clone.edge_left) | copy-start | bytes 6148
  0.0 36.3 %copy-start.7 = (bf16[64,64]{1,0:T(8,128)(2,1)S(1)}, bf16[64,64]{1,0:T(8,128)(2,1)}, u32[]{:S(2)}) copy-start(bf16[64,64]{1,0:T(8,128)(2,1)} %constant.31.clone.inv_left) | copy-start | bytes 24580
  0.0 36.3 %copy-start.8 = (f32[16,128]{1,0:T(8,128)S(1)}, f32[16,128]{1,0:T(8,128)}, u32[]{:S(2)}) copy-start(f32[16,128]{1,0:T(8,128)} %constant.30.clone.rest_mask) | copy-start | bytes 24580
  0.0 36.3 %copy-start.6 = (bf16[128,256]{1,0:T(8,128)(2,1)S(1)}, bf16[128,256]{1,0:T(8,128)(2,1)}, u32[]{:S(2)}) copy-start(bf16[128,256]{1,0:T(8,128)(2,1)} %constant.29.clone.rest) | copy-start | bytes 196612
  0.1 36.3 %copy-start.2 = (bf16[128,512]{1,0:T(8,128)(2,1)S(1)}, bf16[128,512]{1,0:T(8,128)(2,1)}, u32[]{:S(2)}) copy-start(bf16[128,512]{1,0:T(8,128)(2,1)} %constant.28.clone.spread_low) | copy-start | bytes 393220
  0.1 36.3 %copy-start.3 = (bf16[128,512]{1,0:T(8,128)(2,1)S(1)}, bf16[128,512]{1,0:T(8,128)(2,1)}, u32[]{:S(2)}) copy-start(bf16[128,512]{1,0:T(8,128)(2,1)} %constant.27.clone.spread_up) | copy-start | bytes 393220
  0.1 36.3 %copy-start.4 = (bf16[192,192]{1,0:T(8,128)(2,1)S(1)}, bf16[192,192]{1,0:T(8,128)(2,1)}, u32[]{:S(2)}) copy-start(bf16[192,192]{1,0:T(8,128)(2,1)} %constant.26.clone.turned) | copy-start | bytes 221188
  0.1 18.7 %copy-start.9 = (s32[8,16]{1,0:T(8,128)S(1)}, s32[8,16]{1,0:T(8,128)}, u32[]{:S(2)}) copy-start(s32[8,16]{1,0:T(8,128)} %counts.1) | copy-start | bytes 1540
  21.2 15.1 %all-to-all-start.1 = ((bf16[8,224,128]{2,1,0:T(8,128)(2,1)}), bf16[8,224,128]{2,1,0:T(8,128)(2,1)S(1)}, u32[]{:S(2)}, u32[]{:S(2)}) async-start(bf16[8,224,128]{2,1,0:T(8,128)(2,1)} %shard_map.182), calls=%async_computation.1 | async-start | bytes 917504 | tf_op jit(solution)/shard_map/all_to_all | solution.py:480

commit v3 on v2

v3 whole, which is shorter than its diff:
```python
import functools

import jax
import jax.numpy as jnp
import ml_dtypes
import numpy as np
from jax import lax
from jax.experimental import pallas as pl
from jax.experimental.pallas import tpu as pltpu
from jax.sharding import PartitionSpec as P

REACH = 8
TILE = 384
NF = 32
NK = 16
Q = 64
SLOTS = 6
ROWS = 8
COLS = 16
CELLS = 32
LANES = 128
HALF = NF // 2
EXTRA = 3 * HALF
IDS = EXTRA + SLOTS
DOSES = IDS + 4
PACKET = EXTRA + 16
WINDOW = 4 * 6
MOST = 14
REST = MOST * HALF // 2
OUTGOING = REST + 16
STACK = Q + 2 * REACH
SPLIT = TILE - 2 * REACH
BF16 = jnp.bfloat16
F32 = jnp.float32


def split(table):
    high = table.astype(ml_dtypes.bfloat16)
    low = (table - high.astype(np.float64)).astype(ml_dtypes.bfloat16)
    return high, low


@functools.lru_cache(maxsize=None)
def tables():
    freq = np.arange(NF) - NF // 2
    pixels = np.arange(TILE)
    points = np.arange(Q)
    turn = np.mod(freq[:, None] * pixels[None, :], TILE) * (2.0 * np.pi / TILE)
    forward = np.concatenate([np.cos(turn), np.sin(turn)]) / TILE
    high, low = split(forward)
    forward_rows = np.concatenate([high, low])
    forward_cols = np.ascontiguousarray(forward_rows.T)

    turn = np.mod(points[:, None] * freq[None, :], Q) * (2.0 * np.pi / Q)
    cos, sin = np.cos(turn), np.sin(turn)
    inverse_left = np.concatenate([cos, -sin], axis=1)
    edges = np.concatenate([np.arange(TILE - REACH, TILE), np.arange(REACH)])
    turn = np.mod(edges[:, None] * freq[None, :], TILE) * (2.0 * np.pi / TILE)
    edge_left = np.concatenate([np.cos(turn), -np.sin(turn)], axis=1)
    right = np.zeros((LANES, 2 * LANES))
    for k in range(2):
        re = slice(2 * k * NF, (2 * k + 1) * NF)
        im = slice((2 * k + 1) * NF, (2 * k + 2) * NF)
        out_re = slice(k * LANES, k * LANES + Q)
        out_im = slice(k * LANES + Q, (k + 1) * LANES)
        right[re, out_re], right[re, out_im] = cos.T, sin.T
        right[im, out_re], right[im, out_im] = -sin.T, cos.T

    spread_up = np.zeros((LANES, 4 * LANES))
    spread_low = np.zeros((LANES, 4 * LANES))
    rest = np.zeros((LANES, 2 * LANES))
    for copy in range(4):
        for part in range(2):
            for b in range(NF):
                for tile in range(2):
                    lane = tile * Q + part * NF + b
                    base = tile * 2 * LANES + part * LANES + copy * NF
                    spread_up[lane, base + b] = 1.0
                    if b:
                        spread_low[lane, base + NF - b] = -1.0 if part else 1.0
                rest[part * NF + b, part * LANES + copy * NF + b] = 1.0
            for i in range(1, HALF):
                rest[Q + part * (HALF - 1) + i - 1, part * LANES + copy * NF] = 1.0
        rest[Q + 2 * (HALF - 1), copy * NF + HALF] = 1.0
    rest_mask = np.zeros((HALF, LANES), np.float32)
    rest_mask[0, :Q] = rest_mask[0, Q + 2 * (HALF - 1)] = 1.0
    turned = np.zeros((WINDOW * HALF // 2, WINDOW * HALF // 2))
    for i in range(1, HALF):
        rest_mask[i, Q + i - 1] = rest_mask[i, Q + HALF - 1 + i - 1] = 1.0
        for pair in range(WINDOW // 2):
            turned[pair * HALF + i, pair * HALF + HALF - i] = 1.0

    harmonic = np.arange(Q) - Q // 2
    fine = np.mod(pixels[:, None] * harmonic[None, :], TILE) * (2.0 * np.pi / TILE)
    grid = np.mod(points[:, None] * harmonic[None, :], Q) * (2.0 * np.pi / Q)
    interp = (np.cos(fine) @ np.cos(grid).T + np.sin(fine) @ np.sin(grid).T) / Q
    interp = interp.astype(ml_dtypes.bfloat16).astype(np.float64)

    offsets = np.arange(2 * REACH + 1) - REACH
    taps = np.exp(-offsets * offsets / 32.0)
    taps = taps / taps.sum()

    def blur(out_pixels, in_pixels):
        gap = out_pixels[:, None] - in_pixels[None, :]
        inside = np.abs(gap) <= REACH
        return np.where(inside, taps[np.clip(gap + REACH, 0, 2 * REACH)], 0.0)

    across = np.zeros((4 * Q, TILE))
    for n in range(3):
        across[n * Q : (n + 1) * Q] = (blur(pixels, pixels + (n - 1) * TILE) @ interp).T

    out_rows = np.arange(2 * TILE)
    down = np.zeros((2 * TILE, 2 * STACK))
    down[:, :Q] = blur(out_rows, pixels) @ interp
    down[:, Q : Q + REACH] = blur(out_rows, np.arange(-REACH, 0))
    down[:, STACK : STACK + Q] = blur(out_rows, pixels + TILE) @ interp
    down[:, STACK + Q : STACK + Q + REACH] = blur(out_rows, 2 * TILE + np.arange(REACH))
    assert not down[:SPLIT, STACK:].any()

    bf16 = dict(
        forward_rows=forward_rows,
        forward_cols=forward_cols,
        inverse_left=inverse_left,
        edge_left=edge_left,
        inverse_right=right,
        spread_up=spread_up,
        spread_low=spread_low,
        rest=rest,
        turned=turned,
        across=across,
        down_upper=4.0 * down[:SPLIT, :STACK],
        down_lower=4.0 * down[SPLIT:],
    )
    out = {name: value.astype(ml_dtypes.bfloat16) for name, value in bf16.items()}
    out["rest_mask"] = rest_mask
    return out


def dot(a, b):
    return jnp.dot(a, b, preferred_element_type=F32)


def halves(x):
    high = x.astype(BF16)
    return high, (x - high.astype(F32)).astype(BF16)


def lanes_of(shape):
    return lax.broadcasted_iota(jnp.int32, shape, 1)


def spectra_kernel(
    mask, ids, dose, fwd_cols, fwd_rows, kernels, weights, counts,
    out, ker, starts,
    mask_v, ids_v, dose_v, cols_v, rows_v, kernels_v, weights_s, counts_s, extra, sems,
):
    moves = [(fwd_cols, cols_v)]
    moves += [(mask.at[s], mask_v.at[s]) for s in range(SLOTS)]
    moves += [(kernels, kernels_v), (weights, weights_s), (counts, counts_s)]
    moves += [(fwd_rows, rows_v), (ids, ids_v), (dose, dose_v)]
    copies = [
        pltpu.make_async_copy(src, dst, sems.at[i]) for i, (src, dst) in enumerate(moves)
    ]
    for copy in copies:
        copy.start()
    for copy in copies[:4]:
        copy.wait()

    left = lanes_of((TILE, LANES)) < Q
    pairs = []
    for slot in range(SLOTS):
        if slot == 3:
            for copy in copies[4:]:
                copy.wait()
            for two in range(NK // 2):
                re, im = [], []
                for k in (2 * two, 2 * two + 1):
                    scale = jnp.sqrt(jnp.full((NF, NF), weights_s[k], F32))
                    re.append(kernels_v[0, k] * scale)
                    im.append(kernels_v[1, k] * scale)
                ker[0, two] = jnp.concatenate([re[0], im[0], re[1], im[1]], axis=1)
                ker[1, two] = jnp.concatenate([-im[0], re[0], -im[1], re[1]], axis=1)
            start = jnp.int32(0)
            for c in range(COLS):
                starts[c] = start
                start = start + counts_s[lax.axis_index("rows"), c]
        cols = dot(mask_v[slot], cols_v[...])
        cols = cols + pltpu.roll(cols, Q, 1)
        high = cols.astype(BF16).astype(F32)
        pairs.append(jnp.where(left, high, cols - high).astype(BF16))

    lane = lanes_of((NF, LANES))
    line = lax.broadcasted_iota(jnp.int32, (NF, LANES), 0)
    even = (lane // NF) % 2 == 0
    in_re = lane == line + Q - HALF - 1
    in_im = lane == line + Q - HALF - 1 + HALF - 1
    column = line > HALF
    lane1 = lanes_of((1, LANES))
    blocks, rows = [], []
    for slot in range(SLOTS):
        both = dot(rows_v[...], pairs[slot])
        both = both[:Q] + both[Q:]
        both = both + pltpu.roll(both, Q, 1)
        top, bottom = both[:NF], both[NF:]
        real = top - pltpu.roll(bottom, NF, 1)
        imag = -(bottom + pltpu.roll(top, NF, 1))
        blocks.append(jnp.where(even, real, pltpu.roll(imag, NF, 1)))
        first = jnp.where(column & in_re, jnp.broadcast_to(real[:, 0:1], (NF, LANES)), 0.0)
        second = jnp.where(column & in_im, jnp.broadcast_to(imag[:, 0:1], (NF, LANES)), 0.0)
        turned = jnp.sum(first + second, axis=0, keepdims=True)
        mean = real[HALF : HALF + 1, HALF : HALF + 1]
        mean = jnp.broadcast_to(mean - mean.astype(BF16).astype(F32), (1, LANES))
        turned = jnp.where(lane1 == Q + 2 * (HALF - 1), mean, turned)
        rows.append(jnp.where(lane1 < Q, blocks[slot][HALF : HALF + 1], turned))
    half = lanes_of((HALF, LANES)) < Q
    packed = [
        jnp.where(half, blocks[2 * i][:HALF], blocks[2 * i + 1][:HALF]).astype(BF16)
        for i in range(SLOTS // 2)
    ]
    extra[...] = jnp.zeros_like(extra)
    for slot in range(SLOTS):
        extra[slot : slot + 1, :] = rows[slot]
    extra[IDS - EXTRA : IDS - EXTRA + 4, 0:16] = ids_v[...].astype(F32)
    at = slice(DOSES - EXTRA, DOSES - EXTRA + 2)
    high = dose_v[...].astype(BF16).astype(F32)
    middle = (dose_v[...] - high).astype(BF16).astype(F32)
    extra[at, 4:8] = high
    extra[at, 8:12] = middle
    extra[at, 12:16] = dose_v[...] - high - middle
    packed.append(extra[...].astype(BF16))
    for c in range(COLS):
        for i in range(4):
            out[c, i * HALF : (i + 1) * HALF, :] = packed[i]


def routing_kernel(
    packets, starts,
    out, place,
    held, rests, buffer, where_v, where_s, chosen, taken, sem,
):
    row, col = lax.axis_index("rows"), lax.axis_index("cols")
    for c in range(COLS):
        rests[c * 16 : (c + 1) * 16, :] = packets[c, EXTRA : EXTRA + 16, :].astype(F32)

    def rest_of(c):
        return rests[pl.ds(pl.multiple_of(c * 16, 16), 16), :]

    before = rest_of(jnp.maximum(col - 1, 0))
    here = rest_of(col)
    after = rest_of(jnp.minimum(col + 1, COLS - 1))
    line = lax.broadcasted_iota(jnp.int32, (16, LANES), 0)
    first = IDS - EXTRA
    window = jnp.where(
        line == 0,
        pltpu.roll(before, 16 - first - 3, 0),
        jnp.where(line < 5, pltpu.roll(here, 16 - first + 1, 0), pltpu.roll(after, 16 - first + 5, 0)),
    ).astype(jnp.int32)
    exists = ((line > 0) | (col > 0)) & ((line < 5) | (col < COLS - 1)) & (line < 6)
    where_v[...] = jnp.where(exists, window, -1)
    copy = pltpu.make_async_copy(where_v, where_s, sem)
    copy.start()

    left = lanes_of((HALF, LANES)) < Q
    for c in range(COLS):
        start = starts[c]
        for s in range(SLOTS):
            pair = packets[c, (s // 2) * HALF : (s // 2 + 1) * HALF, :].astype(F32)
            moved = pltpu.roll(pair, Q, 1)
            both = jnp.where(left, moved, pair) if s % 2 else jnp.where(left, pair, moved)
            held[start + s] = both
            buffer[pl.ds(start + s, 1), :] = rests[c * 16 + s : c * 16 + s + 1, :]
    held[CELLS] = jnp.zeros((HALF, LANES), F32)
    buffer[CELLS : CELLS + 1, :] = jnp.zeros((1, LANES), F32)

    lane = lanes_of((2, LANES))
    at = slice(DOSES - EXTRA, DOSES - EXTRA + 2)
    doses = jnp.where(
        lane < 16,
        before[at],
        jnp.where(lane < 32, pltpu.roll(here[at], 16, 1), pltpu.roll(after[at], 32, 1)),
    )
    for n in range(ROWS + 1):
        taken[n] = jnp.int32(0)
    copy.wait()

    for i in range(4):
        tile_row = 2 * row - 1 + i
        inside = (tile_row >= 0) & (tile_row < 2 * ROWS)
        for j in range(6):
            cell = where_s[j, jnp.clip(tile_row, 0, 2 * ROWS - 1)]
            cell = jnp.where(inside, cell, -1)
            source = cell >> 5
            rank = taken[source + 1]
            taken[source + 1] = rank + 1
            place[6 * i + j] = jnp.where(cell >= 0, source * 16 + rank, -1)

    for dest in range(ROWS):
        count = jnp.int32(0)
        for i in range(4):
            tile_row = 2 * dest - 1 + i
            if 0 <= tile_row < 2 * ROWS:
                for j in range(6):
                    cell = where_s[j, tile_row]
                    chosen[dest * 16 + count] = cell & (CELLS - 1)
                    count = count + ((cell >> 5) == row).astype(jnp.int32)
        cells = [jnp.where(n < count, chosen[dest * 16 + n], CELLS) for n in range(MOST)]
        for pair in range(MOST // 2):
            one, two = cells[2 * pair], cells[2 * pair + 1]
            at = pair * HALF
            out[dest, at : at + HALF, :] = jnp.where(left, held[one], held[two]).astype(BF16)
        rows = [buffer[pl.ds(cell, 1), :] for cell in cells]
        out[dest, REST : REST + 16, :] = jnp.concatenate(rows + [doses], axis=0).astype(BF16)


def develop_kernel(
    tiles, place, ker, threshold, turned, spread_up, spread_low, rest, rest_mask,
    inv_left, edge_left, inv_right, across, down_upper, down_lower,
    out,
    after_rows, stage, sems,
):
    row = lax.axis_index("rows")
    for source in range(ROWS):
        at = slice(source * 16, (source + 1) * 16)
        after_rows[at, :] = tiles[source, REST : REST + 16, :].astype(F32)
    left = lanes_of((HALF, LANES)) < Q
    held, rests = [], []
    for t in range(0, WINDOW, 2):
        both = []
        for n in (t, t + 1):
            here = jnp.maximum(place[n], 0)
            rank = here & 15
            at = pl.multiple_of((rank >> 1) * HALF, HALF)
            pair = tiles[here >> 4, pl.ds(at, HALF), :].astype(F32)
            tile = jnp.where((rank & 1) == (n & 1), pair, pltpu.roll(pair, Q, 1))
            both.append(jnp.where(place[n] >= 0, tile, 0.0))
            line = jnp.where(place[n] >= 0, after_rows[pl.ds(here, 1), :], 0.0)
            rests.append(jnp.broadcast_to(line, (HALF, LANES)) * rest_mask[...])
        held.append(jnp.where(left, both[0], both[1]).astype(BF16))
    held = jnp.concatenate(held, axis=0)
    upper = dot(held, spread_up[...])
    lower = dot(dot(turned[...], held).astype(BF16), spread_low[...])
    rests = dot(jnp.concatenate(rests, axis=0).astype(BF16), rest[...])

    def doses(source):
        info = after_rows[pl.ds(pl.multiple_of(source * 16, 16), 16), :][MOST:]
        return info + pltpu.roll(info, LANES - 4, 1) + pltpu.roll(info, LANES - 8, 1)

    own = doses(row)
    above = doses(jnp.maximum(row - 1, 0))
    below = doses(jnp.minimum(row + 1, ROWS - 1))

    def picture(i, j):
        whole_tile = i in (1, 2)
        m, t = 3 * i + j // 2, 6 * i + j
        a, r = slice(m * HALF, (m + 1) * HALF), slice(t * HALF, (t + 1) * HALF)
        re = slice((j % 2) * 2 * LANES, (j % 2) * 2 * LANES + LANES)
        im = slice(re.stop, re.stop + LANES)
        real = jnp.concatenate([upper[a, re], lower[a, re] + rests[r, :LANES]], axis=0)
        imag = jnp.concatenate([upper[a, im], lower[a, im] + rests[r, LANES:]], axis=0)
        prods = []
        for two in range(NK // 2):
            ka, kb = ker[0, two], ker[1, two]
            prod = jnp.concatenate([ka * real + kb * imag, ka * imag - kb * real], axis=0)
            prods.append(prod.astype(BF16))
        prod = jnp.concatenate(prods, axis=1)
        half = dot(inv_left[...] if whole_tile else edge_left[...], prod)
        if not whole_tile:
            half = half[:REACH] if i == 0 else half[REACH:]
        return jnp.concatenate(
            [half[:, n * LANES : (n + 1) * LANES] for n in range(NK // 2)], axis=0
        ).astype(BF16)

    def intensity(halfway):
        field = dot(halfway, inv_right[...])
        power = field * field
        power = power[:, :LANES] + power[:, LANES:]
        height = power.shape[0] // (NK // 2)
        total = power[:height]
        for n in range(1, NK // 2):
            total = total + power[n * height : (n + 1) * height]
        return total + pltpu.roll(total, Q, 1)

    lane_of = [7] + [20 + j for j in range(4)] + [36]
    dose_rows = [above[1:2], own[0:1], own[1:2], below[0:1]]
    left = lanes_of((STACK, LANES)) < Q

    images = {}
    for group in ((0, 3), (1,), (2,)):
        halfway = {(i, j): picture(i, j) for i in group for j in range(6)}
        for i in group:
            for j in range(6):
                scale = dose_rows[i][:, lane_of[j] : lane_of[j] + 1]
                images[i, j] = intensity(halfway[i, j]) * scale

    def columns(strip, tile):
        none = jnp.zeros((REACH, LANES), F32)
        stack = [
            jnp.concatenate([images[tile, j], images[strip, j], none], axis=0) for j in range(6)
        ]
        wide = []
        for j in range(1, 5):
            two = jnp.where(left, stack[j - 1], stack[j])
            three = jnp.concatenate([two, stack[j + 1]], axis=1).astype(BF16)
            wide.append(dot(three, across[...]).astype(BF16))
        return jnp.concatenate(wide, axis=1)

    shift = 4.0 * threshold[0]
    copies = []

    def finish(start, stop, level):
        rows = slice(start, stop)
        stage[rows, :] = (0.5 * jnp.tanh(level - shift) + 0.5).astype(BF16)
        copy = pltpu.make_async_copy(stage.at[rows, :], out.at[rows, :], sems.at[len(copies)])
        copy.start()
        copies.append(copy)

    upper_rows = columns(0, 1)
    finish(0, SPLIT, dot(down_upper[...], upper_rows))
    both_rows = jnp.concatenate([upper_rows, columns(3, 2)], axis=0)
    middle = SPLIT + 192
    finish(SPLIT, middle, dot(down_lower[: middle - SPLIT, :], both_rows))
    finish(middle, 2 * TILE, dot(down_lower[middle - SPLIT :, :], both_rows))
    for copy in copies:
        copy.wait()


PARAMS = pltpu.CompilerParams(vmem_limit_bytes=48 * 1024 * 1024)
IN_HBM = pl.BlockSpec(memory_space=pltpu.HBM)
IN_VMEM = pl.BlockSpec(memory_space=pltpu.VMEM)
IN_SMEM = pl.BlockSpec(memory_space=pltpu.SMEM)


def spectra(masks, cell_ids, dose, kernels, kernel_weights, owned_counts):
    table = tables()
    operands = [masks, cell_ids.T, dose]
    operands += [jnp.asarray(table[n]) for n in ("forward_cols", "forward_rows")]
    operands += [kernels, kernel_weights, owned_counts]
    in_hbm = [pltpu.with_memory_space_constraint(op, pltpu.HBM) for op in operands]
    return pl.pallas_call(
        spectra_kernel,
        out_shape=(
            jax.ShapeDtypeStruct((COLS, PACKET, LANES), BF16),
            jax.ShapeDtypeStruct((2, NK // 2, NF, LANES), F32),
            pltpu.SMEM((COLS,), jnp.int32),
        ),
        in_specs=[IN_HBM] * len(operands),
        out_specs=(IN_VMEM, IN_VMEM, IN_SMEM),
        scratch_shapes=[
            *[pltpu.VMEM(op.shape, op.dtype) for op in operands[:-2]],
            *[pltpu.SMEM(op.shape, op.dtype) for op in operands[-2:]],
            pltpu.VMEM((16, LANES), F32),
            pltpu.SemaphoreType.DMA((len(operands) + SLOTS - 1,)),
        ],
        compiler_params=PARAMS,
    )(*in_hbm)


def route(packets, starts):
    return pl.pallas_call(
        routing_kernel,
        out_shape=(
            jax.ShapeDtypeStruct((ROWS, OUTGOING, LANES), BF16),
            pltpu.SMEM((WINDOW,), jnp.int32),
        ),
        in_specs=[IN_VMEM, IN_SMEM],
        out_specs=(IN_VMEM, IN_SMEM),
        scratch_shapes=[
            pltpu.VMEM((CELLS + SLOTS, HALF, LANES), F32),
            pltpu.VMEM((COLS * 16, LANES), F32),
            pltpu.VMEM((CELLS + 8, LANES), F32),
            pltpu.VMEM((16, LANES), jnp.int32),
            pltpu.SMEM((16, LANES), jnp.int32),
            pltpu.SMEM((ROWS * 16 + 16,), jnp.int32),
            pltpu.SMEM((16,), jnp.int32),
            pltpu.SemaphoreType.DMA,
        ],
        compiler_params=PARAMS,
    )(packets, starts)


def develop(incoming, place, ker, threshold):
    table = tables()
    names = ("turned", "spread_up", "spread_low", "rest", "rest_mask")
    names += ("inverse_left", "edge_left", "inverse_right", "across", "down_upper", "down_lower")
    constants = [jnp.asarray(table[n]) for n in names]
    return pl.pallas_call(
        develop_kernel,
        out_shape=jax.ShapeDtypeStruct((2 * TILE, 4 * TILE), BF16),
        in_specs=[IN_VMEM, IN_SMEM, IN_VMEM, IN_SMEM, *[IN_VMEM] * len(constants)],
        out_specs=IN_HBM,
        scratch_shapes=[
            pltpu.VMEM((ROWS * 16, LANES), F32),
            pltpu.VMEM((2 * TILE, 4 * TILE), BF16),
            pltpu.SemaphoreType.DMA((3,)),
        ],
        compiler_params=PARAMS,
    )(incoming, place, ker, threshold, *constants)


def local(masks, owned_counts, cell_ids, kernels, kernel_weights, dose, threshold):
    packet, ker, starts = spectra(
        masks, cell_ids, dose, kernels, kernel_weights, owned_counts
    )
    packets = lax.all_to_all(packet, "cols", split_axis=0, concat_axis=0, tiled=True)
    outgoing, place = route(packets, starts)
    incoming = lax.all_to_all(outgoing, "rows", split_axis=0, concat_axis=0, tiled=True)
    return develop(incoming, place, ker, threshold)


def solution(mesh):
    return jax.shard_map(
        local,
        mesh=mesh,
        in_specs=(
            P(("rows", "cols"), None, None),
            P(),
            P(None, "cols"),
            P(),
            P(),
            P("rows", "cols"),
            P(),
        ),
        out_specs=P("rows", "cols"),
        check_vma=False,
    )
```

time: 41 us -> 38.6 us (0.941)
  waiting for transfers between devices: 8.13 us -> 5.85 us
    all_to_all x1, waiting for transfers between devices: 8.13 us -> 5.85 us  [local(): lax.all_to_all(outgoing, 'rows', split_axis=0, concat_axis=0, tiled=True)]
where the time goes in v3:
time: 38.6 us; the launch traced here: 38.4 us
  blocking collectives  15.9 us (41%)
  Pallas kernels  9.47 us (25%)
  starting transfers between devices  6.32 us (16%)
  waiting for transfers between devices  5.85 us (15%)
  between operations  0.8 us (2%)
    all_to_all x1, blocking collectives, local(): lax.all_to_all(packet, 'cols', split_axis=0, concat_axis=0, tiled=True)  15.9 us
    all_to_all x1, starting transfers between devices, local(): lax.all_to_all(outgoing, 'rows', split_axis=0, concat_axis=0, tiled=True)  6.32 us
    all_to_all x1, waiting for transfers between devices, local(): lax.all_to_all(outgoing, 'rows', split_axis=0, concat_axis=0, tiled=True)  5.85 us
    pallas_call x1, Pallas kernels, develop(): pl.pallas_call(develop_kernel, out_shape=jax.ShapeDtypeStruct((2 * TILE,...  4.35 us
    pallas_call x1, Pallas kernels, spectra(): pl.pallas_call(spectra_kernel, out_shape=(jax.ShapeDtypeStruct((COLS, PAC...  2.96 us
    pallas_call x1, Pallas kernels, route(): pl.pallas_call(routing_kernel, out_shape=(jax.ShapeDtypeStruct((ROWS, OUT...  2.17 us
  transfers between devices with their start and end apart: 1, of which 1 were waited for; matrix products, arithmetic and copies ran while one was open for 0% of the time, Pallas kernels for 0%

profile of v3, /device:TPU:1, one launch (start us, length us, event | category | flops | bytes accessed | tf_op | source)
XLA Modules:
  0.0 38.4 jit_solution(7921419226598541041)
XLA Ops:
  0.0 0.0 copy-start.6
  0.0 0.0 copy-start.10
  0.0 0.0 copy-start.8
  0.0 0.0 copy-start.9
  0.1 0.0 copy-start.7
  0.1 0.0 copy-start.2
  0.1 0.0 copy-start.3
  0.1 0.0 copy-start.4
  0.1 3.0 %shard_map.190 = (bf16[16,64,128]{2,1,0:T(8,128)(2,1)S(1)}, f32[2,8,32,128]{3,2,1,0:T(8,128)S(1)}, s32[16]{0:T(128)S(4)}) custom-call(bf16[6,384,384]{2,1,0:T(8,128)(2,1)} %mask.1, s32[4,16]{1,0:T(4,128)} %bitcast.1, f32[2,4]{1,0:T(2,128)} %dose.1, bf16[384,128]{1,0:T(8,128)(2,1)} %constant.26.clone.fwd_cols, bf16[128,384]{1,0:T(8,128)(2,1)} %constant.27.clone.fwd_rows, ...), custom_call_target="tpu_custom_call" | custom-call | tf_op jit(solution)/shard_map/pallas_call | solution.py:439
  3.1 15.9 %all_to_all.10.packets = bf16[16,64,128]{2,1,0:T(8,128)(2,1)S(1)} all-to-all(bf16[16,64,128]{2,1,0:T(8,128)(2,1)S(1)} %get-tuple-element.10), channel_id=1, replica_groups=mesh['rows'=8,'cols'=16] {'cols'}, dimensions={0} | all-to-all | bytes 524288 | tf_op jit(solution)/shard_map/all_to_all | solution.py:504
  18.9 2.2 %shard_map.191 = (bf16[8,128,128]{2,1,0:T(8,128)(2,1)}, s32[24]{0:T(128)S(4)}) custom-call(bf16[16,64,128]{2,1,0:T(8,128)(2,1)S(1)} %all_to_all.10.packets, s32[16]{0:T(128)S(4)} %get-tuple-element.11.starts), custom_call_target="tpu_custom_call" | custom-call | tf_op jit(solution)/shard_map/pallas_call | solution.py:459
  21.1 6.3 %all-to-all-start.1 = ((bf16[8,128,128]{2,1,0:T(8,128)(2,1)}), bf16[8,128,128]{2,1,0:T(8,128)(2,1)S(1)}, u32[]{:S(2)}, u32[]{:S(2)}) async-start(bf16[8,128,128]{2,1,0:T(8,128)(2,1)} %get-tuple-element.12), calls=%async_computation.1 | async-start | bytes 524288 | tf_op jit(solution)/shard_map/all_to_all | solution.py:506
  28.1 5.9 %all-to-all-done.1.tiles = bf16[8,128,128]{2,1,0:T(8,128)(2,1)S(1)} async-done(((bf16[8,128,128]{2,1,0:T(8,128)(2,1)}), bf16[8,128,128]{2,1,0:T(8,128)(2,1)S(1)}, u32[]{:S(2)}, u32[]{:S(2)}) %all-to-all-start.1) | async-done | bytes 262176 | tf_op jit(solution)/shard_map/all_to_all | solution.py:506
  33.9 0.0 copy-done
  33.9 0.0 copy-done.5
  33.9 0.0 copy-done.6
  34.0 0.0 copy-done.10
  34.0 0.0 copy-done.8
  34.0 0.0 copy-done.9
  34.0 0.0 copy-done.7
  34.0 0.0 copy-done.2
  34.0 0.0 copy-done.3
  34.0 0.0 copy-done.4
  34.0 4.3 %shard_map.192 = bf16[768,1536]{1,0:T(8,128)(2,1)} custom-call(bf16[8,128,128]{2,1,0:T(8,128)(2,1)S(1)} %all-to-all-done.1.tiles, s32[24]{0:T(128)S(4)} %get-tuple-element.13.place, f32[2,8,32,128]{3,2,1,0:T(8,128)S(1)} %get-tuple-element.14.ker, f32[1]{0:T(128)S(6)} %copy.21.threshold, bf16[192,192]{1,0:T(8,128)(2,1)S(1)} %copy-done.4, ...), custom_call_target="tpu_custom_call" | custom-call | tf_op jit(solution)/shard_map/pallas_call | solution.py:486
  (4 shorter events, 0.0 us)
Async XLA Ops:
  0.0 33.9 %copy-start = (bf16[400,160]{1,0:T(8,128)(2,1)S(1)}, bf16[400,160]{1,0:T(8,128)(2,1)}, u32[]{:S(2)}) copy-start(bf16[400,160]{1,0:T(8,128)(2,1)} %constant.38.clone.down_lower) | copy-start | bytes 384004
  0.0 33.9 %copy-start.5 = (bf16[368,80]{1,0:T(8,128)(2,1)S(1)}, bf16[368,80]{1,0:T(8,128)(2,1)}, u32[]{:S(2)}) copy-start(bf16[368,80]{1,0:T(8,128)(2,1)} %constant.37.clone.down_upper) | copy-start | bytes 176644
  0.0 33.9 %copy-start.1 = (bf16[256,384]{1,0:T(8,128)(2,1)S(1)}, bf16[256,384]{1,0:T(8,128)(2,1)}, u32[]{:S(2)}) copy-start(bf16[256,384]{1,0:T(8,128)(2,1)} %constant.36.clone.across) | copy-start | bytes 589828
  0.0 33.9 %copy-start.6 = (bf16[128,256]{1,0:T(8,128)(2,1)S(1)}, bf16[128,256]{1,0:T(8,128)(2,1)}, u32[]{:S(2)}) copy-start(bf16[128,256]{1,0:T(8,128)(2,1)} %constant.35.clone.inv_right) | copy-start | bytes 196612
  0.0 33.9 %copy-start.10 = (bf16[16,64]{1,0:T(8,128)(2,1)S(1)}, bf16[16,64]{1,0:T(8,128)(2,1)}, u32[]{:S(2)}) copy-start(bf16[16,64]{1,0:T(8,128)(2,1)} %constant.34.clone.edge_left) | copy-start | bytes 6148
  0.0 33.9 %copy-start.8 = (bf16[64,64]{1,0:T(8,128)(2,1)S(1)}, bf16[64,64]{1,0:T(8,128)(2,1)}, u32[]{:S(2)}) copy-start(bf16[64,64]{1,0:T(8,128)(2,1)} %constant.33.clone.inv_left) | copy-start | bytes 24580
  0.0 33.9 %copy-start.9 = (f32[16,128]{1,0:T(8,128)S(1)}, f32[16,128]{1,0:T(8,128)}, u32[]{:S(2)}) copy-start(f32[16,128]{1,0:T(8,128)} %constant.32.clone.rest_mask) | copy-start | bytes 24580
  0.1 33.9 %copy-start.7 = (bf16[128,256]{1,0:T(8,128)(2,1)S(1)}, bf16[128,256]{1,0:T(8,128)(2,1)}, u32[]{:S(2)}) copy-start(bf16[128,256]{1,0:T(8,128)(2,1)} %constant.31.clone.rest) | copy-start | bytes 196612
  0.1 33.9 %copy-start.2 = (bf16[128,512]{1,0:T(8,128)(2,1)S(1)}, bf16[128,512]{1,0:T(8,128)(2,1)}, u32[]{:S(2)}) copy-start(bf16[128,512]{1,0:T(8,128)(2,1)} %constant.30.clone.spread_low) | copy-start | bytes 393220
  0.1 33.9 %copy-start.3 = (bf16[128,512]{1,0:T(8,128)(2,1)S(1)}, bf16[128,512]{1,0:T(8,128)(2,1)}, u32[]{:S(2)}) copy-start(bf16[128,512]{1,0:T(8,128)(2,1)} %constant.29.clone.spread_up) | copy-start | bytes 393220
  0.1 33.9 %copy-start.4 = (bf16[192,192]{1,0:T(8,128)(2,1)S(1)}, bf16[192,192]{1,0:T(8,128)(2,1)}, u32[]{:S(2)}) copy-start(bf16[192,192]{1,0:T(8,128)(2,1)} %constant.28.clone.turned) | copy-start | bytes 221188
  21.1 12.8 %all-to-all-start.1 = ((bf16[8,128,128]{2,1,0:T(8,128)(2,1)}), bf16[8,128,128]{2,1,0:T(8,128)(2,1)S(1)}, u32[]{:S(2)}, u32[]{:S(2)}) async-start(bf16[8,128,128]{2,1,0:T(8,128)(2,1)} %get-tuple-element.12), calls=%async_computation.1 | async-start | bytes 524288 | tf_op jit(solution)/shard_map/all_to_all | solution.py:506

commit v4 on v3

--- a/solution.py
+++ b/solution.py
@@ -25,9 +25,12 @@
 DOSES = IDS + 4
 PACKET = EXTRA + 16
 WINDOW = 4 * 6
-MOST = 14
+NEAR = 6
+FAR = 8
+MOST = NEAR + FAR
 REST = MOST * HALF // 2
 OUTGOING = REST + 16
+STARTS, SEATS, PLACES = 0, COLS, COLS + ROWS * NEAR
 STACK = Q + 2 * REACH
 SPLIT = TILE - 2 * REACH
 BF16 = jnp.bfloat16
@@ -149,28 +152,79 @@
     return lax.broadcasted_iota(jnp.int32, shape, 1)
 
 
+def seats(cells, chosen, dest, row):
+    count = jnp.int32(0)
+    for cell in cells:
+        chosen[dest * 16 + count] = cell & (CELLS - 1)
+        count = count + ((cell >> 5) == row).astype(jnp.int32)
+    return count
+
+
+def sources(cells, place, at, taken, first):
+    for n in range(ROWS + 1):
+        taken[n] = jnp.int32(first)
+    for n, cell in enumerate(cells):
+        source = cell >> 5
+        rank = taken[source + 1]
+        taken[source + 1] = rank + 1
+        place[at + n] = jnp.where(cell >= 0, source * 16 + rank, -1)
+
+
+def rows_of(dest):
+    return [i for i in range(2 * dest - 1, 2 * dest + 3) if 0 <= i < 2 * ROWS]
+
+
+def window_rows(ids_s, columns):
+    cells = []
+    for i in range(4):
+        tile_row = 2 * lax.axis_index("rows") - 1 + i
+        inside = (tile_row >= 0) & (tile_row < 2 * ROWS)
+        tile_row = jnp.clip(tile_row, 0, 2 * ROWS - 1)
+        cells += [jnp.where(inside, ids_s[j, tile_row], -1) for j in columns]
+    return cells
+
+
+def near_table(ids_s, counts_s, table, chosen, taken):
+    row = lax.axis_index("rows")
+    start = jnp.int32(0)
+    for c in range(COLS):
+        table[STARTS + c] = start
+        start = start + counts_s[row, c]
+    for dest in range(ROWS):
+        cells = [ids_s[j, i] for i in rows_of(dest) for j in range(4)]
+        count = seats(cells, chosen, dest, row)
+        for n in range(NEAR):
+            cell = jnp.where(n < count, chosen[dest * 16 + n], CELLS)
+            table[SEATS + dest * NEAR + n] = cell
+    sources(window_rows(ids_s, range(4)), table, PLACES, taken, 0)
+
+
 def spectra_kernel(
     mask, ids, dose, fwd_cols, fwd_rows, kernels, weights, counts,
-    out, ker, starts,
-    mask_v, ids_v, dose_v, cols_v, rows_v, kernels_v, weights_s, counts_s, extra, sems,
+    out, ker, table,
+    mask_v, ids_v, dose_v, cols_v, rows_v, kernels_v, weights_s, counts_s,
+    ids_s, chosen, taken, extra, sems,
 ):
-    moves = [(fwd_cols, cols_v)]
+    moves = [(ids, ids_s), (counts, counts_s), (fwd_cols, cols_v)]
     moves += [(mask.at[s], mask_v.at[s]) for s in range(SLOTS)]
-    moves += [(kernels, kernels_v), (weights, weights_s), (counts, counts_s)]
-    moves += [(fwd_rows, rows_v), (ids, ids_v), (dose, dose_v)]
+    moves += [(kernels, kernels_v), (weights, weights_s), (fwd_rows, rows_v)]
+    moves += [(ids, ids_v), (dose, dose_v)]
     copies = [
         pltpu.make_async_copy(src, dst, sems.at[i]) for i, (src, dst) in enumerate(moves)
     ]
     for copy in copies:
         copy.start()
-    for copy in copies[:4]:
+    for copy in copies[:2]:
+        copy.wait()
+    near_table(ids_s, counts_s, table, chosen, taken)
+    for copy in copies[2:6]:
         copy.wait()
 
     left = lanes_of((TILE, LANES)) < Q
     pairs = []
     for slot in range(SLOTS):
         if slot == 3:
-            for copy in copies[4:]:
+            for copy in copies[6:]:
                 copy.wait()
             for two in range(NK // 2):
                 re, im = [], []
@@ -180,10 +234,6 @@
                     im.append(kernels_v[1, k] * scale)
                 ker[0, two] = jnp.concatenate([re[0], im[0], re[1], im[1]], axis=1)
                 ker[1, two] = jnp.concatenate([-im[0], re[0], -im[1], re[1]], axis=1)
-            start = jnp.int32(0)
-            for c in range(COLS):
-                starts[c] = start
-                start = start + counts_s[lax.axis_index("rows"), c]
         cols = dot(mask_v[slot], cols_v[...])
         cols = cols + pltpu.roll(cols, Q, 1)
         high = cols.astype(BF16).astype(F32)
@@ -234,7 +284,7 @@
 
 
 def routing_kernel(
-    packets, starts,
+    packets, table,
     out, place,
     held, rests, buffer, where_v, where_s, chosen, taken, sem,
 ):
@@ -251,18 +301,16 @@
     line = lax.broadcasted_iota(jnp.int32, (16, LANES), 0)
     first = IDS - EXTRA
     window = jnp.where(
-        line == 0,
-        pltpu.roll(before, 16 - first - 3, 0),
-        jnp.where(line < 5, pltpu.roll(here, 16 - first + 1, 0), pltpu.roll(after, 16 - first + 5, 0)),
+        line == 0, pltpu.roll(before, 16 - first - 3, 0), pltpu.roll(after, 16 - first + 1, 0)
     ).astype(jnp.int32)
-    exists = ((line > 0) | (col > 0)) & ((line < 5) | (col < COLS - 1)) & (line < 6)
+    exists = ((line == 0) & (col > 0)) | ((line == 1) & (col < COLS - 1))
     where_v[...] = jnp.where(exists, window, -1)
     copy = pltpu.make_async_copy(where_v, where_s, sem)
     copy.start()
 
     left = lanes_of((HALF, LANES)) < Q
     for c in range(COLS):
-        start = starts[c]
+        start = table[STARTS + c]
         for s in range(SLOTS):
             pair = packets[c, (s // 2) * HALF : (s // 2 + 1) * HALF, :].astype(F32)
             moved = pltpu.roll(pair, Q, 1)
@@ -279,41 +327,31 @@
         before[at],
         jnp.where(lane < 32, pltpu.roll(here[at], 16, 1), pltpu.roll(after[at], 32, 1)),
     )
-    for n in range(ROWS + 1):
-        taken[n] = jnp.int32(0)
+
+    def send(dest, cells, at):
+        for n in range(0, len(cells), 2):
+            one, two = held[cells[n]], held[cells[n + 1]]
+            rows = slice(at + n // 2 * HALF, at + (n // 2 + 1) * HALF)
+            out[dest, rows, :] = jnp.where(left, one, two).astype(BF16)
+
+    near = [
+        [table[SEATS + dest * NEAR + n] for n in range(NEAR)] for dest in range(ROWS)
+    ]
+    for dest in range(ROWS):
+        send(dest, near[dest], 0)
     copy.wait()
-
-    for i in range(4):
-        tile_row = 2 * row - 1 + i
-        inside = (tile_row >= 0) & (tile_row < 2 * ROWS)
-        for j in range(6):
-            cell = where_s[j, jnp.clip(tile_row, 0, 2 * ROWS - 1)]
-            cell = jnp.where(inside, cell, -1)
-            source = cell >> 5
-            rank = taken[source + 1]
-            taken[source + 1] = rank + 1
-            place[6 * i + j] = jnp.where(cell >= 0, source * 16 + rank, -1)
-
+    sources(window_rows(where_s, range(2)), place, 0, taken, NEAR)
     for dest in range(ROWS):
-        count = jnp.int32(0)
-        for i in range(4):
-            tile_row = 2 * dest - 1 + i
-            if 0 <= tile_row < 2 * ROWS:
-                for j in range(6):
-                    cell = where_s[j, tile_row]
-                    chosen[dest * 16 + count] = cell & (CELLS - 1)
-                    count = count + ((cell >> 5) == row).astype(jnp.int32)
-        cells = [jnp.where(n < count, chosen[dest * 16 + n], CELLS) for n in range(MOST)]
-        for pair in range(MOST // 2):
-            one, two = cells[2 * pair], cells[2 * pair + 1]
-            at = pair * HALF
-            out[dest, at : at + HALF, :] = jnp.where(left, held[one], held[two]).astype(BF16)
-        rows = [buffer[pl.ds(cell, 1), :] for cell in cells]
+        cells = [where_s[j, i] for i in rows_of(dest) for j in range(2)]
+        count = seats(cells, chosen, dest, row)
+        cells = [jnp.where(n < count, chosen[dest * 16 + n], CELLS) for n in range(FAR)]
+        send(dest, cells, NEAR // 2 * HALF)
+        rows = [buffer[pl.ds(cell, 1), :] for cell in near[dest] + cells]
         out[dest, REST : REST + 16, :] = jnp.concatenate(rows + [doses], axis=0).astype(BF16)
 
 
 def develop_kernel(
-    tiles, place, ker, threshold, turned, spread_up, spread_low, rest, rest_mask,
+    tiles, table, place, ker, threshold, turned, spread_up, spread_low, rest, rest_mask,
     inv_left, edge_left, inv_right, across, down_upper, down_lower,
     out,
     after_rows, stage, sems,
@@ -327,13 +365,15 @@
     for t in range(0, WINDOW, 2):
         both = []
         for n in (t, t + 1):
-            here = jnp.maximum(place[n], 0)
+            i, j = n // 6, n % 6
+            found = table[PLACES + 4 * i + j - 1] if 1 <= j < 5 else place[2 * i + j // 5]
+            here = jnp.maximum(found, 0)
             rank = here & 15
             at = pl.multiple_of((rank >> 1) * HALF, HALF)
             pair = tiles[here >> 4, pl.ds(at, HALF), :].astype(F32)
             tile = jnp.where((rank & 1) == (n & 1), pair, pltpu.roll(pair, Q, 1))
-            both.append(jnp.where(place[n] >= 0, tile, 0.0))
-            line = jnp.where(place[n] >= 0, after_rows[pl.ds(here, 1), :], 0.0)
+            both.append(jnp.where(found >= 0, tile, 0.0))
+            line = jnp.where(found >= 0, after_rows[pl.ds(here, 1), :], 0.0)
             rests.append(jnp.broadcast_to(line, (HALF, LANES)) * rest_mask[...])
         held.append(jnp.where(left, both[0], both[1]).astype(BF16))
     held = jnp.concatenate(held, axis=0)
@@ -441,26 +481,29 @@
         out_shape=(
             jax.ShapeDtypeStruct((COLS, PACKET, LANES), BF16),
             jax.ShapeDtypeStruct((2, NK // 2, NF, LANES), F32),
-            pltpu.SMEM((COLS,), jnp.int32),
+            pltpu.SMEM((PLACES + 16,), jnp.int32),
         ),
         in_specs=[IN_HBM] * len(operands),
         out_specs=(IN_VMEM, IN_VMEM, IN_SMEM),
         scratch_shapes=[
             *[pltpu.VMEM(op.shape, op.dtype) for op in operands[:-2]],
             *[pltpu.SMEM(op.shape, op.dtype) for op in operands[-2:]],
+            pltpu.SMEM((4, 2 * ROWS), jnp.int32),
+            pltpu.SMEM((ROWS * 16 + 16,), jnp.int32),
+            pltpu.SMEM((16,), jnp.int32),
             pltpu.VMEM((16, LANES), F32),
-            pltpu.SemaphoreType.DMA((len(operands) + SLOTS - 1,)),
+            pltpu.SemaphoreType.DMA((len(operands) + SLOTS,)),
         ],
         compiler_params=PARAMS,
     )(*in_hbm)
 
 
-def route(packets, starts):
+def route(packets, seating):
     return pl.pallas_call(
         routing_kernel,
         out_shape=(
             jax.ShapeDtypeStruct((ROWS, OUTGOING, LANES), BF16),
-            pltpu.SMEM((WINDOW,), jnp.int32),
+            pltpu.SMEM((8,), jnp.int32),
         ),
         in_specs=[IN_VMEM, IN_SMEM],
         out_specs=(IN_VMEM, IN_SMEM),
@@ -475,10 +518,10 @@
             pltpu.SemaphoreType.DMA,
         ],
         compiler_params=PARAMS,
-    )(packets, starts)
-
-
-def develop(incoming, place, ker, threshold):
+    )(packets, seating)
+
+
+def develop(incoming, seating, place, ker, threshold):
     table = tables()
     names = ("turned", "spread_up", "spread_low", "rest", "rest_mask")
     names += ("inverse_left", "edge_left", "inverse_right", "across", "down_upper", "down_lower")
@@ -486,7 +529,7 @@
     return pl.pallas_call(
         develop_kernel,
         out_shape=jax.ShapeDtypeStruct((2 * TILE, 4 * TILE), BF16),
-        in_specs=[IN_VMEM, IN_SMEM, IN_VMEM, IN_SMEM, *[IN_VMEM] * len(constants)],
+        in_specs=[IN_VMEM, IN_SMEM, IN_SMEM, IN_VMEM, IN_SMEM, *[IN_VMEM] * len(constants)],
         out_specs=IN_HBM,
         scratch_shapes=[
             pltpu.VMEM((ROWS * 16, LANES), F32),
@@ -494,17 +537,17 @@
             pltpu.SemaphoreType.DMA((3,)),
         ],
         compiler_params=PARAMS,
-    )(incoming, place, ker, threshold, *constants)
+    )(incoming, seating, place, ker, threshold, *constants)
 
 
 def local(masks, owned_counts, cell_ids, kernels, kernel_weights, dose, threshold):
-    packet, ker, starts = spectra(
+    packet, ker, seating = spectra(
         masks, cell_ids, dose, kernels, kernel_weights, owned_counts
     )
     packets = lax.all_to_all(packet, "cols", split_axis=0, concat_axis=0, tiled=True)
-    outgoing, place = route(packets, starts)
+    outgoing, place = route(packets, seating)
     incoming = lax.all_to_all(outgoing, "rows", split_axis=0, concat_axis=0, tiled=True)
-    return develop(incoming, place, ker, threshold)
+    return develop(incoming, seating, place, ker, threshold)
 
 
 def solution(mesh):

time: 38.6 us -> 38.3 us (level)
  no operation moved by 1% of the time
where the time goes in v4:
time: 38.3 us; the launch traced here: 38.1 us
  blocking collectives  15.9 us (42%)
  Pallas kernels  9.15 us (24%)
  starting transfers between devices  6.32 us (17%)
  waiting for transfers between devices  5.85 us (15%)
  between operations  0.8 us (2%)
    all_to_all x1, blocking collectives, local(): lax.all_to_all(packet, 'cols', split_axis=0, concat_axis=0, tiled=True)  15.9 us
    all_to_all x1, starting transfers between devices, local(): lax.all_to_all(outgoing, 'rows', split_axis=0, concat_axis=0, tiled=True)  6.32 us
    all_to_all x1, waiting for transfers between devices, local(): lax.all_to_all(outgoing, 'rows', split_axis=0, concat_axis=0, tiled=True)  5.85 us
    pallas_call x1, Pallas kernels, develop(): pl.pallas_call(develop_kernel, out_shape=jax.ShapeDtypeStruct((2 * TILE,...  4.33 us
    pallas_call x1, Pallas kernels, spectra(): pl.pallas_call(spectra_kernel, out_shape=(jax.ShapeDtypeStruct((COLS, PAC...  2.98 us
    pallas_call x1, Pallas kernels, route(): pl.pallas_call(routing_kernel, out_shape=(jax.ShapeDtypeStruct((ROWS, OUT...  1.84 us
  transfers between devices with their start and end apart: 1, of which 1 were waited for; matrix products, arithmetic and copies ran while one was open for 0% of the time, Pallas kernels for 0%

profile of v4, /device:TPU:1, one launch (start us, length us, event | category | flops | bytes accessed | tf_op | source)
XLA Modules:
  0.0 38.1 jit_solution(7314922058827241675)
XLA Ops:
  0.0 0.0 copy-start.6
  0.0 0.0 copy-start.10
  0.0 0.0 copy-start.8
  0.0 0.0 copy-start.9
  0.1 0.0 copy-start.7
  0.1 0.0 copy-start.2
  0.1 0.0 copy-start.3
  0.1 0.0 copy-start.4
  0.1 3.0 %shard_map.190 = (bf16[16,64,128]{2,1,0:T(8,128)(2,1)S(1)}, f32[2,8,32,128]{3,2,1,0:T(8,128)S(1)}, s32[80]{0:T(128)S(4)}) custom-call(bf16[6,384,384]{2,1,0:T(8,128)(2,1)} %mask.1, s32[4,16]{1,0:T(4,128)} %bitcast.1, f32[2,4]{1,0:T(2,128)} %dose.1, bf16[384,128]{1,0:T(8,128)(2,1)} %constant.26.clone.fwd_cols, bf16[128,384]{1,0:T(8,128)(2,1)} %constant.27.clone.fwd_rows, ...), custom_call_target="tpu_custom_call" | custom-call | tf_op jit(solution)/shard_map/pallas_call | solution.py:479
  3.1 15.9 %all_to_all.10.packets = bf16[16,64,128]{2,1,0:T(8,128)(2,1)S(1)} all-to-all(bf16[16,64,128]{2,1,0:T(8,128)(2,1)S(1)} %get-tuple-element.10), channel_id=1, replica_groups=mesh['rows'=8,'cols'=16] {'cols'}, dimensions={0} | all-to-all | bytes 524288 | tf_op jit(solution)/shard_map/all_to_all | solution.py:547
  19.0 1.8 %shard_map.191 = (bf16[8,128,128]{2,1,0:T(8,128)(2,1)}, s32[8]{0:T(128)S(4)}) custom-call(bf16[16,64,128]{2,1,0:T(8,128)(2,1)S(1)} %all_to_all.10.packets, s32[80]{0:T(128)S(4)} %get-tuple-element.11.table), custom_call_target="tpu_custom_call" | custom-call | tf_op jit(solution)/shard_map/pallas_call | solution.py:502
  20.8 6.3 %all-to-all-start.1 = ((bf16[8,128,128]{2,1,0:T(8,128)(2,1)}), bf16[8,128,128]{2,1,0:T(8,128)(2,1)S(1)}, u32[]{:S(2)}, u32[]{:S(2)}) async-start(bf16[8,128,128]{2,1,0:T(8,128)(2,1)} %get-tuple-element.12), calls=%async_computation.1 | async-start | bytes 524288 | tf_op jit(solution)/shard_map/all_to_all | solution.py:549
  27.8 5.9 %all-to-all-done.1.tiles = bf16[8,128,128]{2,1,0:T(8,128)(2,1)S(1)} async-done(((bf16[8,128,128]{2,1,0:T(8,128)(2,1)}), bf16[8,128,128]{2,1,0:T(8,128)(2,1)S(1)}, u32[]{:S(2)}, u32[]{:S(2)}) %all-to-all-start.1) | async-done | bytes 262176 | tf_op jit(solution)/shard_map/all_to_all | solution.py:549
  33.6 0.0 copy-done
  33.6 0.0 copy-done.5
  33.6 0.0 copy-done.1
  33.6 0.0 copy-done.6
  33.6 0.0 copy-done.10
  33.7 0.0 copy-done.8
  33.7 0.0 copy-done.9
  33.7 0.0 copy-done.7
  33.7 0.0 copy-done.2
  33.7 0.0 copy-done.3
  33.7 4.3 %shard_map.192 = bf16[768,1536]{1,0:T(8,128)(2,1)} custom-call(bf16[8,128,128]{2,1,0:T(8,128)(2,1)S(1)} %all-to-all-done.1.tiles, s32[80]{0:T(128)S(4)} %get-tuple-element.11.table, s32[8]{0:T(128)S(4)} %get-tuple-element.13.place, f32[2,8,32,128]{3,2,1,0:T(8,128)S(1)} %get-tuple-element.14.ker, f32[1]{0:T(128)S(6)} %copy.21.threshold, ...), custom_call_target="tpu_custom_call" | custom-call | tf_op jit(solution)/shard_map/pallas_call | solution.py:529
  (4 shorter events, 0.0 us)
Async XLA Ops:
  0.0 33.6 %copy-start = (bf16[400,160]{1,0:T(8,128)(2,1)S(1)}, bf16[400,160]{1,0:T(8,128)(2,1)}, u32[]{:S(2)}) copy-start(bf16[400,160]{1,0:T(8,128)(2,1)} %constant.38.clone.down_lower) | copy-start | bytes 384004
  0.0 33.6 %copy-start.5 = (bf16[368,80]{1,0:T(8,128)(2,1)S(1)}, bf16[368,80]{1,0:T(8,128)(2,1)}, u32[]{:S(2)}) copy-start(bf16[368,80]{1,0:T(8,128)(2,1)} %constant.37.clone.down_upper) | copy-start | bytes 176644
  0.0 33.6 %copy-start.1 = (bf16[256,384]{1,0:T(8,128)(2,1)S(1)}, bf16[256,384]{1,0:T(8,128)(2,1)}, u32[]{:S(2)}) copy-start(bf16[256,384]{1,0:T(8,128)(2,1)} %constant.36.clone.across) | copy-start | bytes 589828
  0.0 33.6 %copy-start.6 = (bf16[128,256]{1,0:T(8,128)(2,1)S(1)}, bf16[128,256]{1,0:T(8,128)(2,1)}, u32[]{:S(2)}) copy-start(bf16[128,256]{1,0:T(8,128)(2,1)} %constant.35.clone.inv_right) | copy-start | bytes 196612
  0.0 33.6 %copy-start.10 = (bf16[16,64]{1,0:T(8,128)(2,1)S(1)}, bf16[16,64]{1,0:T(8,128)(2,1)}, u32[]{:S(2)}) copy-start(bf16[16,64]{1,0:T(8,128)(2,1)} %constant.34.clone.edge_left) | copy-start | bytes 6148
  0.0 33.6 %copy-start.8 = (bf16[64,64]{1,0:T(8,128)(2,1)S(1)}, bf16[64,64]{1,0:T(8,128)(2,1)}, u32[]{:S(2)}) copy-start(bf16[64,64]{1,0:T(8,128)(2,1)} %constant.33.clone.inv_left) | copy-start | bytes 24580
  0.0 33.6 %copy-start.9 = (f32[16,128]{1,0:T(8,128)S(1)}, f32[16,128]{1,0:T(8,128)}, u32[]{:S(2)}) copy-start(f32[16,128]{1,0:T(8,128)} %constant.32.clone.rest_mask) | copy-start | bytes 24580
  0.1 33.6 %copy-start.7 = (bf16[128,256]{1,0:T(8,128)(2,1)S(1)}, bf16[128,256]{1,0:T(8,128)(2,1)}, u32[]{:S(2)}) copy-start(bf16[128,256]{1,0:T(8,128)(2,1)} %constant.31.clone.rest) | copy-start | bytes 196612
  0.1 33.6 %copy-start.2 = (bf16[128,512]{1,0:T(8,128)(2,1)S(1)}, bf16[128,512]{1,0:T(8,128)(2,1)}, u32[]{:S(2)}) copy-start(bf16[128,512]{1,0:T(8,128)(2,1)} %constant.30.clone.spread_low) | copy-start | bytes 393220
  0.1 33.6 %copy-start.3 = (bf16[128,512]{1,0:T(8,128)(2,1)S(1)}, bf16[128,512]{1,0:T(8,128)(2,1)}, u32[]{:S(2)}) copy-start(bf16[128,512]{1,0:T(8,128)(2,1)} %constant.29.clone.spread_up) | copy-start | bytes 393220
  0.1 33.6 %copy-start.4 = (bf16[192,192]{1,0:T(8,128)(2,1)S(1)}, bf16[192,192]{1,0:T(8,128)(2,1)}, u32[]{:S(2)}) copy-start(bf16[192,192]{1,0:T(8,128)(2,1)} %constant.28.clone.turned) | copy-start | bytes 221188
  20.8 12.8 %all-to-all-start.1 = ((bf16[8,128,128]{2,1,0:T(8,128)(2,1)}), bf16[8,128,128]{2,1,0:T(8,128)(2,1)S(1)}, u32[]{:S(2)}, u32[]{:S(2)}) async-start(bf16[8,128,128]{2,1,0:T(8,128)(2,1)} %get-tuple-element.12), calls=%async_computation.1 | async-start | bytes 524288 | tf_op jit(solution)/shard_map/all_to_all | solution.py:549

commit v5 on v4

--- a/solution.py
+++ b/solution.py
@@ -205,9 +205,9 @@
     mask_v, ids_v, dose_v, cols_v, rows_v, kernels_v, weights_s, counts_s,
     ids_s, chosen, taken, extra, sems,
 ):
-    moves = [(ids, ids_s), (counts, counts_s), (fwd_cols, cols_v)]
+    moves = [(ids, ids_s), (counts, counts_s), (fwd_rows, rows_v)]
     moves += [(mask.at[s], mask_v.at[s]) for s in range(SLOTS)]
-    moves += [(kernels, kernels_v), (weights, weights_s), (fwd_rows, rows_v)]
+    moves += [(kernels, kernels_v), (weights, weights_s), (fwd_cols, cols_v)]
     moves += [(ids, ids_v), (dose, dose_v)]
     copies = [
         pltpu.make_async_copy(src, dst, sems.at[i]) for i, (src, dst) in enumerate(moves)
@@ -220,7 +220,6 @@
     for copy in copies[2:6]:
         copy.wait()
 
-    left = lanes_of((TILE, LANES)) < Q
     pairs = []
     for slot in range(SLOTS):
         if slot == 3:
@@ -234,10 +233,9 @@
                     im.append(kernels_v[1, k] * scale)
                 ker[0, two] = jnp.concatenate([re[0], im[0], re[1], im[1]], axis=1)
                 ker[1, two] = jnp.concatenate([-im[0], re[0], -im[1], re[1]], axis=1)
-        cols = dot(mask_v[slot], cols_v[...])
-        cols = cols + pltpu.roll(cols, Q, 1)
-        high = cols.astype(BF16).astype(F32)
-        pairs.append(jnp.where(left, high, cols - high).astype(BF16))
+        cols = dot(rows_v[...], mask_v[slot])
+        high, low = halves(cols[:Q] + cols[Q:])
+        pairs.append(jnp.concatenate([high, low], axis=0))
 
     lane = lanes_of((NF, LANES))
     line = lax.broadcasted_iota(jnp.int32, (NF, LANES), 0)
@@ -248,7 +246,7 @@
     lane1 = lanes_of((1, LANES))
     blocks, rows = [], []
     for slot in range(SLOTS):
-        both = dot(rows_v[...], pairs[slot])
+        both = dot(pairs[slot], cols_v[...])
         both = both[:Q] + both[Q:]
         both = both + pltpu.roll(both, Q, 1)
         top, bottom = both[:NF], both[NF:]
@@ -289,14 +287,10 @@
     held, rests, buffer, where_v, where_s, chosen, taken, sem,
 ):
     row, col = lax.axis_index("rows"), lax.axis_index("cols")
-    for c in range(COLS):
-        rests[c * 16 : (c + 1) * 16, :] = packets[c, EXTRA : EXTRA + 16, :].astype(F32)
-
     def rest_of(c):
-        return rests[pl.ds(pl.multiple_of(c * 16, 16), 16), :]
+        return packets[c, EXTRA : EXTRA + 16, :].astype(F32)
 
     before = rest_of(jnp.maximum(col - 1, 0))
-    here = rest_of(col)
     after = rest_of(jnp.minimum(col + 1, COLS - 1))
     line = lax.broadcasted_iota(jnp.int32, (16, LANES), 0)
     first = IDS - EXTRA
@@ -308,6 +302,9 @@
     copy = pltpu.make_async_copy(where_v, where_s, sem)
     copy.start()
 
+    here = rest_of(col)
+    for c in range(COLS):
+        rests[c * 16 : (c + 1) * 16, :] = rest_of(c)
     left = lanes_of((HALF, LANES)) < Q
     for c in range(COLS):
         start = table[STARTS + c]

time: 38.3 us -> 38 us (level)
  no operation moved by 1% of the time
where the time goes in v5:
time: 38 us; the launch traced here: 37.8 us
  blocking collectives  15.8 us (42%)
  Pallas kernels  8.86 us (23%)
  starting transfers between devices  6.32 us (17%)
  waiting for transfers between devices  5.85 us (15%)
  between operations  0.8 us (2%)
    all_to_all x1, blocking collectives, local(): lax.all_to_all(packet, 'cols', split_axis=0, concat_axis=0, tiled=True)  15.8 us
    all_to_all x1, starting transfers between devices, local(): lax.all_to_all(outgoing, 'rows', split_axis=0, concat_axis=0, tiled=True)  6.32 us
    all_to_all x1, waiting for transfers between devices, local(): lax.all_to_all(outgoing, 'rows', split_axis=0, concat_axis=0, tiled=True)  5.85 us
    pallas_call x1, Pallas kernels, develop(): pl.pallas_call(develop_kernel, out_shape=jax.ShapeDtypeStruct((2 * TILE,...  4.33 us
    pallas_call x1, Pallas kernels, spectra(): pl.pallas_call(spectra_kernel, out_shape=(jax.ShapeDtypeStruct((COLS, PAC...  2.7 us
    pallas_call x1, Pallas kernels, route(): pl.pallas_call(routing_kernel, out_shape=(jax.ShapeDtypeStruct((ROWS, OUT...  1.83 us
  transfers between devices with their start and end apart: 1, of which 1 were waited for; matrix products, arithmetic and copies ran while one was open for 0% of the time, Pallas kernels for 0%

profile of v5, /device:TPU:1, one launch (start us, length us, event | category | flops | bytes accessed | tf_op | source)
XLA Modules:
  0.0 37.8 jit_solution(506294149576476981)
XLA Ops:
  0.0 0.0 copy-start.6
  0.0 0.0 copy-start.10
  0.0 0.0 copy-start.8
  0.0 0.0 copy-start.9
  0.1 0.0 copy-start.7
  0.1 0.0 copy-start.2
  0.1 0.0 copy-start.3
  0.1 0.0 copy-start.4
  0.1 2.7 %shard_map.190 = (bf16[16,64,128]{2,1,0:T(8,128)(2,1)S(1)}, f32[2,8,32,128]{3,2,1,0:T(8,128)S(1)}, s32[80]{0:T(128)S(4)}) custom-call(bf16[6,384,384]{2,1,0:T(8,128)(2,1)} %mask.1, s32[4,16]{1,0:T(4,128)} %bitcast.1, f32[2,4]{1,0:T(2,128)} %dose.1, bf16[384,128]{1,0:T(8,128)(2,1)} %constant.26.clone.fwd_cols, bf16[128,384]{1,0:T(8,128)(2,1)} %constant.27.clone.fwd_rows, ...), custom_call_target="tpu_custom_call" | custom-call | tf_op jit(solution)/shard_map/pallas_call | solution.py:476
  2.8 15.8 %all_to_all.10.packets = bf16[16,64,128]{2,1,0:T(8,128)(2,1)S(1)} all-to-all(bf16[16,64,128]{2,1,0:T(8,128)(2,1)S(1)} %get-tuple-element.10), channel_id=1, replica_groups=mesh['rows'=8,'cols'=16] {'cols'}, dimensions={0} | all-to-all | bytes 524288 | tf_op jit(solution)/shard_map/all_to_all | solution.py:544
  18.7 1.8 %shard_map.191 = (bf16[8,128,128]{2,1,0:T(8,128)(2,1)}, s32[8]{0:T(128)S(4)}) custom-call(bf16[16,64,128]{2,1,0:T(8,128)(2,1)S(1)} %all_to_all.10.packets, s32[80]{0:T(128)S(4)} %get-tuple-element.11.table), custom_call_target="tpu_custom_call" | custom-call | tf_op jit(solution)/shard_map/pallas_call | solution.py:499
  20.5 6.3 %all-to-all-start.1 = ((bf16[8,128,128]{2,1,0:T(8,128)(2,1)}), bf16[8,128,128]{2,1,0:T(8,128)(2,1)S(1)}, u32[]{:S(2)}, u32[]{:S(2)}) async-start(bf16[8,128,128]{2,1,0:T(8,128)(2,1)} %get-tuple-element.12), calls=%async_computation.1 | async-start | bytes 524288 | tf_op jit(solution)/shard_map/all_to_all | solution.py:546
  27.5 5.9 %all-to-all-done.1.tiles = bf16[8,128,128]{2,1,0:T(8,128)(2,1)S(1)} async-done(((bf16[8,128,128]{2,1,0:T(8,128)(2,1)}), bf16[8,128,128]{2,1,0:T(8,128)(2,1)S(1)}, u32[]{:S(2)}, u32[]{:S(2)}) %all-to-all-start.1) | async-done | bytes 262176 | tf_op jit(solution)/shard_map/all_to_all | solution.py:546
  33.3 0.0 copy-done
  33.3 0.0 copy-done.5
  33.3 0.0 copy-done.1
  33.3 0.0 copy-done.6
  33.4 0.0 copy-done.10
  33.4 0.0 copy-done.8
  33.4 0.0 copy-done.9
  33.4 0.0 copy-done.7
  33.4 0.0 copy-done.2
  33.4 0.0 copy-done.3
  33.4 4.3 %shard_map.192 = bf16[768,1536]{1,0:T(8,128)(2,1)} custom-call(bf16[8,128,128]{2,1,0:T(8,128)(2,1)S(1)} %all-to-all-done.1.tiles, s32[80]{0:T(128)S(4)} %get-tuple-element.11.table, s32[8]{0:T(128)S(4)} %get-tuple-element.13.place, f32[2,8,32,128]{3,2,1,0:T(8,128)S(1)} %get-tuple-element.14.ker, f32[1]{0:T(128)S(6)} %copy.21.threshold, ...), custom_call_target="tpu_custom_call" | custom-call | tf_op jit(solution)/shard_map/pallas_call | solution.py:526
  (4 shorter events, 0.0 us)
Async XLA Ops:
  0.0 33.3 %copy-start = (bf16[400,160]{1,0:T(8,128)(2,1)S(1)}, bf16[400,160]{1,0:T(8,128)(2,1)}, u32[]{:S(2)}) copy-start(bf16[400,160]{1,0:T(8,128)(2,1)} %constant.38.clone.down_lower) | copy-start | bytes 384004
  0.0 33.3 %copy-start.5 = (bf16[368,80]{1,0:T(8,128)(2,1)S(1)}, bf16[368,80]{1,0:T(8,128)(2,1)}, u32[]{:S(2)}) copy-start(bf16[368,80]{1,0:T(8,128)(2,1)} %constant.37.clone.down_upper) | copy-start | bytes 176644
  0.0 33.3 %copy-start.1 = (bf16[256,384]{1,0:T(8,128)(2,1)S(1)}, bf16[256,384]{1,0:T(8,128)(2,1)}, u32[]{:S(2)}) copy-start(bf16[256,384]{1,0:T(8,128)(2,1)} %constant.36.clone.across) | copy-start | bytes 589828
  0.0 33.3 %copy-start.6 = (bf16[128,256]{1,0:T(8,128)(2,1)S(1)}, bf16[128,256]{1,0:T(8,128)(2,1)}, u32[]{:S(2)}) copy-start(bf16[128,256]{1,0:T(8,128)(2,1)} %constant.35.clone.inv_right) | copy-start | bytes 196612
  0.0 33.3 %copy-start.10 = (bf16[16,64]{1,0:T(8,128)(2,1)S(1)}, bf16[16,64]{1,0:T(8,128)(2,1)}, u32[]{:S(2)}) copy-start(bf16[16,64]{1,0:T(8,128)(2,1)} %constant.34.clone.edge_left) | copy-start | bytes 6148
  0.0 33.3 %copy-start.8 = (bf16[64,64]{1,0:T(8,128)(2,1)S(1)}, bf16[64,64]{1,0:T(8,128)(2,1)}, u32[]{:S(2)}) copy-start(bf16[64,64]{1,0:T(8,128)(2,1)} %constant.33.clone.inv_left) | copy-start | bytes 24580
  0.0 33.3 %copy-start.9 = (f32[16,128]{1,0:T(8,128)S(1)}, f32[16,128]{1,0:T(8,128)}, u32[]{:S(2)}) copy-start(f32[16,128]{1,0:T(8,128)} %constant.32.clone.rest_mask) | copy-start | bytes 24580
  0.1 33.3 %copy-start.7 = (bf16[128,256]{1,0:T(8,128)(2,1)S(1)}, bf16[128,256]{1,0:T(8,128)(2,1)}, u32[]{:S(2)}) copy-start(bf16[128,256]{1,0:T(8,128)(2,1)} %constant.31.clone.rest) | copy-start | bytes 196612
  0.1 33.3 %copy-start.2 = (bf16[128,512]{1,0:T(8,128)(2,1)S(1)}, bf16[128,512]{1,0:T(8,128)(2,1)}, u32[]{:S(2)}) copy-start(bf16[128,512]{1,0:T(8,128)(2,1)} %constant.30.clone.spread_low) | copy-start | bytes 393220
  0.1 33.3 %copy-start.3 = (bf16[128,512]{1,0:T(8,128)(2,1)S(1)}, bf16[128,512]{1,0:T(8,128)(2,1)}, u32[]{:S(2)}) copy-start(bf16[128,512]{1,0:T(8,128)(2,1)} %constant.29.clone.spread_up) | copy-start | bytes 393220
  0.1 33.3 %copy-start.4 = (bf16[192,192]{1,0:T(8,128)(2,1)S(1)}, bf16[192,192]{1,0:T(8,128)(2,1)}, u32[]{:S(2)}) copy-start(bf16[192,192]{1,0:T(8,128)(2,1)} %constant.28.clone.turned) | copy-start | bytes 221188
  20.5 12.8 %all-to-all-start.1 = ((bf16[8,128,128]{2,1,0:T(8,128)(2,1)}), bf16[8,128,128]{2,1,0:T(8,128)(2,1)S(1)}, u32[]{:S(2)}, u32[]{:S(2)}) async-start(bf16[8,128,128]{2,1,0:T(8,128)(2,1)} %get-tuple-element.12), calls=%async_computation.1 | async-start | bytes 524288 | tf_op jit(solution)/shard_map/all_to_all | solution.py:546

commit v6 on v5

--- a/solution.py
+++ b/solution.py
@@ -200,8 +200,8 @@
 
 
 def spectra_kernel(
-    mask, ids, dose, fwd_cols, fwd_rows, kernels, weights, counts,
-    out, ker, table,
+    mask, ids, dose, fwd_cols, fwd_rows, kernels, weights, counts, threshold,
+    out, ker, table, threshold_s,
     mask_v, ids_v, dose_v, cols_v, rows_v, kernels_v, weights_s, counts_s,
     ids_s, chosen, taken, extra, sems,
 ):
@@ -214,6 +214,7 @@
     ]
     for copy in copies:
         copy.start()
+    threshold_s[0] = threshold[0]
     for copy in copies[:2]:
         copy.wait()
     near_table(ids_s, counts_s, table, chosen, taken)
@@ -467,29 +468,31 @@
 IN_SMEM = pl.BlockSpec(memory_space=pltpu.SMEM)
 
 
-def spectra(masks, cell_ids, dose, kernels, kernel_weights, owned_counts):
+def spectra(masks, cell_ids, dose, kernels, kernel_weights, owned_counts, threshold):
     table = tables()
     operands = [masks, cell_ids.T, dose]
     operands += [jnp.asarray(table[n]) for n in ("forward_cols", "forward_rows")]
-    operands += [kernels, kernel_weights, owned_counts]
-    in_hbm = [pltpu.with_memory_space_constraint(op, pltpu.HBM) for op in operands]
+    operands += [kernels, kernel_weights, owned_counts, threshold]
+    in_hbm = [pltpu.with_memory_space_constraint(op, pltpu.HBM) for op in operands[:-1]]
+    in_hbm.append(operands[-1])
     return pl.pallas_call(
         spectra_kernel,
         out_shape=(
             jax.ShapeDtypeStruct((COLS, PACKET, LANES), BF16),
             jax.ShapeDtypeStruct((2, NK // 2, NF, LANES), F32),
             pltpu.SMEM((PLACES + 16,), jnp.int32),
+            pltpu.SMEM((1,), F32),
         ),
-        in_specs=[IN_HBM] * len(operands),
-        out_specs=(IN_VMEM, IN_VMEM, IN_SMEM),
+        in_specs=[IN_HBM] * (len(operands) - 1) + [IN_SMEM],
+        out_specs=(IN_VMEM, IN_VMEM, IN_SMEM, IN_SMEM),
         scratch_shapes=[
-            *[pltpu.VMEM(op.shape, op.dtype) for op in operands[:-2]],
-            *[pltpu.SMEM(op.shape, op.dtype) for op in operands[-2:]],
+            *[pltpu.VMEM(op.shape, op.dtype) for op in operands[:-3]],
+            *[pltpu.SMEM(op.shape, op.dtype) for op in operands[-3:-1]],
             pltpu.SMEM((4, 2 * ROWS), jnp.int32),
             pltpu.SMEM((ROWS * 16 + 16,), jnp.int32),
             pltpu.SMEM((16,), jnp.int32),
             pltpu.VMEM((16, LANES), F32),
-            pltpu.SemaphoreType.DMA((len(operands) + SLOTS,)),
+            pltpu.SemaphoreType.DMA((len(operands) + SLOTS - 1,)),
         ],
         compiler_params=PARAMS,
     )(*in_hbm)
@@ -538,8 +541,8 @@
 
 
 def local(masks, owned_counts, cell_ids, kernels, kernel_weights, dose, threshold):
-    packet, ker, seating = spectra(
-        masks, cell_ids, dose, kernels, kernel_weights, owned_counts
+    packet, ker, seating, threshold = spectra(
+        masks, cell_ids, dose, kernels, kernel_weights, owned_counts, threshold
     )
     packets = lax.all_to_all(packet, "cols", split_axis=0, concat_axis=0, tiled=True)
     outgoing, place = route(packets, seating)

time: 38 us -> 37.6 us (0.989)
  blocking collectives: 15.8 us -> 28.5 us
  starting transfers between devices: 6.32 us -> 0 us
  waiting for transfers between devices: 5.85 us -> 0 us
  Pallas kernels: 8.86 us -> 7.95 us
    all_to_all x0 -> x1, blocking collectives: none -> 12.6 us  [local(): lax.all_to_all(outgoing, 'rows', split_axis=0, concat_axis=0, tiled=True)]
    all_to_all x1 -> x0, starting transfers between devices: 6.32 us -> none  [local(): lax.all_to_all(outgoing, 'rows', split_axis=0, concat_axis=0, tiled=True)]
    all_to_all x1 -> x0, waiting for transfers between devices: 5.85 us -> none  [local(): lax.all_to_all(outgoing, 'rows', split_axis=0, concat_axis=0, tiled=True)]
    pallas_call x1, Pallas kernels: 1.83 us -> 1.09 us  [route(): pl.pallas_call(routing_kernel, out_shape=(jax.ShapeDtypeStruct((ROWS, OUT...]
  transfers between devices with their start and end apart: 1 -> 0, of which waited for: 1 -> 0; matrix products, arithmetic and copies ran while one was open for 0% -> 0% of each run, Pallas kernels for 0% -> 0%
where the time goes in v6:
time: 37.6 us; the launch traced here: 37.4 us
  blocking collectives  28.5 us (76%)
  Pallas kernels  7.95 us (21%)
  between operations  0.94 us (2%)
    all_to_all x1, blocking collectives, local(): lax.all_to_all(packet, 'cols', split_axis=0, concat_axis=0, tiled=True)  15.9 us
    all_to_all x1, blocking collectives, local(): lax.all_to_all(outgoing, 'rows', split_axis=0, concat_axis=0, tiled=True)  12.6 us
    pallas_call x1, Pallas kernels, develop(): pl.pallas_call(develop_kernel, out_shape=jax.ShapeDtypeStruct((2 * TILE,...  4.33 us
    pallas_call x1, Pallas kernels, spectra(): pl.pallas_call(spectra_kernel, out_shape=(jax.ShapeDtypeStruct((COLS, PAC...  2.53 us
    pallas_call x1, Pallas kernels, route(): pl.pallas_call(routing_kernel, out_shape=(jax.ShapeDtypeStruct((ROWS, OUT...  1.09 us

profile of v6, /device:TPU:1, one launch (start us, length us, event | category | flops | bytes accessed | tf_op | source)
XLA Modules:
  0.0 37.4 jit_solution(15418210493591539498)
XLA Ops:
  0.0 0.0 copy-start.6
  0.0 0.0 copy-start.10
  0.0 0.0 copy-start.8
  0.0 0.0 copy-start.9
  0.1 0.0 copy-start.7
  0.1 0.0 copy-start.2
  0.1 0.0 copy-start.3
  0.1 0.0 copy-start.4
  0.9 2.5 %shard_map.190 = (bf16[16,64,128]{2,1,0:T(8,128)(2,1)S(1)}, f32[2,8,32,128]{3,2,1,0:T(8,128)S(1)}, s32[80]{0:T(128)S(4)}, f32[1]{0:T(128)S(4)}) custom-call(bf16[6,384,384]{2,1,0:T(8,128)(2,1)} %mask.1, s32[4,16]{1,0:T(4,128)} %bitcast.1, f32[2,4]{1,0:T(2,128)} %dose.1, bf16[384,128]{1,0:T(8,128)(2,1)} %constant.26.clone.fwd_cols, ...), custom_call_target="tpu_custom_call" | custom-call | tf_op jit(solution)/shard_map/pallas_call | solution.py:478
  3.4 15.9 %all_to_all.10.packets = bf16[16,64,128]{2,1,0:T(8,128)(2,1)S(1)} all-to-all(bf16[16,64,128]{2,1,0:T(8,128)(2,1)S(1)} %get-tuple-element.11), channel_id=1, replica_groups=mesh['rows'=8,'cols'=16] {'cols'}, dimensions={0} | all-to-all | bytes 524288 | tf_op jit(solution)/shard_map/all_to_all | solution.py:547
  19.3 1.1 %shard_map.191 = (bf16[8,128,128]{2,1,0:T(8,128)(2,1)S(1)}, s32[8]{0:T(128)S(4)}) custom-call(bf16[16,64,128]{2,1,0:T(8,128)(2,1)S(1)} %all_to_all.10.packets, s32[80]{0:T(128)S(4)} %get-tuple-element.12.table), custom_call_target="tpu_custom_call" | custom-call | tf_op jit(solution)/shard_map/pallas_call | solution.py:502
  20.4 12.6 %all_to_all.11.tiles = bf16[8,128,128]{2,1,0:T(8,128)(2,1)S(1)} all-to-all(bf16[8,128,128]{2,1,0:T(8,128)(2,1)S(1)} %get-tuple-element.13), channel_id=1, replica_groups=mesh['rows'=8,'cols'=16] {'rows'}, dimensions={0} | all-to-all | bytes 524288 | tf_op jit(solution)/shard_map/all_to_all | solution.py:549
  33.0 0.0 copy-done
  33.0 0.0 copy-done.5
  33.0 0.0 copy-done.1
  33.0 0.0 copy-done.6
  33.0 0.0 copy-done.10
  33.0 0.0 copy-done.8
  33.0 0.0 copy-done.9
  33.0 0.0 copy-done.7
  33.1 0.0 copy-done.2
  33.1 0.0 copy-done.3
  33.1 0.0 copy-done.4
  33.1 4.3 %shard_map.192 = bf16[768,1536]{1,0:T(8,128)(2,1)} custom-call(bf16[8,128,128]{2,1,0:T(8,128)(2,1)S(1)} %all_to_all.11.tiles, s32[80]{0:T(128)S(4)} %get-tuple-element.12.table, s32[8]{0:T(128)S(4)} %get-tuple-element.14.place, f32[2,8,32,128]{3,2,1,0:T(8,128)S(1)} %get-tuple-element.15.ker, f32[1]{0:T(128)S(4)} %get-tuple-element.16.threshold, ...), custom_call_target="tpu_custom_call" | custom-call | tf_op jit(solution)/shard_map/pallas_call | solution.py:529
  (3 shorter events, 0.0 us)
Async XLA Ops:
  0.0 33.0 %copy-start = (bf16[400,160]{1,0:T(8,128)(2,1)S(1)}, bf16[400,160]{1,0:T(8,128)(2,1)}, u32[]{:S(2)}) copy-start(bf16[400,160]{1,0:T(8,128)(2,1)} %constant.38.clone.down_lower) | copy-start | bytes 384004
  0.0 33.0 %copy-start.5 = (bf16[368,80]{1,0:T(8,128)(2,1)S(1)}, bf16[368,80]{1,0:T(8,128)(2,1)}, u32[]{:S(2)}) copy-start(bf16[368,80]{1,0:T(8,128)(2,1)} %constant.37.clone.down_upper) | copy-start | bytes 176644
  0.0 33.0 %copy-start.1 = (bf16[256,384]{1,0:T(8,128)(2,1)S(1)}, bf16[256,384]{1,0:T(8,128)(2,1)}, u32[]{:S(2)}) copy-start(bf16[256,384]{1,0:T(8,128)(2,1)} %constant.36.clone.across) | copy-start | bytes 589828
  0.0 33.0 %copy-start.6 = (bf16[128,256]{1,0:T(8,128)(2,1)S(1)}, bf16[128,256]{1,0:T(8,128)(2,1)}, u32[]{:S(2)}) copy-start(bf16[128,256]{1,0:T(8,128)(2,1)} %constant.35.clone.inv_right) | copy-start | bytes 196612
  0.0 33.0 %copy-start.10 = (bf16[16,64]{1,0:T(8,128)(2,1)S(1)}, bf16[16,64]{1,0:T(8,128)(2,1)}, u32[]{:S(2)}) copy-start(bf16[16,64]{1,0:T(8,128)(2,1)} %constant.34.clone.edge_left) | copy-start | bytes 6148
  0.0 33.0 %copy-start.8 = (bf16[64,64]{1,0:T(8,128)(2,1)S(1)}, bf16[64,64]{1,0:T(8,128)(2,1)}, u32[]{:S(2)}) copy-start(bf16[64,64]{1,0:T(8,128)(2,1)} %constant.33.clone.inv_left) | copy-start | bytes 24580
  0.0 33.0 %copy-start.9 = (f32[16,128]{1,0:T(8,128)S(1)}, f32[16,128]{1,0:T(8,128)}, u32[]{:S(2)}) copy-start(f32[16,128]{1,0:T(8,128)} %constant.32.clone.rest_mask) | copy-start | bytes 24580
  0.1 33.0 %copy-start.7 = (bf16[128,256]{1,0:T(8,128)(2,1)S(1)}, bf16[128,256]{1,0:T(8,128)(2,1)}, u32[]{:S(2)}) copy-start(bf16[128,256]{1,0:T(8,128)(2,1)} %constant.31.clone.rest) | copy-start | bytes 196612
  0.1 33.0 %copy-start.2 = (bf16[128,512]{1,0:T(8,128)(2,1)S(1)}, bf16[128,512]{1,0:T(8,128)(2,1)}, u32[]{:S(2)}) copy-start(bf16[128,512]{1,0:T(8,128)(2,1)} %constant.30.clone.spread_low) | copy-start | bytes 393220
  0.1 33.0 %copy-start.3 = (bf16[128,512]{1,0:T(8,128)(2,1)S(1)}, bf16[128,512]{1,0:T(8,128)(2,1)}, u32[]{:S(2)}) copy-start(bf16[128,512]{1,0:T(8,128)(2,1)} %constant.29.clone.spread_up) | copy-start | bytes 393220
  0.1 33.0 %copy-start.4 = (bf16[192,192]{1,0:T(8,128)(2,1)S(1)}, bf16[192,192]{1,0:T(8,128)(2,1)}, u32[]{:S(2)}) copy-start(bf16[192,192]{1,0:T(8,128)(2,1)} %constant.28.clone.turned) | copy-start | bytes 221188

commit v7 on v6

--- a/solution.py
+++ b/solution.py
@@ -56,10 +56,11 @@
 
     turn = np.mod(points[:, None] * freq[None, :], Q) * (2.0 * np.pi / Q)
     cos, sin = np.cos(turn), np.sin(turn)
-    inverse_left = np.concatenate([cos, -sin], axis=1)
+    order = np.concatenate([np.arange(HALF + 1), np.arange(NF - 1, HALF, -1)])
+    inverse_left = np.concatenate([cos[:, order], -sin[:, order]], axis=1)
     edges = np.concatenate([np.arange(TILE - REACH, TILE), np.arange(REACH)])
     turn = np.mod(edges[:, None] * freq[None, :], TILE) * (2.0 * np.pi / TILE)
-    edge_left = np.concatenate([np.cos(turn), -np.sin(turn)], axis=1)
+    edge_left = np.concatenate([np.cos(turn)[:, order], -np.sin(turn)[:, order]], axis=1)
     right = np.zeros((LANES, 2 * LANES))
     for k in range(2):
         re = slice(2 * k * NF, (2 * k + 1) * NF)
@@ -87,11 +88,8 @@
         rest[Q + 2 * (HALF - 1), copy * NF + HALF] = 1.0
     rest_mask = np.zeros((HALF, LANES), np.float32)
     rest_mask[0, :Q] = rest_mask[0, Q + 2 * (HALF - 1)] = 1.0
-    turned = np.zeros((WINDOW * HALF // 2, WINDOW * HALF // 2))
     for i in range(1, HALF):
-        rest_mask[i, Q + i - 1] = rest_mask[i, Q + HALF - 1 + i - 1] = 1.0
-        for pair in range(WINDOW // 2):
-            turned[pair * HALF + i, pair * HALF + HALF - i] = 1.0
+        rest_mask[HALF - i, Q + i - 1] = rest_mask[HALF - i, Q + HALF - 1 + i - 1] = 1.0
 
     harmonic = np.arange(Q) - Q // 2
     fine = np.mod(pixels[:, None] * harmonic[None, :], TILE) * (2.0 * np.pi / TILE)
@@ -129,7 +127,6 @@
         spread_up=spread_up,
         spread_low=spread_low,
         rest=rest,
-        turned=turned,
         across=across,
         down_upper=4.0 * down[:SPLIT, :STACK],
         down_lower=4.0 * down[SPLIT:],
@@ -232,8 +229,12 @@
                     scale = jnp.sqrt(jnp.full((NF, NF), weights_s[k], F32))
                     re.append(kernels_v[0, k] * scale)
                     im.append(kernels_v[1, k] * scale)
-                ker[0, two] = jnp.concatenate([re[0], im[0], re[1], im[1]], axis=1)
-                ker[1, two] = jnp.concatenate([-im[0], re[0], -im[1], re[1]], axis=1)
+                for part, four in enumerate(
+                    ([re[0], im[0], re[1], im[1]], [-im[0], re[0], -im[1], re[1]])
+                ):
+                    block = jnp.concatenate(four, axis=1)
+                    turned = [block[n : n + 1] for n in range(NF - 1, HALF, -1)]
+                    ker[part, two] = jnp.concatenate([block[: HALF + 1], *turned], axis=0)
         cols = dot(rows_v[...], mask_v[slot])
         high, low = halves(cols[:Q] + cols[Q:])
         pairs.append(jnp.concatenate([high, low], axis=0))
@@ -349,7 +350,7 @@
 
 
 def develop_kernel(
-    tiles, table, place, ker, threshold, turned, spread_up, spread_low, rest, rest_mask,
+    tiles, table, place, ker, threshold, spread_up, spread_low, rest, rest_mask,
     inv_left, edge_left, inv_right, across, down_upper, down_lower,
     out,
     after_rows, stage, sems,
@@ -359,7 +360,8 @@
         at = slice(source * 16, (source + 1) * 16)
         after_rows[at, :] = tiles[source, REST : REST + 16, :].astype(F32)
     left = lanes_of((HALF, LANES)) < Q
-    held, rests = [], []
+    first = lax.broadcasted_iota(jnp.int32, (HALF, LANES), 0) == 0
+    held, paired, rests = [], [], []
     for t in range(0, WINDOW, 2):
         both = []
         for n in (t, t + 1):
@@ -373,10 +375,13 @@
             both.append(jnp.where(found >= 0, tile, 0.0))
             line = jnp.where(found >= 0, after_rows[pl.ds(here, 1), :], 0.0)
             rests.append(jnp.broadcast_to(line, (HALF, LANES)) * rest_mask[...])
-        held.append(jnp.where(left, both[0], both[1]).astype(BF16))
+        pair = jnp.where(left, both[0], both[1])
+        held.append(pair.astype(BF16))
+        paired.append(jnp.where(first, 0.0, pair).astype(BF16))
     held = jnp.concatenate(held, axis=0)
+    paired = jnp.concatenate(paired, axis=0)
     upper = dot(held, spread_up[...])
-    lower = dot(dot(turned[...], held).astype(BF16), spread_low[...])
+    lower = dot(paired, spread_low[...])
     rests = dot(jnp.concatenate(rests, axis=0).astype(BF16), rest[...])
 
     def doses(source):
@@ -523,7 +528,7 @@
 
 def develop(incoming, seating, place, ker, threshold):
     table = tables()
-    names = ("turned", "spread_up", "spread_low", "rest", "rest_mask")
+    names = ("spread_up", "spread_low", "rest", "rest_mask")
     names += ("inverse_left", "edge_left", "inverse_right", "across", "down_upper", "down_lower")
     constants = [jnp.asarray(table[n]) for n in names]
     return pl.pallas_call(

time: 37.6 us -> 37.5 us (level)
  no operation moved by 1% of the time
where the time goes in v7:
time: 37.5 us; the launch traced here: 37.3 us
  blocking collectives  28.5 us (76%)
  Pallas kernels  7.85 us (21%)
  between operations  0.9 us (2%)
    all_to_all x1, blocking collectives, local(): lax.all_to_all(packet, 'cols', split_axis=0, concat_axis=0, tiled=True)  15.9 us
    all_to_all x1, blocking collectives, local(): lax.all_to_all(outgoing, 'rows', split_axis=0, concat_axis=0, tiled=True)  12.6 us
    pallas_call x1, Pallas kernels, develop(): pl.pallas_call(develop_kernel, out_shape=jax.ShapeDtypeStruct((2 * TILE,...  4.23 us
    pallas_call x1, Pallas kernels, spectra(): pl.pallas_call(spectra_kernel, out_shape=(jax.ShapeDtypeStruct((COLS, PAC...  2.53 us
    pallas_call x1, Pallas kernels, route(): pl.pallas_call(routing_kernel, out_shape=(jax.ShapeDtypeStruct((ROWS, OUT...  1.09 us

profile of v7, /device:TPU:1, one launch (start us, length us, event | category | flops | bytes accessed | tf_op | source)
XLA Modules:
  0.0 37.3 jit_solution(13749489321976874012)
XLA Ops:
  0.0 0.0 copy-start
  0.0 0.0 copy-start.1
  0.0 0.0 copy-start.5
  0.0 0.0 copy-start.9
  0.0 0.0 copy-start.7
  0.0 0.0 copy-start.8
  0.1 0.0 copy-start.6
  0.1 0.0 copy-start.2
  0.1 0.0 copy-start.3
  0.9 2.5 %shard_map.181 = (bf16[16,64,128]{2,1,0:T(8,128)(2,1)S(1)}, f32[2,8,32,128]{3,2,1,0:T(8,128)S(1)}, s32[80]{0:T(128)S(4)}, f32[1]{0:T(128)S(4)}) custom-call(bf16[6,384,384]{2,1,0:T(8,128)(2,1)} %mask.1, s32[4,16]{1,0:T(4,128)} %bitcast.1, f32[2,4]{1,0:T(2,128)} %dose.1, bf16[384,128]{1,0:T(8,128)(2,1)} %constant.24.clone.fwd_cols, ...), custom_call_target="tpu_custom_call" | custom-call | tf_op jit(solution)/shard_map/pallas_call | solution.py:483
  3.4 15.9 %all_to_all.10.packets = bf16[16,64,128]{2,1,0:T(8,128)(2,1)S(1)} all-to-all(bf16[16,64,128]{2,1,0:T(8,128)(2,1)S(1)} %get-tuple-element.11), channel_id=1, replica_groups=mesh['rows'=8,'cols'=16] {'cols'}, dimensions={0} | all-to-all | bytes 524288 | tf_op jit(solution)/shard_map/all_to_all | solution.py:552
  19.3 1.1 %shard_map.182 = (bf16[8,128,128]{2,1,0:T(8,128)(2,1)S(1)}, s32[8]{0:T(128)S(4)}) custom-call(bf16[16,64,128]{2,1,0:T(8,128)(2,1)S(1)} %all_to_all.10.packets, s32[80]{0:T(128)S(4)} %get-tuple-element.12.table), custom_call_target="tpu_custom_call" | custom-call | tf_op jit(solution)/shard_map/pallas_call | solution.py:507
  20.4 12.6 %all_to_all.11.tiles = bf16[8,128,128]{2,1,0:T(8,128)(2,1)S(1)} all-to-all(bf16[8,128,128]{2,1,0:T(8,128)(2,1)S(1)} %get-tuple-element.13), channel_id=1, replica_groups=mesh['rows'=8,'cols'=16] {'rows'}, dimensions={0} | all-to-all | bytes 524288 | tf_op jit(solution)/shard_map/all_to_all | solution.py:554
  33.0 0.0 copy-done
  33.0 0.0 copy-done.4
  33.0 0.0 copy-done.1
  33.0 0.0 copy-done.5
  33.0 0.0 copy-done.9
  33.0 0.0 copy-done.7
  33.0 0.0 copy-done.8
  33.0 0.0 copy-done.6
  33.0 0.0 copy-done.2
  33.0 0.0 copy-done.3
  33.0 4.2 %shard_map.183 = bf16[768,1536]{1,0:T(8,128)(2,1)} custom-call(bf16[8,128,128]{2,1,0:T(8,128)(2,1)S(1)} %all_to_all.11.tiles, s32[80]{0:T(128)S(4)} %get-tuple-element.12.table, s32[8]{0:T(128)S(4)} %get-tuple-element.14.place, f32[2,8,32,128]{3,2,1,0:T(8,128)S(1)} %get-tuple-element.15.ker, f32[1]{0:T(128)S(4)} %get-tuple-element.16.threshold, ...), custom_call_target="tpu_custom_call" | custom-call | tf_op jit(solution)/shard_map/pallas_call | solution.py:534
  (1 shorter events, 0.0 us)
Async XLA Ops:
  0.0 33.0 %copy-start = (bf16[400,160]{1,0:T(8,128)(2,1)S(1)}, bf16[400,160]{1,0:T(8,128)(2,1)}, u32[]{:S(2)}) copy-start(bf16[400,160]{1,0:T(8,128)(2,1)} %constant.35.clone.down_lower) | copy-start | bytes 384004
  0.0 33.0 %copy-start.4 = (bf16[368,80]{1,0:T(8,128)(2,1)S(1)}, bf16[368,80]{1,0:T(8,128)(2,1)}, u32[]{:S(2)}) copy-start(bf16[368,80]{1,0:T(8,128)(2,1)} %constant.34.clone.down_upper) | copy-start | bytes 176644
  0.0 33.0 %copy-start.1 = (bf16[256,384]{1,0:T(8,128)(2,1)S(1)}, bf16[256,384]{1,0:T(8,128)(2,1)}, u32[]{:S(2)}) copy-start(bf16[256,384]{1,0:T(8,128)(2,1)} %constant.33.clone.across) | copy-start | bytes 589828
  0.0 33.0 %copy-start.5 = (bf16[128,256]{1,0:T(8,128)(2,1)S(1)}, bf16[128,256]{1,0:T(8,128)(2,1)}, u32[]{:S(2)}) copy-start(bf16[128,256]{1,0:T(8,128)(2,1)} %constant.32.clone.inv_right) | copy-start | bytes 196612
  0.0 33.0 %copy-start.9 = (bf16[16,64]{1,0:T(8,128)(2,1)S(1)}, bf16[16,64]{1,0:T(8,128)(2,1)}, u32[]{:S(2)}) copy-start(bf16[16,64]{1,0:T(8,128)(2,1)} %constant.31.clone.edge_left) | copy-start | bytes 6148
  0.0 33.0 %copy-start.7 = (bf16[64,64]{1,0:T(8,128)(2,1)S(1)}, bf16[64,64]{1,0:T(8,128)(2,1)}, u32[]{:S(2)}) copy-start(bf16[64,64]{1,0:T(8,128)(2,1)} %constant.30.clone.inv_left) | copy-start | bytes 24580
  0.0 33.0 %copy-start.8 = (f32[16,128]{1,0:T(8,128)S(1)}, f32[16,128]{1,0:T(8,128)}, u32[]{:S(2)}) copy-start(f32[16,128]{1,0:T(8,128)} %constant.29.clone.rest_mask) | copy-start | bytes 24580
  0.1 33.0 %copy-start.6 = (bf16[128,256]{1,0:T(8,128)(2,1)S(1)}, bf16[128,256]{1,0:T(8,128)(2,1)}, u32[]{:S(2)}) copy-start(bf16[128,256]{1,0:T(8,128)(2,1)} %constant.28.clone.rest) | copy-start | bytes 196612
  0.1 33.0 %copy-start.2 = (bf16[128,512]{1,0:T(8,128)(2,1)S(1)}, bf16[128,512]{1,0:T(8,128)(2,1)}, u32[]{:S(2)}) copy-start(bf16[128,512]{1,0:T(8,128)(2,1)} %constant.27.clone.spread_low) | copy-start | bytes 393220
  0.1 33.0 %copy-start.3 = (bf16[128,512]{1,0:T(8,128)(2,1)S(1)}, bf16[128,512]{1,0:T(8,128)(2,1)}, u32[]{:S(2)}) copy-start(bf16[128,512]{1,0:T(8,128)(2,1)} %constant.26.clone.spread_up) | copy-start | bytes 393220

commit v8 on v7

--- a/solution.py
+++ b/solution.py
@@ -286,7 +286,7 @@
 def routing_kernel(
     packets, table,
     out, place,
-    held, rests, buffer, where_v, where_s, chosen, taken, sem,
+    held, rests, buffer, chosen, taken,
 ):
     row, col = lax.axis_index("rows"), lax.axis_index("cols")
     def rest_of(c):
@@ -300,9 +300,11 @@
         line == 0, pltpu.roll(before, 16 - first - 3, 0), pltpu.roll(after, 16 - first + 1, 0)
     ).astype(jnp.int32)
     exists = ((line == 0) & (col > 0)) | ((line == 1) & (col < COLS - 1))
-    where_v[...] = jnp.where(exists, window, -1)
-    copy = pltpu.make_async_copy(where_v, where_s, sem)
-    copy.start()
+    outer = jnp.where(exists, window, -1)
+    shift = jnp.where(row > 0, LANES + 1 - 2 * row, 1)
+    mine = pltpu.roll(outer, shift, 1)
+    ids = [[outer[j, i] for i in range(2 * ROWS)] for j in range(2)]
+    own = [[mine[j, i] for i in range(4)] for j in range(2)]
 
     here = rest_of(col)
     for c in range(COLS):
@@ -338,10 +340,13 @@
     ]
     for dest in range(ROWS):
         send(dest, near[dest], 0)
-    copy.wait()
-    sources(window_rows(where_s, range(2)), place, 0, taken, NEAR)
+    cells = []
+    for i in range(4):
+        inside = (2 * row - 1 + i >= 0) & (2 * row - 1 + i < 2 * ROWS)
+        cells += [jnp.where(inside, own[j][i], -1) for j in range(2)]
+    sources(cells, place, 0, taken, NEAR)
     for dest in range(ROWS):
-        cells = [where_s[j, i] for i in rows_of(dest) for j in range(2)]
+        cells = [ids[j][i] for i in rows_of(dest) for j in range(2)]
         count = seats(cells, chosen, dest, row)
         cells = [jnp.where(n < count, chosen[dest * 16 + n], CELLS) for n in range(FAR)]
         send(dest, cells, NEAR // 2 * HALF)
@@ -516,11 +521,8 @@
             pltpu.VMEM((CELLS + SLOTS, HALF, LANES), F32),
             pltpu.VMEM((COLS * 16, LANES), F32),
             pltpu.VMEM((CELLS + 8, LANES), F32),
-            pltpu.VMEM((16, LANES), jnp.int32),
-            pltpu.SMEM((16, LANES), jnp.int32),
             pltpu.SMEM((ROWS * 16 + 16,), jnp.int32),
             pltpu.SMEM((16,), jnp.int32),
-            pltpu.SemaphoreType.DMA,
         ],
         compiler_params=PARAMS,
     )(packets, seating)

time: 37.5 us -> 37 us (0.987)
  Pallas kernels: 7.85 us -> 7.33 us
    pallas_call x1, Pallas kernels: 1.09 us -> 0.57 us  [route(): pl.pallas_call(routing_kernel, out_shape=(jax.ShapeDtypeStruct((ROWS, OUT...]
where the time goes in v8:
time: 37 us; the launch traced here: 36.8 us
  blocking collectives  28.5 us (77%)
  Pallas kernels  7.33 us (20%)
  between operations  0.9 us (2%)
    all_to_all x1, blocking collectives, local(): lax.all_to_all(packet, 'cols', split_axis=0, concat_axis=0, tiled=True)  15.9 us
    all_to_all x1, blocking collectives, local(): lax.all_to_all(outgoing, 'rows', split_axis=0, concat_axis=0, tiled=True)  12.6 us
    pallas_call x1, Pallas kernels, develop(): pl.pallas_call(develop_kernel, out_shape=jax.ShapeDtypeStruct((2 * TILE,...  4.23 us
    pallas_call x1, Pallas kernels, spectra(): pl.pallas_call(spectra_kernel, out_shape=(jax.ShapeDtypeStruct((COLS, PAC...  2.53 us

profile of v8, /device:TPU:1, one launch (start us, length us, event | category | flops | bytes accessed | tf_op | source)
XLA Modules:
  0.0 36.8 jit_solution(15589266121736214578)
XLA Ops:
  0.0 0.0 copy-start
  0.0 0.0 copy-start.1
  0.0 0.0 copy-start.5
  0.0 0.0 copy-start.9
  0.0 0.0 copy-start.7
  0.0 0.0 copy-start.8
  0.1 0.0 copy-start.6
  0.1 0.0 copy-start.2
  0.1 0.0 copy-start.3
  0.9 2.5 %shard_map.181 = (bf16[16,64,128]{2,1,0:T(8,128)(2,1)S(1)}, f32[2,8,32,128]{3,2,1,0:T(8,128)S(1)}, s32[80]{0:T(128)S(4)}, f32[1]{0:T(128)S(4)}) custom-call(bf16[6,384,384]{2,1,0:T(8,128)(2,1)} %mask.1, s32[4,16]{1,0:T(4,128)} %bitcast.1, f32[2,4]{1,0:T(2,128)} %dose.1, bf16[384,128]{1,0:T(8,128)(2,1)} %constant.24.clone.fwd_cols, ...), custom_call_target="tpu_custom_call" | custom-call | tf_op jit(solution)/shard_map/pallas_call | solution.py:488
  3.4 15.9 %all_to_all.10.packets = bf16[16,64,128]{2,1,0:T(8,128)(2,1)S(1)} all-to-all(bf16[16,64,128]{2,1,0:T(8,128)(2,1)S(1)} %get-tuple-element.11), channel_id=1, replica_groups=mesh['rows'=8,'cols'=16] {'cols'}, dimensions={0} | all-to-all | bytes 524288 | tf_op jit(solution)/shard_map/all_to_all | solution.py:554
  19.3 0.6 %shard_map.182 = (bf16[8,128,128]{2,1,0:T(8,128)(2,1)S(1)}, s32[8]{0:T(128)S(4)}) custom-call(bf16[16,64,128]{2,1,0:T(8,128)(2,1)S(1)} %all_to_all.10.packets, s32[80]{0:T(128)S(4)} %get-tuple-element.12.table), custom_call_target="tpu_custom_call" | custom-call | tf_op jit(solution)/shard_map/pallas_call | solution.py:512
  19.8 12.6 %all_to_all.11.tiles = bf16[8,128,128]{2,1,0:T(8,128)(2,1)S(1)} all-to-all(bf16[8,128,128]{2,1,0:T(8,128)(2,1)S(1)} %get-tuple-element.13), channel_id=1, replica_groups=mesh['rows'=8,'cols'=16] {'rows'}, dimensions={0} | all-to-all | bytes 524288 | tf_op jit(solution)/shard_map/all_to_all | solution.py:556
  32.4 0.0 copy-done
  32.4 0.0 copy-done.4
  32.4 0.0 copy-done.1
  32.5 0.0 copy-done.5
  32.5 0.0 copy-done.9
  32.5 0.0 copy-done.7
  32.5 0.0 copy-done.8
  32.5 0.0 copy-done.6
  32.5 0.0 copy-done.2
  32.5 0.0 copy-done.3
  32.5 4.2 %shard_map.183 = bf16[768,1536]{1,0:T(8,128)(2,1)} custom-call(bf16[8,128,128]{2,1,0:T(8,128)(2,1)S(1)} %all_to_all.11.tiles, s32[80]{0:T(128)S(4)} %get-tuple-element.12.table, s32[8]{0:T(128)S(4)} %get-tuple-element.14.place, f32[2,8,32,128]{3,2,1,0:T(8,128)S(1)} %get-tuple-element.15.ker, f32[1]{0:T(128)S(4)} %get-tuple-element.16.threshold, ...), custom_call_target="tpu_custom_call" | custom-call | tf_op jit(solution)/shard_map/pallas_call | solution.py:536
  (1 shorter events, 0.0 us)
Async XLA Ops:
  0.0 32.4 %copy-start = (bf16[400,160]{1,0:T(8,128)(2,1)S(1)}, bf16[400,160]{1,0:T(8,128)(2,1)}, u32[]{:S(2)}) copy-start(bf16[400,160]{1,0:T(8,128)(2,1)} %constant.35.clone.down_lower) | copy-start | bytes 384004
  0.0 32.4 %copy-start.4 = (bf16[368,80]{1,0:T(8,128)(2,1)S(1)}, bf16[368,80]{1,0:T(8,128)(2,1)}, u32[]{:S(2)}) copy-start(bf16[368,80]{1,0:T(8,128)(2,1)} %constant.34.clone.down_upper) | copy-start | bytes 176644
  0.0 32.4 %copy-start.1 = (bf16[256,384]{1,0:T(8,128)(2,1)S(1)}, bf16[256,384]{1,0:T(8,128)(2,1)}, u32[]{:S(2)}) copy-start(bf16[256,384]{1,0:T(8,128)(2,1)} %constant.33.clone.across) | copy-start | bytes 589828
  0.0 32.4 %copy-start.5 = (bf16[128,256]{1,0:T(8,128)(2,1)S(1)}, bf16[128,256]{1,0:T(8,128)(2,1)}, u32[]{:S(2)}) copy-start(bf16[128,256]{1,0:T(8,128)(2,1)} %constant.32.clone.inv_right) | copy-start | bytes 196612
  0.0 32.4 %copy-start.9 = (bf16[16,64]{1,0:T(8,128)(2,1)S(1)}, bf16[16,64]{1,0:T(8,128)(2,1)}, u32[]{:S(2)}) copy-start(bf16[16,64]{1,0:T(8,128)(2,1)} %constant.31.clone.edge_left) | copy-start | bytes 6148
  0.0 32.4 %copy-start.7 = (bf16[64,64]{1,0:T(8,128)(2,1)S(1)}, bf16[64,64]{1,0:T(8,128)(2,1)}, u32[]{:S(2)}) copy-start(bf16[64,64]{1,0:T(8,128)(2,1)} %constant.30.clone.inv_left) | copy-start | bytes 24580
  0.0 32.4 %copy-start.8 = (f32[16,128]{1,0:T(8,128)S(1)}, f32[16,128]{1,0:T(8,128)}, u32[]{:S(2)}) copy-start(f32[16,128]{1,0:T(8,128)} %constant.29.clone.rest_mask) | copy-start | bytes 24580
  0.1 32.4 %copy-start.6 = (bf16[128,256]{1,0:T(8,128)(2,1)S(1)}, bf16[128,256]{1,0:T(8,128)(2,1)}, u32[]{:S(2)}) copy-start(bf16[128,256]{1,0:T(8,128)(2,1)} %constant.28.clone.rest) | copy-start | bytes 196612
  0.1 32.4 %copy-start.2 = (bf16[128,512]{1,0:T(8,128)(2,1)S(1)}, bf16[128,512]{1,0:T(8,128)(2,1)}, u32[]{:S(2)}) copy-start(bf16[128,512]{1,0:T(8,128)(2,1)} %constant.27.clone.spread_low) | copy-start | bytes 393220
  0.1 32.4 %copy-start.3 = (bf16[128,512]{1,0:T(8,128)(2,1)S(1)}, bf16[128,512]{1,0:T(8,128)(2,1)}, u32[]{:S(2)}) copy-start(bf16[128,512]{1,0:T(8,128)(2,1)} %constant.26.clone.spread_up) | copy-start | bytes 393220

commit v9 on v8

--- a/solution.py
+++ b/solution.py
@@ -19,6 +19,7 @@
 COLS = 16
 CELLS = 32
 LANES = 128
+FORWARD = NF + 8
 HALF = NF // 2
 EXTRA = 3 * HALF
 IDS = EXTRA + SLOTS
@@ -51,8 +52,13 @@
     turn = np.mod(freq[:, None] * pixels[None, :], TILE) * (2.0 * np.pi / TILE)
     forward = np.concatenate([np.cos(turn), np.sin(turn)]) / TILE
     high, low = split(forward)
-    forward_rows = np.concatenate([high, low])
-    forward_cols = np.ascontiguousarray(forward_rows.T)
+    forward_cols = np.ascontiguousarray(np.concatenate([high, low]).T)
+    turn = np.mod(freq[: HALF + 1, None] * pixels[None, :], TILE) * (2.0 * np.pi / TILE)
+    forward = np.zeros((FORWARD, TILE))
+    forward[:HALF] = np.cos(turn[:HALF])
+    forward[HALF:NF] = -np.sin(turn[:HALF])
+    forward[NF] = np.cos(turn[HALF])
+    forward_rows = np.concatenate(split(forward / TILE))
 
     turn = np.mod(points[:, None] * freq[None, :], Q) * (2.0 * np.pi / Q)
     cos, sin = np.cos(turn), np.sin(turn)
@@ -236,35 +242,37 @@
                     turned = [block[n : n + 1] for n in range(NF - 1, HALF, -1)]
                     ker[part, two] = jnp.concatenate([block[: HALF + 1], *turned], axis=0)
         cols = dot(rows_v[...], mask_v[slot])
-        high, low = halves(cols[:Q] + cols[Q:])
-        pairs.append(jnp.concatenate([high, low], axis=0))
-
-    lane = lanes_of((NF, LANES))
-    line = lax.broadcasted_iota(jnp.int32, (NF, LANES), 0)
+        cols = cols[:FORWARD] + cols[FORWARD:]
+        high = cols.astype(BF16).astype(F32)
+        pairs.append(jnp.concatenate([high, cols - high], axis=0).astype(BF16))
+
+    lane = lanes_of((HALF, LANES))
+    line = lax.broadcasted_iota(jnp.int32, (HALF, LANES), 0)
     even = (lane // NF) % 2 == 0
-    in_re = lane == line + Q - HALF - 1
-    in_im = lane == line + Q - HALF - 1 + HALF - 1
-    column = line > HALF
+    in_re = (lane == Q + HALF - 1 - line) & (line > 0)
+    in_im = (lane == Q + 2 * (HALF - 1) - line) & (line > 0)
     lane1 = lanes_of((1, LANES))
     blocks, rows = [], []
     for slot in range(SLOTS):
         both = dot(pairs[slot], cols_v[...])
-        both = both[:Q] + both[Q:]
+        both = both[:FORWARD] + both[FORWARD:]
         both = both + pltpu.roll(both, Q, 1)
-        top, bottom = both[:NF], both[NF:]
-        real = top - pltpu.roll(bottom, NF, 1)
-        imag = -(bottom + pltpu.roll(top, NF, 1))
+        cos, sin, zero = both[:HALF], both[HALF:NF], both[NF : NF + 1]
+        cos_sin, sin_sin = pltpu.roll(cos, NF, 1), pltpu.roll(sin, NF, 1)
+        real = cos + sin_sin
+        imag = sin - cos_sin
         blocks.append(jnp.where(even, real, pltpu.roll(imag, NF, 1)))
-        first = jnp.where(column & in_re, jnp.broadcast_to(real[:, 0:1], (NF, LANES)), 0.0)
-        second = jnp.where(column & in_im, jnp.broadcast_to(imag[:, 0:1], (NF, LANES)), 0.0)
-        turned = jnp.sum(first + second, axis=0, keepdims=True)
-        mean = real[HALF : HALF + 1, HALF : HALF + 1]
+        first = jnp.broadcast_to((cos - sin_sin)[:, 0:1], (HALF, LANES))
+        second = jnp.broadcast_to(-(sin + cos_sin)[:, 0:1], (HALF, LANES))
+        turned = jnp.where(in_re, first, 0.0) + jnp.where(in_im, second, 0.0)
+        turned = jnp.sum(turned, axis=0, keepdims=True)
+        mean = zero[:, HALF : HALF + 1]
         mean = jnp.broadcast_to(mean - mean.astype(BF16).astype(F32), (1, LANES))
         turned = jnp.where(lane1 == Q + 2 * (HALF - 1), mean, turned)
-        rows.append(jnp.where(lane1 < Q, blocks[slot][HALF : HALF + 1], turned))
+        rows.append(jnp.where(lane1 < NF, zero, jnp.where(lane1 < Q, -zero, turned)))
     half = lanes_of((HALF, LANES)) < Q
     packed = [
-        jnp.where(half, blocks[2 * i][:HALF], blocks[2 * i + 1][:HALF]).astype(BF16)
+        jnp.where(half, blocks[2 * i], blocks[2 * i + 1]).astype(BF16)
         for i in range(SLOTS // 2)
     ]
     extra[...] = jnp.zeros_like(extra)

time: 37 us -> 36.9 us (level)
  no operation moved by 1% of the time
where the time goes in v9:
time: 36.9 us; the launch traced here: 36.7 us
  blocking collectives  28.5 us (77%)
  Pallas kernels  7.25 us (20%)
  between operations  0.9 us (2%)
    all_to_all x1, blocking collectives, local(): lax.all_to_all(packet, 'cols', split_axis=0, concat_axis=0, tiled=True)  15.9 us
    all_to_all x1, blocking collectives, local(): lax.all_to_all(outgoing, 'rows', split_axis=0, concat_axis=0, tiled=True)  12.6 us
    pallas_call x1, Pallas kernels, develop(): pl.pallas_call(develop_kernel, out_shape=jax.ShapeDtypeStruct((2 * TILE,...  4.23 us
    pallas_call x1, Pallas kernels, spectra(): pl.pallas_call(spectra_kernel, out_shape=(jax.ShapeDtypeStruct((COLS, PAC...  2.45 us

profile of v9, /device:TPU:1, one launch (start us, length us, event | category | flops | bytes accessed | tf_op | source)
XLA Modules:
  0.0 36.7 jit_solution(17562839308998190407)
XLA Ops:
  0.0 0.0 copy-start
  0.0 0.0 copy-start.4
  0.0 0.0 copy-start.5
  0.0 0.0 copy-start.9
  0.0 0.0 copy-start.7
  0.0 0.0 copy-start.8
  0.1 0.0 copy-start.6
  0.1 0.0 copy-start.2
  0.1 0.0 copy-start.3
  0.9 2.5 %shard_map.181 = (bf16[16,64,128]{2,1,0:T(8,128)(2,1)S(1)}, f32[2,8,32,128]{3,2,1,0:T(8,128)S(1)}, s32[80]{0:T(128)S(4)}, f32[1]{0:T(128)S(4)}) custom-call(bf16[6,384,384]{2,1,0:T(8,128)(2,1)} %mask.1, s32[4,16]{1,0:T(4,128)} %bitcast.1, f32[2,4]{1,0:T(2,128)} %dose.1, bf16[384,128]{1,0:T(8,128)(2,1)} %constant.24.clone.fwd_cols, ...), custom_call_target="tpu_custom_call" | custom-call | tf_op jit(solution)/shard_map/pallas_call | solution.py:496
  3.3 15.9 %all_to_all.10.packets = bf16[16,64,128]{2,1,0:T(8,128)(2,1)S(1)} all-to-all(bf16[16,64,128]{2,1,0:T(8,128)(2,1)S(1)} %get-tuple-element.11), channel_id=1, replica_groups=mesh['rows'=8,'cols'=16] {'cols'}, dimensions={0} | all-to-all | bytes 524288 | tf_op jit(solution)/shard_map/all_to_all | solution.py:562
  19.2 0.6 %shard_map.182 = (bf16[8,128,128]{2,1,0:T(8,128)(2,1)S(1)}, s32[8]{0:T(128)S(4)}) custom-call(bf16[16,64,128]{2,1,0:T(8,128)(2,1)S(1)} %all_to_all.10.packets, s32[80]{0:T(128)S(4)} %get-tuple-element.12.table), custom_call_target="tpu_custom_call" | custom-call | tf_op jit(solution)/shard_map/pallas_call | solution.py:520
  19.8 12.6 %all_to_all.11.tiles = bf16[8,128,128]{2,1,0:T(8,128)(2,1)S(1)} all-to-all(bf16[8,128,128]{2,1,0:T(8,128)(2,1)S(1)} %get-tuple-element.13), channel_id=1, replica_groups=mesh['rows'=8,'cols'=16] {'rows'}, dimensions={0} | all-to-all | bytes 524288 | tf_op jit(solution)/shard_map/all_to_all | solution.py:564
  32.4 0.0 copy-done
  32.4 0.0 copy-done.4
  32.4 0.0 copy-done.1
  32.4 0.0 copy-done.5
  32.4 0.0 copy-done.9
  32.4 0.0 copy-done.7
  32.4 0.0 copy-done.8
  32.4 0.0 copy-done.6
  32.4 0.0 copy-done.2
  32.4 0.0 copy-done.3
  32.5 4.2 %shard_map.183 = bf16[768,1536]{1,0:T(8,128)(2,1)} custom-call(bf16[8,128,128]{2,1,0:T(8,128)(2,1)S(1)} %all_to_all.11.tiles, s32[80]{0:T(128)S(4)} %get-tuple-element.12.table, s32[8]{0:T(128)S(4)} %get-tuple-element.14.place, f32[2,8,32,128]{3,2,1,0:T(8,128)S(1)} %get-tuple-element.15.ker, f32[1]{0:T(128)S(4)} %get-tuple-element.16.threshold, ...), custom_call_target="tpu_custom_call" | custom-call | tf_op jit(solution)/shard_map/pallas_call | solution.py:544
  (1 shorter events, 0.0 us)
Async XLA Ops:
  0.0 32.4 %copy-start = (bf16[400,160]{1,0:T(8,128)(2,1)S(1)}, bf16[400,160]{1,0:T(8,128)(2,1)}, u32[]{:S(2)}) copy-start(bf16[400,160]{1,0:T(8,128)(2,1)} %constant.35.clone.down_lower) | copy-start | bytes 384004
  0.0 32.4 %copy-start.4 = (bf16[368,80]{1,0:T(8,128)(2,1)S(1)}, bf16[368,80]{1,0:T(8,128)(2,1)}, u32[]{:S(2)}) copy-start(bf16[368,80]{1,0:T(8,128)(2,1)} %constant.34.clone.down_upper) | copy-start | bytes 176644
  0.0 32.4 %copy-start.1 = (bf16[256,384]{1,0:T(8,128)(2,1)S(1)}, bf16[256,384]{1,0:T(8,128)(2,1)}, u32[]{:S(2)}) copy-start(bf16[256,384]{1,0:T(8,128)(2,1)} %constant.33.clone.across) | copy-start | bytes 589828
  0.0 32.4 %copy-start.5 = (bf16[128,256]{1,0:T(8,128)(2,1)S(1)}, bf16[128,256]{1,0:T(8,128)(2,1)}, u32[]{:S(2)}) copy-start(bf16[128,256]{1,0:T(8,128)(2,1)} %constant.32.clone.inv_right) | copy-start | bytes 196612
  0.0 32.4 %copy-start.9 = (bf16[16,64]{1,0:T(8,128)(2,1)S(1)}, bf16[16,64]{1,0:T(8,128)(2,1)}, u32[]{:S(2)}) copy-start(bf16[16,64]{1,0:T(8,128)(2,1)} %constant.31.clone.edge_left) | copy-start | bytes 6148
  0.0 32.4 %copy-start.7 = (bf16[64,64]{1,0:T(8,128)(2,1)S(1)}, bf16[64,64]{1,0:T(8,128)(2,1)}, u32[]{:S(2)}) copy-start(bf16[64,64]{1,0:T(8,128)(2,1)} %constant.30.clone.inv_left) | copy-start | bytes 24580
  0.0 32.4 %copy-start.8 = (f32[16,128]{1,0:T(8,128)S(1)}, f32[16,128]{1,0:T(8,128)}, u32[]{:S(2)}) copy-start(f32[16,128]{1,0:T(8,128)} %constant.29.clone.rest_mask) | copy-start | bytes 24580
  0.1 32.4 %copy-start.6 = (bf16[128,256]{1,0:T(8,128)(2,1)S(1)}, bf16[128,256]{1,0:T(8,128)(2,1)}, u32[]{:S(2)}) copy-start(bf16[128,256]{1,0:T(8,128)(2,1)} %constant.28.clone.rest) | copy-start | bytes 196612
  0.1 32.4 %copy-start.2 = (bf16[128,512]{1,0:T(8,128)(2,1)S(1)}, bf16[128,512]{1,0:T(8,128)(2,1)}, u32[]{:S(2)}) copy-start(bf16[128,512]{1,0:T(8,128)(2,1)} %constant.27.clone.spread_low) | copy-start | bytes 393220
  0.1 32.4 %copy-start.3 = (bf16[128,512]{1,0:T(8,128)(2,1)S(1)}, bf16[128,512]{1,0:T(8,128)(2,1)}, u32[]{:S(2)}) copy-start(bf16[128,512]{1,0:T(8,128)(2,1)} %constant.26.clone.spread_up) | copy-start | bytes 393220

commit v10 on v9

--- a/solution.py
+++ b/solution.py
@@ -440,9 +440,9 @@
     dose_rows = [above[1:2], own[0:1], own[1:2], below[0:1]]
     left = lanes_of((STACK, LANES)) < Q
 
-    images = {}
-    for group in ((0, 3), (1,), (2,)):
-        halfway = {(i, j): picture(i, j) for i in group for j in range(6)}
+    images, halfway = {}, {}
+    for group in ((0, 3, 1), (2,)):
+        halfway.update({(i, j): picture(i, j) for i in group for j in range(6)})
         for i in group:
             for j in range(6):
                 scale = dose_rows[i][:, lane_of[j] : lane_of[j] + 1]

time: 36.9 us -> 36.9 us (level)
  no operation moved by 1% of the time
where the time goes in v10:
time: 36.9 us; the launch traced here: 36.7 us
  blocking collectives  28.5 us (77%)
  Pallas kernels  7.25 us (20%)
  between operations  0.9 us (2%)
    all_to_all x1, blocking collectives, local(): lax.all_to_all(packet, 'cols', split_axis=0, concat_axis=0, tiled=True)  15.9 us
    all_to_all x1, blocking collectives, local(): lax.all_to_all(outgoing, 'rows', split_axis=0, concat_axis=0, tiled=True)  12.6 us
    pallas_call x1, Pallas kernels, develop(): pl.pallas_call(develop_kernel, out_shape=jax.ShapeDtypeStruct((2 * TILE,...  4.23 us
    pallas_call x1, Pallas kernels, spectra(): pl.pallas_call(spectra_kernel, out_shape=(jax.ShapeDtypeStruct((COLS, PAC...  2.45 us

profile of v10, /device:TPU:1, one launch (start us, length us, event | category | flops | bytes accessed | tf_op | source)
XLA Modules:
  0.0 36.7 jit_solution(15184633375607653022)
XLA Ops:
  0.0 0.0 copy-start.4
  0.0 0.0 copy-start.1
  0.0 0.0 copy-start.5
  0.0 0.0 copy-start.9
  0.0 0.0 copy-start.7
  0.0 0.0 copy-start.8
  0.1 0.0 copy-start.6
  0.1 0.0 copy-start.2
  0.1 0.0 copy-start.3
  0.9 2.5 %shard_map.181 = (bf16[16,64,128]{2,1,0:T(8,128)(2,1)S(1)}, f32[2,8,32,128]{3,2,1,0:T(8,128)S(1)}, s32[80]{0:T(128)S(4)}, f32[1]{0:T(128)S(4)}) custom-call(bf16[6,384,384]{2,1,0:T(8,128)(2,1)} %mask.1, s32[4,16]{1,0:T(4,128)} %bitcast.1, f32[2,4]{1,0:T(2,128)} %dose.1, bf16[384,128]{1,0:T(8,128)(2,1)} %constant.24.clone.fwd_cols, ...), custom_call_target="tpu_custom_call" | custom-call | tf_op jit(solution)/shard_map/pallas_call | solution.py:496
  3.3 15.9 %all_to_all.10.packets = bf16[16,64,128]{2,1,0:T(8,128)(2,1)S(1)} all-to-all(bf16[16,64,128]{2,1,0:T(8,128)(2,1)S(1)} %get-tuple-element.11), channel_id=1, replica_groups=mesh['rows'=8,'cols'=16] {'cols'}, dimensions={0} | all-to-all | bytes 524288 | tf_op jit(solution)/shard_map/all_to_all | solution.py:562
  19.2 0.6 %shard_map.182 = (bf16[8,128,128]{2,1,0:T(8,128)(2,1)S(1)}, s32[8]{0:T(128)S(4)}) custom-call(bf16[16,64,128]{2,1,0:T(8,128)(2,1)S(1)} %all_to_all.10.packets, s32[80]{0:T(128)S(4)} %get-tuple-element.12.table), custom_call_target="tpu_custom_call" | custom-call | tf_op jit(solution)/shard_map/pallas_call | solution.py:520
  19.8 12.6 %all_to_all.11.tiles = bf16[8,128,128]{2,1,0:T(8,128)(2,1)S(1)} all-to-all(bf16[8,128,128]{2,1,0:T(8,128)(2,1)S(1)} %get-tuple-element.13), channel_id=1, replica_groups=mesh['rows'=8,'cols'=16] {'rows'}, dimensions={0} | all-to-all | bytes 524288 | tf_op jit(solution)/shard_map/all_to_all | solution.py:564
  32.4 0.0 copy-done
  32.4 0.0 copy-done.4
  32.4 0.0 copy-done.1
  32.4 0.0 copy-done.5
  32.4 0.0 copy-done.9
  32.4 0.0 copy-done.7
  32.4 0.0 copy-done.8
  32.4 0.0 copy-done.6
  32.4 0.0 copy-done.2
  32.4 0.0 copy-done.3
  32.5 4.2 %shard_map.183 = bf16[768,1536]{1,0:T(8,128)(2,1)} custom-call(bf16[8,128,128]{2,1,0:T(8,128)(2,1)S(1)} %all_to_all.11.tiles, s32[80]{0:T(128)S(4)} %get-tuple-element.12.table, s32[8]{0:T(128)S(4)} %get-tuple-element.14.place, f32[2,8,32,128]{3,2,1,0:T(8,128)S(1)} %get-tuple-element.15.ker, f32[1]{0:T(128)S(4)} %get-tuple-element.16.threshold, ...), custom_call_target="tpu_custom_call" | custom-call | tf_op jit(solution)/shard_map/pallas_call | solution.py:544
  (1 shorter events, 0.0 us)
Async XLA Ops:
  0.0 32.4 %copy-start = (bf16[400,160]{1,0:T(8,128)(2,1)S(1)}, bf16[400,160]{1,0:T(8,128)(2,1)}, u32[]{:S(2)}) copy-start(bf16[400,160]{1,0:T(8,128)(2,1)} %constant.35.clone.down_lower) | copy-start | bytes 384004
  0.0 32.4 %copy-start.4 = (bf16[368,80]{1,0:T(8,128)(2,1)S(1)}, bf16[368,80]{1,0:T(8,128)(2,1)}, u32[]{:S(2)}) copy-start(bf16[368,80]{1,0:T(8,128)(2,1)} %constant.34.clone.down_upper) | copy-start | bytes 176644
  0.0 32.4 %copy-start.1 = (bf16[256,384]{1,0:T(8,128)(2,1)S(1)}, bf16[256,384]{1,0:T(8,128)(2,1)}, u32[]{:S(2)}) copy-start(bf16[256,384]{1,0:T(8,128)(2,1)} %constant.33.clone.across) | copy-start | bytes 589828
  0.0 32.4 %copy-start.5 = (bf16[128,256]{1,0:T(8,128)(2,1)S(1)}, bf16[128,256]{1,0:T(8,128)(2,1)}, u32[]{:S(2)}) copy-start(bf16[128,256]{1,0:T(8,128)(2,1)} %constant.32.clone.inv_right) | copy-start | bytes 196612
  0.0 32.4 %copy-start.9 = (bf16[16,64]{1,0:T(8,128)(2,1)S(1)}, bf16[16,64]{1,0:T(8,128)(2,1)}, u32[]{:S(2)}) copy-start(bf16[16,64]{1,0:T(8,128)(2,1)} %constant.31.clone.edge_left) | copy-start | bytes 6148
  0.0 32.4 %copy-start.7 = (bf16[64,64]{1,0:T(8,128)(2,1)S(1)}, bf16[64,64]{1,0:T(8,128)(2,1)}, u32[]{:S(2)}) copy-start(bf16[64,64]{1,0:T(8,128)(2,1)} %constant.30.clone.inv_left) | copy-start | bytes 24580
  0.0 32.4 %copy-start.8 = (f32[16,128]{1,0:T(8,128)S(1)}, f32[16,128]{1,0:T(8,128)}, u32[]{:S(2)}) copy-start(f32[16,128]{1,0:T(8,128)} %constant.29.clone.rest_mask) | copy-start | bytes 24580
  0.1 32.4 %copy-start.6 = (bf16[128,256]{1,0:T(8,128)(2,1)S(1)}, bf16[128,256]{1,0:T(8,128)(2,1)}, u32[]{:S(2)}) copy-start(bf16[128,256]{1,0:T(8,128)(2,1)} %constant.28.clone.rest) | copy-start | bytes 196612
  0.1 32.4 %copy-start.2 = (bf16[128,512]{1,0:T(8,128)(2,1)S(1)}, bf16[128,512]{1,0:T(8,128)(2,1)}, u32[]{:S(2)}) copy-start(bf16[128,512]{1,0:T(8,128)(2,1)} %constant.27.clone.spread_low) | copy-start | bytes 393220
  0.1 32.4 %copy-start.3 = (bf16[128,512]{1,0:T(8,128)(2,1)S(1)}, bf16[128,512]{1,0:T(8,128)(2,1)}, u32[]{:S(2)}) copy-start(bf16[128,512]{1,0:T(8,128)(2,1)} %constant.26.clone.spread_up) | copy-start | bytes 393220
